TPU v7x, 256 devices: a whole 4x4x8 slice. The times are simulated.
256 devices in a mesh: row: 8 (over x, core), col: 32 (over z, y).
Axes of the slice: x: 4, y: 4, z: 8, core: 2. Of those that a mesh axis runs over, the one named last changes fastest.
Arguments:
- matrix: float32 [8, 8, 256, 2, 32, 256], P(None, 'row', None, None, 'col'), as said below
- pattern: int32 [64, 64], replicated, may hold values from 0 to 1, as said below
Outputs:
- factored: float32 [8, 8, 256, 2, 32, 256], P(None, 'row', None, None, 'col')
Inputs may be any that keep to these rules, and one draw needn't show every extreme that they name: pattern is symmetric with ones on its diagonal and pattern[1, 0] = 1; writing c0 and c1 for its columns 0 and 1, c1[I] >= c0[I], and pattern[I, J] = 1 wherever c0[I] = c0[J] = 1 or c1[I] = c1[J] = 1 with I, J >= 1 (closed under the fill of the two panels). matrix is symmetric positive definite.
All inputs are finite; a program needn't handle non-finite values.
Results may differ from a plain program's by a relative error of at most 0.0001.
Values sent between devices are 32-bit elements; how exact they have to be, the bound alone decides.
No kernel may reach another device: no remote copies, remote signals or barrier semaphores. Data moves between devices by JAX's collectives and lax.ppermute only.
A program may use at most 64 MiB of HBM per device.

v0:
```python
import jax
import jax.numpy as jnp
from jax import lax
from jax.sharding import PartitionSpec as P


def broadcast(value, axis, source):
    kept = jnp.where(lax.axis_index(axis) == source, value, 0).astype(value.dtype)
    return lax.psum(kept, axis)


def solve_rows(pivot, column):
    count, width = (column.shape[0], column.shape[1])
    stacked = column.transpose(2, 0, 1).reshape(width, count * width)
    solved = lax.linalg.triangular_solve(pivot, stacked, left_side=True, lower=True)
    return solved.reshape(width, count, width).transpose(1, 2, 0)


def place_pivot(solved, pivot, global_ids, k):
    kept = jnp.where((global_ids > k)[:, None, None], solved, jnp.zeros_like(solved))
    return jnp.where((global_ids == k)[:, None, None], pivot[None, :, :], kept)


def pick_columns(rows_data, col_ids, nrow):
    picked = [
        lax.dynamic_index_in_dim(rows_data, col_ids[c] // nrow, 0, keepdims=True)
        for c in range(col_ids.shape[0])
    ]
    return jnp.concatenate(picked, axis=0)


def factor_panel(local, k, nrow, ncol, q, row_ids, col_ids):
    rk, ck = (k // nrow, k // ncol)
    pk, qk = (k % nrow, k % ncol)
    column = local[:, :, ck, :]
    pivot = jnp.linalg.cholesky(broadcast(local[rk, :, ck, :], "row", pk))
    own_rows = place_pivot(solve_rows(pivot, column), pivot, row_ids, k)
    row_panel = broadcast(own_rows, "col", qk)
    col_panel = broadcast(pick_columns(row_panel, col_ids, nrow), "row", q % nrow)
    return (row_panel, col_panel)


def apply_update(local, row_panel, col_panel, weight, first, last):
    update = jnp.einsum("rab,cdb->racd", row_panel, col_panel, precision=lax.Precision.HIGHEST)
    changed = local - weight[:, None, :, None] * update
    return local.at[:, :, first:last, :].set(changed)


def per_device(matrix, pattern):
    nrow = lax.axis_size("row")
    ncol = lax.axis_size("col")
    p = lax.axis_index("row")
    q = lax.axis_index("col")
    local = matrix[:, 0, :, :, 0, :]
    row_count, width, col_count = (local.shape[0], local.shape[1], local.shape[2])
    row_ids = jnp.arange(row_count, dtype=jnp.int32) * nrow + p
    col_ids = jnp.arange(col_count, dtype=jnp.int32) * ncol + q
    grid = pattern.reshape(row_count, nrow, col_count, ncol)
    grid = lax.dynamic_index_in_dim(grid, p, 1, keepdims=False)
    local_pattern = lax.dynamic_index_in_dim(grid, q, 2, keepdims=False).astype(jnp.float32)
    lower_mask = (row_ids[:, None] >= col_ids[None, :]).astype(jnp.float32)

    def weights_for(k):
        return local_pattern * lower_mask * (col_ids[None, :] > k).astype(jnp.float32)

    def store_panel(local, row_panel, k):
        ck = k // ncol
        kept = jnp.where(q == k % ncol, row_panel, local[:, :, ck, :])
        return local.at[:, :, ck, :].set(kept)

    first_rows, first_cols = factor_panel(local, 0, nrow, ncol, q, row_ids, col_ids)
    local = store_panel(local, first_rows, 0)
    local = apply_update(local, first_rows, first_cols, weights_for(0), 0, col_count)
    second_rows, second_cols = factor_panel(local, 1, nrow, ncol, q, row_ids, col_ids)
    local = store_panel(local, second_rows, 1)
    local = apply_update(local, second_rows, second_cols, weights_for(1), 0, col_count)
    local = local * lower_mask[:, None, :, None]
    return local.reshape(row_count, 1, width, col_count, 1, width)


def solution(mesh):
    return jax.shard_map(
        per_device,
        mesh=mesh,
        in_specs=(P(None, "row", None, None, "col", None), P()),
        out_specs=P(None, "row", None, None, "col", None),
        check_vma=False,
    )
```

profile of v0, /device:TPU:36, one launch (start us, length us, event | category | flops | bytes accessed | tf_op | source)
XLA Modules:
  0.0 760.8 jit_solution(6440380979272111422)
XLA Ops:
  6.5 10.9 %copy.21 = f32[8,1,256,2,1,256]{2,5,3,0,4,1:T(8,128)} copy(f32[8,1,256,2,1,256]{5,4,3,2,1,0:T(1,128)} %param.17) | data formatting | bytes 8388608 | tf_op args[0]
  17.4 1.7 fusion.13
  19.2 10.9 %copy.51 = f32[8,1,256,2,1,256]{2,5,0,3,1,4:T(8,128)} copy(f32[8,1,256,2,1,256]{5,4,3,2,1,0:T(1,128)} %param.17) | data formatting | bytes 8388608 | tf_op jit(solution)/shard_map/squeeze | solution.py:54
  30.1 3.0 slice_bitcast_fusion.1
  33.1 1.9 copy.25
  35.1 47.8 %all-reduce.8.cloned.1.call-done = f32[256,256]{0,1:T(8,128)} async-done(((f32[256,256]{0,1:T(8,128)}), f32[256,256]{0,1:T(8,128)}) %all-reduce.8.cloned.1.call-update) | async-done | bytes 262160 | tf_op jit(solution)/shard_map/psum | solution.py:9
  82.8 1.1 copy.22
  83.9 1.0 fusion.15
  84.9 11.7 %cholesky.130 = f32[128,128]{1,0:T(8,128)S(1)} custom-call(f32[128,128]{1,0:T(8,128)S(1)} %cholesky.194), custom_call_target="Cholesky" | custom-call | tf_op jit(solution)/shard_map/jit(cholesky)/cholesky | solution.py:36
  96.7 9.8 %custom-call.13 = f32[1,128,128]{1,2,0:T(8,128)S(1)} custom-call(f32[1,128,128]{2,1,0:T(8,128)S(1)} %get-tuple-element.124), custom_call_target="InvertDiagBlocksLowerTriangular" | custom-call | tf_op jit(solution)/shard_map/jit(cholesky)/cholesky | solution.py:36
  106.7 0.3 convolution_subtract_fusion.3
  107.0 11.7 %cholesky.147 = f32[128,128]{1,0:T(8,128)S(1)} custom-call(f32[128,128]{1,0:T(8,128)S(1)} %convolution_subtract_fusion.3), custom_call_target="Cholesky" | custom-call | tf_op jit(solution)/shard_map/jit(cholesky)/cholesky | solution.py:36
  118.8 0.7 compare_reduce_fusion.2
  120.7 3.8 while.10
  120.7 0.6 fusion.42
  121.3 1.3 bitcast_dynamic-update-slice_fusion.5
  122.6 0.6 fusion.42
  123.2 1.3 bitcast_dynamic-update-slice_fusion.5
  124.5 20.1 %custom-call.14 = f32[2,128,128]{1,2,0:T(8,128)S(1)} custom-call(f32[2,128,128]{2,1,0:T(8,128)S(1)} %get-tuple-element.85), custom_call_target="InvertDiagBlocksLowerTriangular" | custom-call | tf_op jit(solution)/shard_map/triangular_solve/custom-call.0 | solution.py:15
  144.6 1.1 fusion.8
  145.7 1.8 convolution_subtract_fusion.1
  147.5 1.1 fusion.23
  148.8 1.8 copy.26
  150.6 1.9 copy.27
  152.7 1.6 fusion.5
  154.4 0.6 fusion.31
  160.5 150.2 %all-reduce.10.cloned.1.call-done = f32[8,256,256]{1,2,0:T(8,128)} async-done(((f32[8,256,256]{1,2,0:T(8,128)}), f32[8,256,256]{1,2,0:T(8,128)}) %all-reduce.10.cloned.1.call-update) | async-done | bytes 2097168 | tf_op jit(solution)/shard_map/psum | solution.py:9
  310.7 1.2 constant_dynamic-slice_fusion.5
  311.9 0.8 maximum_select_fusion
  312.8 3.2 bitcast_dynamic-update-slice_fusion.2
  316.0 56.8 %all-reduce.12.cloned.1.call-done = f32[2,256,256]{1,2,0:T(8,128)} async-done(((f32[2,256,256]{1,2,0:T(8,128)}), f32[2,256,256]{1,2,0:T(8,128)}) %all-reduce.12.cloned.1.call-update) | async-done | bytes 524304 | tf_op jit(solution)/shard_map/psum | solution.py:9
  372.8 5.8 multiply_subtract_fusion
  378.6 2.0 copy-done
  380.6 0.7 fusion.12
  381.4 3.4 fusion.30
  384.8 2.0 copy.37
  386.8 58.9 %all-reduce.14.cloned.1.call-done = f32[256,256]{0,1:T(8,128)} async-done(((f32[256,256]{0,1:T(8,128)}), f32[256,256]{0,1:T(8,128)}) %all-reduce.14.cloned.1.call-update) | async-done | bytes 262160 | tf_op jit(solution)/shard_map/psum | solution.py:9
  445.7 1.1 copy.34
  446.8 1.0 fusion.14
  447.8 11.7 %cholesky.164 = f32[128,128]{1,0:T(8,128)S(1)} custom-call(f32[128,128]{1,0:T(8,128)S(1)} %cholesky.197), custom_call_target="Cholesky" | custom-call | tf_op jit(solution)/shard_map/jit(cholesky)/cholesky | solution.py:36
  459.5 9.8 %custom-call.15 = f32[1,128,128]{1,2,0:T(8,128)S(1)} custom-call(f32[1,128,128]{2,1,0:T(8,128)S(1)} %get-tuple-element.120), custom_call_target="InvertDiagBlocksLowerTriangular" | custom-call | tf_op jit(solution)/shard_map/jit(cholesky)/cholesky | solution.py:36
  469.6 0.3 convolution_subtract_fusion.2
  469.8 11.7 %cholesky.181 = f32[128,128]{1,0:T(8,128)S(1)} custom-call(f32[128,128]{1,0:T(8,128)S(1)} %convolution_subtract_fusion.2), custom_call_target="Cholesky" | custom-call | tf_op jit(solution)/shard_map/jit(cholesky)/cholesky | solution.py:36
  481.5 0.6 compare_reduce_fusion.1
  482.2 0.6 compare_reduce_fusion
  484.0 3.6 while.11
  484.1 0.6 fusion.43
  484.6 1.2 bitcast_dynamic-update-slice_fusion.6
  485.9 0.6 fusion.43
  486.5 1.2 bitcast_dynamic-update-slice_fusion.6
  487.7 19.9 %custom-call.16 = f32[2,128,128]{1,2,0:T(8,128)S(1)} custom-call(f32[2,128,128]{2,1,0:T(8,128)S(1)} %get-tuple-element.86), custom_call_target="InvertDiagBlocksLowerTriangular" | custom-call | tf_op jit(solution)/shard_map/triangular_solve/custom-call.0 | solution.py:15
  507.6 1.1 fusion.6
  508.7 1.8 convolution_subtract_fusion
  510.5 1.1 fusion.19
  511.7 1.8 copy.38
  513.5 1.9 copy.39
  515.6 1.6 fusion.4
  517.4 156.2 %all-reduce.16.cloned.1.call-done = f32[8,256,256]{1,2,0:T(8,128)} async-done(((f32[8,256,256]{1,2,0:T(8,128)}), f32[8,256,256]{1,2,0:T(8,128)}) %all-reduce.16.cloned.1.call-update) | async-done | bytes 2097168 | tf_op jit(solution)/shard_map/psum | solution.py:9
  673.6 1.2 constant_dynamic-slice_fusion.3
  674.8 0.9 maximum_select_fusion.1
  675.7 3.2 fusion.1
  678.9 56.8 %all-reduce.18.cloned.1.call-done = f32[2,256,256]{1,2,0:T(8,128)} async-done(((f32[2,256,256]{1,2,0:T(8,128)}), f32[2,256,256]{1,2,0:T(8,128)}) %all-reduce.18.cloned.1.call-update) | async-done | bytes 524304 | tf_op jit(solution)/shard_map/psum | solution.py:9
  735.7 7.2 multiply_bitcast_fusion
  742.9 10.9 %copy.44 = f32[8,1,256,2,1,256]{5,4,3,2,1,0:T(1,128)} copy(f32[8,1,256,2,1,256]{2,5,3,0,4,1:T(8,128)} %multiply_bitcast_fusion) | data formatting | bytes 8388608 | tf_op jit(solution)/shard_map/mul | solution.py:77
  (57 shorter events, 2.3 us)
Async XLA Ops:
  6.5 76.3 %all-reduce.8.cloned.1.call-start = ((), (), s32[]{:S(2)}) async-start(), calls=%async_computation | async-start | bytes 524288 | tf_op jit(solution)/shard_map/psum | solution.py:9
  19.1 291.5 %all-reduce.10.cloned.1.call-start = ((), (), s32[]{:S(2)}) async-start(), calls=%async_computation.1 | async-start | bytes 4194304 | tf_op jit(solution)/shard_map/psum | solution.py:9
  154.3 5.7 copy-start.4
  154.3 218.5 %all-reduce.12.cloned.1.call-start = ((), (), s32[]{:S(2)}) async-start(), calls=%async_computation.2 | async-start | bytes 1048576 | tf_op jit(solution)/shard_map/psum | solution.py:9
  310.7 2.1 copy-start.1
  312.7 132.9 %all-reduce.14.cloned.1.call-start = ((), (), s32[]{:S(2)}) async-start(), calls=%async_computation.3 | async-start | bytes 524288 | tf_op jit(solution)/shard_map/psum | solution.py:9
  378.6 2.0 copy-start
  381.3 292.3 %all-reduce.16.cloned.1.call-start = ((), (), s32[]{:S(2)}) async-start(), calls=%async_computation.4 | async-start | bytes 4194304 | tf_op jit(solution)/shard_map/psum | solution.py:9
  386.8 120.8 %copy-start.3 = (f32[256,8,256]{0,2,1:T(8,128)S(1)}, f32[256,8,256]{0,2,1:T(8,128)}, u32[]{:S(2)}) copy-start(f32[256,8,256]{0,2,1:T(8,128)} %copy.37) | copy-start | bytes 6291460
  517.2 218.5 %all-reduce.18.cloned.1.call-start = ((), (), s32[]{:S(2)}) async-start(), calls=%async_computation.5 | async-start | bytes 1048576 | tf_op jit(solution)/shard_map/psum | solution.py:9
  673.6 2.1 copy-start.2
Sparse Core Ops, SparseCore 0:
  19.2 63.5 all-reduce.7
  154.5 156.1 all-reduce.9
  313.0 59.7 all-reduce.11
  381.5 64.1 all-reduce.13
  517.4 156.2 all-reduce.15
  675.9 59.7 all-reduce.17
where the time goes:
time: 774 us; the launch traced here: 761 us
  waiting for transfers between devices  527 us (68%)
  other arithmetic  125 us (16%)
  local copies, waits for them, and re-layouts  65.9 us (9%)
  matrix products  21.8 us (3%)
  between operations  21.3 us (3%)
    psum x6, waiting for transfers between devices, broadcast(): return lax.psum(kept, axis)  527 us
    another operation x13, other arithmetic, factor_panel(): pivot = jnp.linalg.cholesky(broadcast(local[rk, :, ck, :], 'row', pk))  68.5 us
    another operation x7, other arithmetic, solve_rows(): lax.linalg.triangular_solve(pivot, stacked, left_side=True, lower=True)  40.4 us
  transfers between devices with their start and end apart: 6, of which 6 were waited for; matrix products, arithmetic and copies ran while one was open for 4% of the time, Pallas kernels for 0%

commit v1 on v0

v1 whole, which is shorter than its diff:
```python
import functools

import jax
import jax.numpy as jnp
import numpy as np
from jax import lax
from jax.experimental import pallas as pl
from jax.experimental.pallas import tpu as pltpu
from jax.sharding import PartitionSpec as P

AXES = ("row", "col")
NX, NCORE, NZ, NY = (4, 2, 8, 4)
BLK = 256
HALF = 128
STEP = 8
DEVICE = np.arange(NX * NCORE * NZ * NY).reshape(NX, NCORE, NZ, NY)
VMEM = pl.BlockSpec(memory_space=pltpu.VMEM)


def dot(a, b, contract=((1,), (0,))):
    return lax.dot_general(a, b, (contract, ((), ())), precision=lax.Precision.HIGHEST, preferred_element_type=jnp.float32)


def invert_factor(block):
    n = block.shape[0]
    lane = lax.broadcasted_iota(jnp.int32, (8, n), 1)
    sub = lax.broadcasted_iota(jnp.int32, (8, n), 0)
    rows = [block[8 * g : 8 * g + 8, :] for g in range(n // 8)]
    for first in range(0, n, STEP):
        top, at = divmod(first, 8)
        inside = (lane >= first) & (lane < first + STEP)
        low = range(top, n // 8)
        column = {
            g: [jnp.broadcast_to(rows[g][:, first + k : first + k + 1], (8, n)) for k in range(STEP)] for g in low
        }
        pivot = [
            [jnp.broadcast_to(column[top][k][at + i : at + i + 1, :], (8, n)) for k in range(i + 1)]
            for i in range(STEP)
        ]
        upper = [
            jnp.where(
                inside,
                (lane == first + k).astype(jnp.float32),
                jnp.broadcast_to(rows[top][at + k : at + k + 1, :], (8, n)),
            )
            for k in range(STEP)
        ]
        inverse = []
        for k in range(STEP):
            inverse.append(1.0 / pivot[k][k])
            for i in range(k + 1, STEP):
                ratio = pivot[i][k] * inverse[k]
                for m in range(k + 1, i + 1):
                    pivot[i][m] = pivot[i][m] - ratio * pivot[m][k]
                upper[i] = upper[i] - ratio * upper[k]
                for g in low:
                    column[g][i] = column[g][i] - ratio * column[g][k]
        scaled = [upper[k] * inverse[k] for k in range(STEP)]
        for g in low:
            left = jnp.where(inside, 0.0, rows[g])
            for k in range(STEP):
                left = left - column[g][k] * scaled[k]
            if g == top:
                done = rows[g]
                for k in range(STEP):
                    done = jnp.where(sub == at + k, upper[k] * lax.rsqrt(pivot[k][k]), done)
                left = jnp.where(sub >= at + STEP, left, done)
            rows[g] = left
    whole = jnp.concatenate(rows, axis=0)
    r = lax.broadcasted_iota(jnp.int32, (n, n), 0)
    c = lax.broadcasted_iota(jnp.int32, (n, n), 1)
    return jnp.where(c <= r, whole, 0.0)


def invert_pair(block, out):
    h = HALF
    top = invert_factor(block[:h, :h])
    link = dot(top, block[:h, h:])
    low = invert_factor(block[h:, h:] - dot(link, link, ((0,), (0,))))
    out[:h, :h] = top
    out[:h, h:] = jnp.zeros((h, h), jnp.float32)
    out[h:, :h] = -dot(dot(low, link, ((1,), (1,))), top)
    out[h:, h:] = low


def pivots_kernel(a00, a01, a11, inv00, u01, inv11):
    invert_pair(a00[...], inv00)
    link = dot(inv00[...], a01[...])
    u01[...] = link
    invert_pair(a11[...] - dot(link, link, ((0,), (0,))), inv11)


def factor_pivots(a00, a01, a11):
    shape = jax.ShapeDtypeStruct((BLK, BLK), jnp.float32)
    return pl.pallas_call(
        pivots_kernel,
        out_shape=(shape, shape, shape),
        in_specs=[VMEM] * 3,
        out_specs=[VMEM] * 3,
        compiler_params=pltpu.CompilerParams(vmem_limit_bytes=32 << 20),
        cost_estimate=pl.CostEstimate(flops=25_000_000_000, bytes_accessed=1 << 20, transcendentals=0),
        name="factor_pivots",
    )(a00, a01, a11)


def update_kernel(ids, pattern, local, g, y, inv00, u01, inv11, out, back0, back1, cols):
    j, h = (pl.program_id(0), pl.program_id(1))
    p, q = (ids[0], ids[1])
    row_id = (j + 4 * h) * 8 + p

    @pl.when((j == 0) & (h == 0))
    def _():
        back0[...] = inv00[...].T
        back1[...] = inv11[...].T
        for c in range(2):
            w = pattern[32 * c + q, 1].astype(jnp.float32)
            first = dot(inv00[...], y[0, c])
            cols[c, :BLK, :] = first
            cols[c, BLK:, :] = dot(inv11[...], y[1, c] - w * dot(u01[...], first, ((0,), (0,))))

    slots = [(ids[2] + 4 - 2 * h - part) % 4 for part in range(2)]
    raw = [jnp.concatenate([g[0, k, slots[0]], g[0, k, slots[1]]], axis=0) for k in range(2)]
    w1 = pattern[row_id, 1].astype(jnp.float32)
    x0 = dot(raw[0], back0[...])
    x1 = dot(raw[1] - w1 * dot(x0, u01[...]), back1[...])
    x = jnp.concatenate([x0, x1], axis=1)
    for c in range(2):
        col_id = 32 * c + q
        places = [pl.ds(2 * c + side, BLK, stride=4) for side in range(2)]

        def put(value):
            for side in range(2):
                out[0, places[side], :] = value[:, side * HALF : (side + 1) * HALF]

        panel = col_id < 2
        lower = row_id >= col_id
        changed = lower & ~panel & (pattern[row_id, col_id] != 0)

        @pl.when(panel)
        def _():
            r = lax.broadcasted_iota(jnp.int32, (BLK, BLK), 0)
            s = lax.broadcasted_iota(jnp.int32, (BLK, BLK), 1)
            kept = (row_id > col_id) | ((row_id == col_id) & (s <= r))
            put(jnp.where(kept, jnp.where(col_id == 0, x0, x1), 0.0))

        @pl.when(~panel & ~lower)
        def _():
            put(jnp.zeros((BLK, BLK), jnp.float32))

        @pl.when(changed)
        def _():
            for side in range(2):
                lanes = slice(side * HALF, (side + 1) * HALF)
                out[0, places[side], :] = local[0, places[side], :] - dot(x, cols[c, :, lanes])

        @pl.when(lower & ~panel & ~changed)
        def _():
            for side in range(2):
                out[0, places[side], :] = local[0, places[side], :]


def update(ids, pattern, local, g, y, inv00, u01, inv11):
    whole = lambda *shape: pl.BlockSpec(shape, lambda j, h, *_: (0,) * len(shape))
    return pl.pallas_call(
        update_kernel,
        out_shape=jax.ShapeDtypeStruct(local.shape, jnp.float32),
        grid_spec=pltpu.PrefetchScalarGridSpec(
            num_scalar_prefetch=2,
            grid=(4, 2),
            in_specs=[
                pl.BlockSpec((1, 4 * BLK, HALF), lambda j, h, *_: (j + 4 * h, 0, 0)),
                pl.BlockSpec((1, 2, 4, HALF, BLK), lambda j, h, *_: (j, 0, 0, 0, 0)),
                whole(2, 2, BLK, BLK),
                whole(BLK, BLK),
                whole(BLK, BLK),
                whole(BLK, BLK),
            ],
            out_specs=pl.BlockSpec((1, 4 * BLK, HALF), lambda j, h, *_: (j + 4 * h, 0, 0)),
            scratch_shapes=[
                pltpu.VMEM((BLK, BLK), jnp.float32),
                pltpu.VMEM((BLK, BLK), jnp.float32),
                pltpu.VMEM((2, 2 * BLK, BLK), jnp.float32),
            ],
        ),
        compiler_params=pltpu.CompilerParams(vmem_limit_bytes=32 << 20),
        cost_estimate=pl.CostEstimate(flops=12_000_000_000, bytes_accessed=14 << 20, transcendentals=0),
        name="update",
    )(ids, pattern, local, g, y, inv00, u01, inv11)


def shifted(value, x=0, core=0, z=0, y=0, where=None):
    pairs = []
    for place in np.ndindex(NX, NCORE, NZ, NY):
        if where is None or where(*place):
            a, b, c, d = place
            to = ((a + x) % NX, (b + core) % NCORE, (c + z) % NZ, (d + y) % NY)
            pairs.append((int(DEVICE[place]), int(DEVICE[to])))
    return lax.ppermute(value, AXES, pairs)


ROUNDS = (
    tuple(dict(z=k) for k in (2, 6, 4)),
    (dict(z=1),),
    tuple(dict(y=k) for k in (1, 3, 2)),
    tuple(dict(x=k) for k in (1, 3, 2)),
    (dict(core=1),),
)


def spread(value, root):
    have = {root}
    names = ("x", "core", "z", "y")
    sizes = (NX, NCORE, NZ, NY)
    for moves in ROUNDS:
        holders = frozenset(have)
        got = [shifted(value, where=lambda *place: place in holders, **move) for move in moves]
        for move in moves:
            have |= {tuple((s + move.get(n, 0)) % m for s, n, m in zip(place, names, sizes)) for place in holders}
        for one in got:
            value = value + one
    return value


def per_device(matrix, pattern):
    p = lax.axis_index("row")
    q = lax.axis_index("col")
    x, core, z, y = (p // NCORE, p % NCORE, q // NY, q % NY)
    local = matrix.reshape(8, 4 * BLK, HALF)
    head = matrix[0, 0, :, :, 0, :].transpose(1, 0, 2)
    turned = head.transpose(0, 2, 1).reshape(4, HALF, BLK)

    parts = []
    for m in range(4):
        pairs = [(32 * c + s, (s % 8) * 32 + 8 * (s // 8) + 4 * c + m) for c in range(2) for s in range(32)]
        parts.append(lax.ppermute(turned[m], AXES, pairs))
    mine = parts[0] + parts[1] + parts[2] + parts[3]
    quarters = jnp.stack([mine] + [shifted(mine, y=k) for k in (1, 2, 3)])
    groups = [[NY * b + a for b in range(NZ)] for a in range(NY)]
    rows = lax.all_gather(quarters, "col", axis=0, axis_index_groups=groups)
    rows = rows.reshape(4, 2, 4, HALF, BLK)

    here = (x == 0) & (z == 0)
    own = head[0]
    a00 = spread(jnp.where(here & (core == 0) & (y == 0), own, 0.0), (0, 0, 0, 0))
    below = shifted(own, core=1, where=lambda *place: place == (0, 1, 0, 1))
    pair = jnp.where(here & (core == 0) & (y == 1), jnp.stack([own, below]), 0.0)
    pair = spread(pair, (0, 0, 0, 1))

    first = jnp.where(x == 0, head, 0.0)
    cols = first
    for k in (1, 3, 2):
        cols = cols + shifted(first, x=k, where=lambda a, *_: a == 0)
    other = shifted(cols, core=1)
    panel = jnp.where(core == 0, jnp.stack([cols, other]), jnp.stack([other, cols]))

    inv00, u01, inv11 = factor_pivots(a00, pair[0], pair[1])
    ids = jnp.stack([p, q, y]).astype(jnp.int32)
    out = update(ids, pattern, local, rows, panel, inv00, u01, inv11)
    return out.reshape(matrix.shape)


def solution(mesh):
    return jax.shard_map(
        per_device,
        mesh=mesh,
        in_specs=(P(None, "row", None, None, "col", None), P()),
        out_specs=P(None, "row", None, None, "col", None),
        check_vma=False,
    )
```

time: 774 us -> 197 us (0.25); the launches traced: 761 us -> 194 us
  waiting for transfers between devices: 527 us -> 98.1 us
  other arithmetic: 125 us -> 2.11 us
  local copies, waits for them, and re-layouts: 65.9 us -> 6.42 us
  Pallas kernels: 0 us -> 45.9 us
  starting transfers between devices: 0.21 us -> 27.5 us
  matrix products: 21.8 us -> 0 us
    psum x6 -> x0, waiting for transfers between devices: 527 us -> none  [broadcast(): return lax.psum(kept, axis)]
    another operation x20 -> x2, other arithmetic: 109 us -> 0.91 us  [the longest x1 0.83 us: per_device(): quarters = jnp.stack([mine] + [shifted(mine, y=k) for k in (1, 2, 3)])]
    ppermute x0 -> x34, waiting for transfers between devices: none -> 98.1 us  [the longest x30 87.3 us: shifted(): return lax.ppermute(value, AXES, pairs)]
    pallas_call x0 -> x2, Pallas kernels: none -> 45.9 us  [the longest x1 24.3 us: update(): pl.pallas_call(update_kernel, out_shape=jax.ShapeDtypeStruct(local.shape,...]
    ppermute x0 -> x34, starting transfers between devices: none -> 27.5 us  [the longest x30 24.2 us: shifted(): return lax.ppermute(value, AXES, pairs)]
    dot_general x2 -> x0, matrix products: 12.9 us -> none  [apply_update(): jnp.einsum('rab,cdb->racd', row_panel, col_panel, precision=lax.Precision...]
    mul x3 -> x0, local copies, waits for them, and re-layouts: 11 us -> none  [the longest x1 10.9 us: per_device(): local = local * lower_mask[:, None, :, None]]
    squeeze x1 -> x2, local copies, waits for them, and re-layouts: 10.9 us -> 0.07 us  [the longest x1 0.04 us: per_device(): parts.append(lax.ppermute(turned[m], AXES, pairs))]
  transfers between devices with their start and end apart: 6 -> 35, of which waited for: 6 -> 8; matrix products, arithmetic and copies ran while one was open for 4% -> 1% of each run, Pallas kernels for 0% -> 11%
where the time goes in v1:
time: 197 us; the launch traced here: 194 us
  waiting for transfers between devices  98.1 us (50%)
  Pallas kernels  45.9 us (23%)
  starting transfers between devices  27.5 us (14%)
  between operations  14.1 us (7%)
  local copies, waits for them, and re-layouts  6.42 us (3%)
  other arithmetic  2.11 us (1%)
    ppermute x30, waiting for transfers between devices, shifted(): return lax.ppermute(value, AXES, pairs)  87.3 us
    pallas_call x1, Pallas kernels, update(): pl.pallas_call(update_kernel, out_shape=jax.ShapeDtypeStruct(local.shape,...  24.3 us
    ppermute x30, starting transfers between devices, shifted(): return lax.ppermute(value, AXES, pairs)  24.2 us
    pallas_call x1, Pallas kernels, factor_pivots(): pl.pallas_call(pivots_kernel, out_shape=(shape, shape, shape), in_specs=[...  21.6 us
    ppermute x4, waiting for transfers between devices, per_device(): parts.append(lax.ppermute(turned[m], AXES, pairs))  10.8 us
    unnamed x7, local copies, waits for them, and re-layouts  4.41 us
  transfers between devices with their start and end apart: 35, of which 8 were waited for; matrix products, arithmetic and copies ran while one was open for 1% of the time, Pallas kernels for 11%

profile of v1, /device:TPU:36, one launch (start us, length us, event | category | flops | bytes accessed | tf_op | source)
XLA Modules:
  0.0 194.1 jit_solution(17659577507133734174)
XLA Ops:
  6.5 1.4 slice.24
  7.9 0.5 copy.12
  8.5 0.7 collective-permute-start.1
  9.2 0.7 collective-permute-start.3
  9.8 0.7 collective-permute-start.2
  10.5 1.3 collective-permute-start
  11.9 10.8 %collective-permute-done = f32[128,256]{1,0:T(8,128)S(1)} collective-permute-done((f32[128,256]{1,0:T(8,128)S(1)}, f32[128,256]{1,0:T(8,128)S(1)}, u32[]{:S(2)}, u32[]{:S(2)}) %collective-permute-start) | collective-permute-done | bytes 131104 | tf_op jit(solution)/shard_map/ppermute | solution.py:235
  22.7 0.7 collective-permute-start.6
  23.3 1.0 collective-permute-start.5
  24.4 1.3 collective-permute-start.4
  25.7 3.0 %collective-permute-done.6 = f32[128,256]{1,0:T(8,128)S(1)} collective-permute-done((f32[128,256]{1,0:T(8,128)S(1)}, f32[128,256]{1,0:T(8,128)S(1)}, u32[]{:S(2)}, u32[]{:S(2)}) %collective-permute-start.6) | collective-permute-done | bytes 131104 | tf_op jit(solution)/shard_map/ppermute | solution.py:198
  28.7 2.3 %collective-permute-done.5 = f32[128,256]{1,0:T(8,128)S(1)} collective-permute-done((f32[128,256]{1,0:T(8,128)S(1)}, f32[128,256]{1,0:T(8,128)S(1)}, u32[]{:S(2)}, u32[]{:S(2)}) %collective-permute-start.5) | collective-permute-done | bytes 131104 | tf_op jit(solution)/shard_map/ppermute | solution.py:198
  31.0 1.4 collective-permute-done.4
  32.3 0.8 pad_maximum_fusion
  33.2 0.0 all-gather.3.cloned.1.call-update
  33.3 0.7 collective-permute-start.22
  34.1 0.7 collective-permute-start.24
  34.8 0.7 collective-permute-start.25
  35.5 0.7 collective-permute-start.23
  36.2 0.1 add_add_fusion.2
  36.4 0.7 collective-permute-start.26
  37.1 0.7 collective-permute-start.12
  37.8 0.7 collective-permute-start.13
  38.5 0.7 collective-permute-start.11
  39.2 0.1 add.115
  39.2 0.7 collective-permute-start.29
  39.9 0.7 collective-permute-start.28
  40.7 0.7 collective-permute-start.27
  41.4 0.1 add_add_fusion.6
  41.5 0.7 collective-permute-start.14
  42.1 0.1 broadcast_select_fusion
  42.2 0.7 collective-permute-start.8
  42.9 1.3 collective-permute-start.9
  44.2 0.7 collective-permute-start.7
  45.0 0.7 collective-permute-start.17
  45.7 0.7 collective-permute-start.16
  46.4 0.1 add_add_fusion.1
  46.5 0.7 collective-permute-start.15
  47.2 41.4 %collective-permute-done.9 = f32[2,256,256]{2,1,0:T(8,128)S(1)} collective-permute-done((f32[2,256,256]{2,1,0:T(8,128)S(1)}, f32[2,256,256]{2,1,0:T(8,128)S(1)}, u32[]{:S(2)}, u32[]{:S(2)}) %collective-permute-start.9) | collective-permute-done | bytes 524320 | tf_op jit(solution)/shard_map/ppermute | solution.py:198
  88.6 1.3 collective-permute-start.32
  89.9 0.7 collective-permute-start.31
  90.6 0.7 collective-permute-start.30
  91.3 0.1 add_add_fusion.3
  91.5 0.1 collective-permute-start.10
  91.6 0.1 add_add_fusion.5
  91.6 1.3 collective-permute-start.20
  92.9 32.9 %collective-permute-done.32 = f32[2,256,256]{2,1,0:T(8,128)S(1)} collective-permute-done((f32[2,256,256]{2,1,0:T(8,128)S(1)}, f32[2,256,256]{2,1,0:T(8,128)S(1)}, u32[]{:S(2)}, u32[]{:S(2)}) %collective-permute-start.32) | collective-permute-done | bytes 524320 | tf_op jit(solution)/shard_map/ppermute | solution.py:198
  125.8 0.7 collective-permute-start.19
  126.5 0.7 collective-permute-start.18
  127.2 0.1 add_add_fusion
  127.3 1.3 collective-permute-start.33
  128.7 5.6 %collective-permute-done.20 = f32[256,256]{1,0:T(8,128)S(1)} collective-permute-done((f32[256,256]{1,0:T(8,128)S(1)}, f32[256,256]{1,0:T(8,128)S(1)}, u32[]{:S(2)}, u32[]{:S(2)}) %collective-permute-start.20) | collective-permute-done | bytes 262176 | tf_op jit(solution)/shard_map/ppermute | solution.py:198
  134.2 0.1 add_add_fusion.4
  134.3 1.5 collective-permute-start.21
  135.8 0.1 pad_add_fusion.ids
  135.9 0.1 maximum_select_fusion.y
  136.0 0.8 collective-permute-done.21
  136.8 0.1 add.122
  136.9 0.0 copy-start.2
  136.9 21.6 %factor_pivots.1 = (f32[256,256]{1,0:T(8,128)S(1)}, f32[256,256]{1,0:T(8,128)S(1)}, f32[256,256]{1,0:T(8,128)S(1)}) custom-call(f32[256,256]{1,0:T(8,128)S(1)} %add.111.a00, f32[256,256]{1,0:T(8,128)S(1)} %get-tuple-element.12.a01, f32[256,256]{1,0:T(8,128)S(1)} %get-tuple-element.11.a11), custom_call_target="tpu_custom_call" | custom-call | flops 24999999488 | bytes 1048576 | tf_op jit(solution)/shard_map/factor_pivots/pallas_call | solution.py:95
  158.5 0.0 all-gather.3.cloned.1.call-done
  158.6 2.2 %copy-done = f32[8,1,256,2,1,256]{5,4,3,2,1,0:T(1,128)S(1)} copy-done((f32[8,1,256,2,1,256]{5,4,3,2,1,0:T(1,128)S(1)}, f32[8,1,256,2,1,256]{5,4,3,2,1,0:T(1,128)}, u32[]{:S(2)}) %copy-start) | copy-done | bytes 4194328
  160.8 2.2 %copy-done.1 = f32[32,128,256]{2,1,0:T(8,128)S(1)} copy-done((f32[32,128,256]{2,1,0:T(8,128)S(1)}, f32[32,128,256]{2,1,0:T(8,128)}, u32[]{:S(2)}) %copy-start.1) | copy-done | bytes 4194328
  163.0 24.3 %update.1 = f32[8,1024,128]{2,1,0:T(8,128)} custom-call(s32[3]{0:T(128)S(1)} %pad_add_fusion.ids, s32[64,64]{1,0:T(8,128)S(1)} %copy-done.2, f32[8,1024,128]{2,1,0:T(8,128)S(1)} %bitcast.44, f32[4,2,4,128,256]{4,3,2,1,0:T(8,128)S(1)} %bitcast.45, f32[2,2,256,256]{3,2,1,0:T(8,128)S(1)} %maximum_select_fusion.y, f32[256,256]{1,0:T(8,128)S(1)} %get-tuple-element.8.inv00, ...), custom_call_target="tpu_custom_call" | custom-call | flops 12000000000 | bytes 14680064 | tf_op jit(solution)/shard_map/update/pallas_call | solution.py:164
  (39 shorter events, 0.4 us)
Async XLA Ops:
  6.5 152.0 %all-gather.3.cloned.1.call-start = ((), (), s32[]{:S(2)}) async-start(), calls=%async_computation | async-start | bytes 4718592 | tf_op jit(solution)/shard_map/all_gather | solution.py:239
  8.5 3.3 %collective-permute-start.1 = (f32[128,256]{1,0:T(8,128)S(1)}, f32[128,256]{1,0:T(8,128)S(1)}, u32[]{:S(2)}, u32[]{:S(2)}) collective-permute-start(f32[128,256]{1,0:T(8,128)S(1)} %get-tuple-element.15), channel_id=1, source_target_pairs={{0,1},{1,33},{2,65},{3,97},{4,129},{5,161},{6,193},{7,225},{8,9},{... | collective-permute-start | bytes 393224 | tf_op jit(solution)/shard_map/ppermute | solution.py:235
  9.2 2.7 %collective-permute-start.3 = (f32[128,256]{1,0:T(8,128)S(1)}, f32[128,256]{1,0:T(8,128)S(1)}, u32[]{:S(2)}, u32[]{:S(2)}) collective-permute-start(f32[128,256]{1,0:T(8,128)S(1)} %get-tuple-element.16), channel_id=1, source_target_pairs={{0,3},{1,35},{2,67},{3,99},{4,131},{5,163},{6,195},{7,227},{8,11},... | collective-permute-start | bytes 393224 | tf_op jit(solution)/shard_map/ppermute | solution.py:235
  9.8 2.0 %collective-permute-start.2 = (f32[128,256]{1,0:T(8,128)S(1)}, f32[128,256]{1,0:T(8,128)S(1)}, u32[]{:S(2)}, u32[]{:S(2)}) collective-permute-start(f32[128,256]{1,0:T(8,128)S(1)} %get-tuple-element.17), channel_id=1, source_target_pairs={{0,2},{1,34},{2,66},{3,98},{4,130},{5,162},{6,194},{7,226},{8,10},... | collective-permute-start | bytes 393224 | tf_op jit(solution)/shard_map/ppermute | solution.py:235
  10.5 12.1 %collective-permute-start = (f32[128,256]{1,0:T(8,128)S(1)}, f32[128,256]{1,0:T(8,128)S(1)}, u32[]{:S(2)}, u32[]{:S(2)}) collective-permute-start(f32[128,256]{1,0:T(8,128)S(1)} %get-tuple-element.18), channel_id=1, source_target_pairs={{0,0},{1,32},{2,64},{3,96},{4,128},{5,160},{6,192},{7,224},{8,8},{... | collective-permute-start | bytes 393224 | tf_op jit(solution)/shard_map/ppermute | solution.py:235
  22.7 6.0 %collective-permute-start.6 = (f32[128,256]{1,0:T(8,128)S(1)}, f32[128,256]{1,0:T(8,128)S(1)}, u32[]{:S(2)}, u32[]{:S(2)}) collective-permute-start(f32[128,256]{1,0:T(8,128)S(1)} %add_add_fusion.7), channel_id=1, source_target_pairs={{0,3},{1,0},{2,1},{3,2},{4,7},{5,4},{6,5},{7,6},{8,11},{9,8},{10,9... | collective-permute-start | bytes 393224 | tf_op jit(solution)/shard_map/ppermute | solution.py:198
  23.3 7.6 %collective-permute-start.5 = (f32[128,256]{1,0:T(8,128)S(1)}, f32[128,256]{1,0:T(8,128)S(1)}, u32[]{:S(2)}, u32[]{:S(2)}) collective-permute-start(f32[128,256]{1,0:T(8,128)S(1)} %add_add_fusion.7), channel_id=1, source_target_pairs={{0,2},{1,3},{2,0},{3,1},{4,6},{5,7},{6,4},{7,5},{8,10},{9,11},{10,... | collective-permute-start | bytes 393224 | tf_op jit(solution)/shard_map/ppermute | solution.py:198
  24.4 7.9 %collective-permute-start.4 = (f32[128,256]{1,0:T(8,128)S(1)}, f32[128,256]{1,0:T(8,128)S(1)}, u32[]{:S(2)}, u32[]{:S(2)}) collective-permute-start(f32[128,256]{1,0:T(8,128)S(1)} %add_add_fusion.7), channel_id=1, source_target_pairs={{0,1},{1,2},{2,3},{3,0},{4,5},{5,6},{6,7},{7,4},{8,9},{9,10},{10,1... | collective-permute-start | bytes 393224 | tf_op jit(solution)/shard_map/ppermute | solution.py:198
  33.3 0.7 collective-permute-start.22
  34.1 2.1 %collective-permute-start.24 = (f32[2,256,256]{2,1,0:T(8,128)S(1)}, f32[2,256,256]{2,1,0:T(8,128)S(1)}, u32[]{:S(2)}, u32[]{:S(2)}) collective-permute-start(f32[2,256,256]{2,1,0:T(8,128)S(1)} %maximum_select_fusion.1), channel_id=1, source_target_pairs={{1,25}} | collective-permute-start | bytes 1572872 | tf_op jit(solution)/shard_map/ppermute | solution.py:198
  34.8 1.4 collective-permute-start.25
  35.5 0.7 collective-permute-start.23
  36.4 2.8 %collective-permute-start.26 = (f32[2,256,256]{2,1,0:T(8,128)S(1)}, f32[2,256,256]{2,1,0:T(8,128)S(1)}, u32[]{:S(2)}, u32[]{:S(2)}) collective-permute-start(f32[2,256,256]{2,1,0:T(8,128)S(1)} %add_add_fusion.2), channel_id=1, source_target_pairs={{1,5},{9,13},{17,21},{25,29}} | collective-permute-start | bytes 1572872 | tf_op jit(solution)/shard_map/ppermute | solution.py:198
  37.1 3.5 %collective-permute-start.12 = (f32[256,256]{1,0:T(8,128)S(1)}, f32[256,256]{1,0:T(8,128)S(1)}, u32[]{:S(2)}, u32[]{:S(2)}) collective-permute-start(f32[256,256]{1,0:T(8,128)S(1)} %broadcast_select_fusion.1), channel_id=1, source_target_pairs={{0,24}} | collective-permute-start | bytes 786440 | tf_op jit(solution)/shard_map/ppermute | solution.py:198
  37.8 3.6 %collective-permute-start.13 = (f32[256,256]{1,0:T(8,128)S(1)}, f32[256,256]{1,0:T(8,128)S(1)}, u32[]{:S(2)}, u32[]{:S(2)}) collective-permute-start(f32[256,256]{1,0:T(8,128)S(1)} %broadcast_select_fusion.1), channel_id=1, source_target_pairs={{0,16}} | collective-permute-start | bytes 786440 | tf_op jit(solution)/shard_map/ppermute | solution.py:198
  38.5 2.9 %collective-permute-start.11 = (f32[256,256]{1,0:T(8,128)S(1)}, f32[256,256]{1,0:T(8,128)S(1)}, u32[]{:S(2)}, u32[]{:S(2)}) collective-permute-start(f32[256,256]{1,0:T(8,128)S(1)} %broadcast_select_fusion.1), channel_id=1, source_target_pairs={{0,8}} | collective-permute-start | bytes 786440 | tf_op jit(solution)/shard_map/ppermute | solution.py:198
  39.2 5.0 %collective-permute-start.29 = (f32[2,256,256]{2,1,0:T(8,128)S(1)}, f32[2,256,256]{2,1,0:T(8,128)S(1)}, u32[]{:S(2)}, u32[]{:S(2)}) collective-permute-start(f32[2,256,256]{2,1,0:T(8,128)S(1)} %add.115), channel_id=1, source_target_pairs={{1,3},{5,7},{9,11},{13,15},{17,19},{21,23},{25,27},{29,31}} | collective-permute-start | bytes 1572872 | tf_op jit(solution)/shard_map/ppermute | solution.py:198
  39.9 5.0 %collective-permute-start.28 = (f32[2,256,256]{2,1,0:T(8,128)S(1)}, f32[2,256,256]{2,1,0:T(8,128)S(1)}, u32[]{:S(2)}, u32[]{:S(2)}) collective-permute-start(f32[2,256,256]{2,1,0:T(8,128)S(1)} %add.115), channel_id=1, source_target_pairs={{1,0},{5,4},{9,8},{13,12},{17,16},{21,20},{25,24},{29,28}} | collective-permute-start | bytes 1572872 | tf_op jit(solution)/shard_map/ppermute | solution.py:198
  40.7 5.0 %collective-permute-start.27 = (f32[2,256,256]{2,1,0:T(8,128)S(1)}, f32[2,256,256]{2,1,0:T(8,128)S(1)}, u32[]{:S(2)}, u32[]{:S(2)}) collective-permute-start(f32[2,256,256]{2,1,0:T(8,128)S(1)} %add.115), channel_id=1, source_target_pairs={{1,2},{5,6},{9,10},{13,14},{17,18},{21,22},{25,26},{29,30}} | collective-permute-start | bytes 1572872 | tf_op jit(solution)/shard_map/ppermute | solution.py:198
  41.5 1.5 collective-permute-start.14
  42.2 4.3 %collective-permute-start.8 = (f32[2,256,256]{2,1,0:T(8,128)S(1)}, f32[2,256,256]{2,1,0:T(8,128)S(1)}, u32[]{:S(2)}, u32[]{:S(2)}) collective-permute-start(f32[2,256,256]{2,1,0:T(8,128)S(1)} %broadcast_select_fusion), channel_id=1, source_target_pairs={{0,192},{1,193},{2,194},{3,195},{4,196},{5,197},{6,198},{7,199},{8... | collective-permute-start | bytes 1572872 | tf_op jit(solution)/shard_map/ppermute | solution.py:198
  42.9 45.7 %collective-permute-start.9 = (f32[2,256,256]{2,1,0:T(8,128)S(1)}, f32[2,256,256]{2,1,0:T(8,128)S(1)}, u32[]{:S(2)}, u32[]{:S(2)}) collective-permute-start(f32[2,256,256]{2,1,0:T(8,128)S(1)} %broadcast_select_fusion), channel_id=1, source_target_pairs={{0,128},{1,129},{2,130},{3,131},{4,132},{5,133},{6,134},{7,135},{8... | collective-permute-start | bytes 1572872 | tf_op jit(solution)/shard_map/ppermute | solution.py:198
  44.2 45.6 %collective-permute-start.7 = (f32[2,256,256]{2,1,0:T(8,128)S(1)}, f32[2,256,256]{2,1,0:T(8,128)S(1)}, u32[]{:S(2)}, u32[]{:S(2)}) collective-permute-start(f32[2,256,256]{2,1,0:T(8,128)S(1)} %broadcast_select_fusion), channel_id=1, source_target_pairs={{0,64},{1,65},{2,66},{3,67},{4,68},{5,69},{6,70},{7,71},{8,72},{9,... | collective-permute-start | bytes 1572872 | tf_op jit(solution)/shard_map/ppermute | solution.py:198
  45.0 45.6 %collective-permute-start.17 = (f32[256,256]{1,0:T(8,128)S(1)}, f32[256,256]{1,0:T(8,128)S(1)}, u32[]{:S(2)}, u32[]{:S(2)}) collective-permute-start(f32[256,256]{1,0:T(8,128)S(1)} %add.104), channel_id=1, source_target_pairs={{0,2},{4,6},{8,10},{12,14},{16,18},{20,22},{24,26},{28,30}} | collective-permute-start | bytes 786440 | tf_op jit(solution)/shard_map/ppermute | solution.py:198
  45.7 45.8 %collective-permute-start.16 = (f32[256,256]{1,0:T(8,128)S(1)}, f32[256,256]{1,0:T(8,128)S(1)}, u32[]{:S(2)}, u32[]{:S(2)}) collective-permute-start(f32[256,256]{1,0:T(8,128)S(1)} %add.104), channel_id=1, source_target_pairs={{0,3},{4,7},{8,11},{12,15},{16,19},{20,23},{24,27},{28,31}} | collective-permute-start | bytes 786440 | tf_op jit(solution)/shard_map/ppermute | solution.py:198
  46.5 45.0 %collective-permute-start.15 = (f32[256,256]{1,0:T(8,128)S(1)}, f32[256,256]{1,0:T(8,128)S(1)}, u32[]{:S(2)}, u32[]{:S(2)}) collective-permute-start(f32[256,256]{1,0:T(8,128)S(1)} %add.104), channel_id=1, source_target_pairs={{0,1},{4,5},{8,9},{12,13},{16,17},{20,21},{24,25},{28,29}} | collective-permute-start | bytes 786440 | tf_op jit(solution)/shard_map/ppermute | solution.py:198
  88.6 37.2 %collective-permute-start.32 = (f32[2,256,256]{2,1,0:T(8,128)S(1)}, f32[2,256,256]{2,1,0:T(8,128)S(1)}, u32[]{:S(2)}, u32[]{:S(2)}) collective-permute-start(f32[2,256,256]{2,1,0:T(8,128)S(1)} %add_add_fusion.1), channel_id=1, source_target_pairs={{0,128},{1,129},{2,130},{3,131},{4,132},{5,133},{6,134},{7,135},{8... | collective-permute-start | bytes 1572872 | tf_op jit(solution)/shard_map/ppermute | solution.py:198
  89.9 36.6 %collective-permute-start.31 = (f32[2,256,256]{2,1,0:T(8,128)S(1)}, f32[2,256,256]{2,1,0:T(8,128)S(1)}, u32[]{:S(2)}, u32[]{:S(2)}) collective-permute-start(f32[2,256,256]{2,1,0:T(8,128)S(1)} %add_add_fusion.1), channel_id=1, source_target_pairs={{0,192},{1,193},{2,194},{3,195},{4,196},{5,197},{6,198},{7,199},{8... | collective-permute-start | bytes 1572872 | tf_op jit(solution)/shard_map/ppermute | solution.py:198
  90.6 36.6 %collective-permute-start.30 = (f32[2,256,256]{2,1,0:T(8,128)S(1)}, f32[2,256,256]{2,1,0:T(8,128)S(1)}, u32[]{:S(2)}, u32[]{:S(2)}) collective-permute-start(f32[2,256,256]{2,1,0:T(8,128)S(1)} %add_add_fusion.1), channel_id=1, source_target_pairs={{0,64},{1,65},{2,66},{3,67},{4,68},{5,69},{6,70},{7,71},{8,72},{9,... | collective-permute-start | bytes 1572872 | tf_op jit(solution)/shard_map/ppermute | solution.py:198
  91.5 44.4 %collective-permute-start.10 = (f32[2,256,256]{2,1,0:T(8,128)S(1)}, f32[2,256,256]{2,1,0:T(8,128)S(1)}, u32[]{:S(2)}, u32[]{:S(2)}) collective-permute-start(f32[2,256,256]{2,1,0:T(8,128)S(1)} %add_add_fusion.3), channel_id=1, source_target_pairs={{0,32},{1,33},{2,34},{3,35},{4,36},{5,37},{6,38},{7,39},{8,40},{9,... | collective-permute-start | bytes 1572872 | tf_op jit(solution)/shard_map/ppermute | solution.py:198
  91.6 42.6 %collective-permute-start.20 = (f32[256,256]{1,0:T(8,128)S(1)}, f32[256,256]{1,0:T(8,128)S(1)}, u32[]{:S(2)}, u32[]{:S(2)}) collective-permute-start(f32[256,256]{1,0:T(8,128)S(1)} %add_add_fusion.5), channel_id=1, source_target_pairs={{0,128},{1,129},{2,130},{3,131},{4,132},{5,133},{6,134},{7,135},{8... | collective-permute-start | bytes 786440 | tf_op jit(solution)/shard_map/ppermute | solution.py:198
  125.8 8.4 %collective-permute-start.19 = (f32[256,256]{1,0:T(8,128)S(1)}, f32[256,256]{1,0:T(8,128)S(1)}, u32[]{:S(2)}, u32[]{:S(2)}) collective-permute-start(f32[256,256]{1,0:T(8,128)S(1)} %add_add_fusion.5), channel_id=1, source_target_pairs={{0,192},{1,193},{2,194},{3,195},{4,196},{5,197},{6,198},{7,199},{8... | collective-permute-start | bytes 786440 | tf_op jit(solution)/shard_map/ppermute | solution.py:198
  126.5 7.7 %collective-permute-start.18 = (f32[256,256]{1,0:T(8,128)S(1)}, f32[256,256]{1,0:T(8,128)S(1)}, u32[]{:S(2)}, u32[]{:S(2)}) collective-permute-start(f32[256,256]{1,0:T(8,128)S(1)} %add_add_fusion.5), channel_id=1, source_target_pairs={{0,64},{1,65},{2,66},{3,67},{4,68},{5,69},{6,70},{7,71},{8,72},{9,... | collective-permute-start | bytes 786440 | tf_op jit(solution)/shard_map/ppermute | solution.py:198
  127.3 9.5 %collective-permute-start.33 = (f32[2,256,256]{2,1,0:T(8,128)S(1)}, f32[2,256,256]{2,1,0:T(8,128)S(1)}, u32[]{:S(2)}, u32[]{:S(2)}) collective-permute-start(f32[2,256,256]{2,1,0:T(8,128)S(1)} %add_add_fusion), channel_id=1, source_target_pairs={{0,32},{1,33},{2,34},{3,35},{4,36},{5,37},{6,38},{7,39},{8,40},{9,... | collective-permute-start | bytes 1572872 | tf_op jit(solution)/shard_map/ppermute | solution.py:198
  134.3 2.4 %collective-permute-start.21 = (f32[256,256]{1,0:T(8,128)S(1)}, f32[256,256]{1,0:T(8,128)S(1)}, u32[]{:S(2)}, u32[]{:S(2)}) collective-permute-start(f32[256,256]{1,0:T(8,128)S(1)} %add_add_fusion.4), channel_id=1, source_target_pairs={{0,32},{1,33},{2,34},{3,35},{4,36},{5,37},{6,38},{7,39},{8,40},{9,... | collective-permute-start | bytes 786440 | tf_op jit(solution)/shard_map/ppermute | solution.py:198
  136.9 21.7 %copy-start.2 = (s32[64,64]{1,0:T(8,128)S(1)}, s32[64,64]{1,0:T(8,128)}, u32[]{:S(2)}) copy-start(s32[64,64]{1,0:T(8,128)} %pattern.1) | copy-start | bytes 49156
  158.6 2.2 %copy-start = (f32[8,1,256,2,1,256]{5,4,3,2,1,0:T(1,128)S(1)}, f32[8,1,256,2,1,256]{5,4,3,2,1,0:T(1,128)}, u32[]{:S(2)}) copy-start(f32[8,1,256,2,1,256]{5,4,3,2,1,0:T(1,128)} %param.2) | copy-start | bytes 12582916
  160.8 2.2 %copy-start.1 = (f32[32,128,256]{2,1,0:T(8,128)S(1)}, f32[32,128,256]{2,1,0:T(8,128)}, u32[]{:S(2)}) copy-start(f32[32,128,256]{2,1,0:T(8,128)} %all-gather.3.cloned.1.call-done) | copy-start | bytes 12582916
Sparse Core Ops, SparseCore 0:
  33.3 56.6 all-gather.2

commit v2 on v1

v2 whole, which is shorter than its diff:
```python
import functools

import jax
import jax.numpy as jnp
import numpy as np
from jax import lax
from jax.experimental import pallas as pl
from jax.experimental.pallas import tpu as pltpu
from jax.sharding import PartitionSpec as P

AXES = ("row", "col")
NX, NCORE, NZ, NY = (4, 2, 8, 4)
BLK = 256
HALF = 128
STEP = 8
DEVICE = np.arange(NX * NCORE * NZ * NY).reshape(NX, NCORE, NZ, NY)
VMEM = pl.BlockSpec(memory_space=pltpu.VMEM)


def dot(a, b, contract=((1,), (0,))):
    return lax.dot_general(a, b, (contract, ((), ())), precision=lax.Precision.HIGHEST, preferred_element_type=jnp.float32)


def invert_factor(block):
    n = block.shape[0]
    lane = lax.broadcasted_iota(jnp.int32, (8, n), 1)
    sub = lax.broadcasted_iota(jnp.int32, (8, n), 0)
    rows = [block[8 * g : 8 * g + 8, :] for g in range(n // 8)]
    for first in range(0, n, STEP):
        top, at = divmod(first, 8)
        inside = (lane >= first) & (lane < first + STEP)
        low = range(top, n // 8)
        column = {
            g: [jnp.broadcast_to(rows[g][:, first + k : first + k + 1], (8, n)) for k in range(STEP)] for g in low
        }
        pivot = [
            [jnp.broadcast_to(column[top][k][at + i : at + i + 1, :], (8, n)) for k in range(i + 1)]
            for i in range(STEP)
        ]
        upper = [
            jnp.where(
                inside,
                (lane == first + k).astype(jnp.float32),
                jnp.broadcast_to(rows[top][at + k : at + k + 1, :], (8, n)),
            )
            for k in range(STEP)
        ]
        inverse = []
        for k in range(STEP):
            inverse.append(1.0 / pivot[k][k])
            for i in range(k + 1, STEP):
                ratio = pivot[i][k] * inverse[k]
                for m in range(k + 1, i + 1):
                    pivot[i][m] = pivot[i][m] - ratio * pivot[m][k]
                upper[i] = upper[i] - ratio * upper[k]
                for g in low:
                    column[g][i] = column[g][i] - ratio * column[g][k]
        scaled = [upper[k] * inverse[k] for k in range(STEP)]
        for g in low:
            left = jnp.where(inside, 0.0, rows[g])
            for k in range(STEP):
                left = left - column[g][k] * scaled[k]
            if g == top:
                done = rows[g]
                for k in range(STEP):
                    done = jnp.where(sub == at + k, upper[k] * lax.rsqrt(pivot[k][k]), done)
                left = jnp.where(sub >= at + STEP, left, done)
            rows[g] = left
    whole = jnp.concatenate(rows, axis=0)
    r = lax.broadcasted_iota(jnp.int32, (n, n), 0)
    c = lax.broadcasted_iota(jnp.int32, (n, n), 1)
    return jnp.where(c <= r, whole, 0.0)


def invert_pair(block, out):
    h = HALF
    top = invert_factor(block[:h, :h])
    link = dot(top, block[:h, h:])
    low = invert_factor(block[h:, h:] - dot(link, link, ((0,), (0,))))
    out[:h, :h] = top
    out[:h, h:] = jnp.zeros((h, h), jnp.float32)
    out[h:, :h] = -dot(dot(low, link, ((1,), (1,))), top)
    out[h:, h:] = low


def first_kernel(a00, inv00):
    invert_pair(a00[...], inv00)


def second_kernel(inv00, a01, a11, u01, inv11):
    link = dot(inv00[...], a01[...])
    u01[...] = link
    invert_pair(a11[...] - dot(link, link, ((0,), (0,))), inv11)


def on_blocks(kernel, outs, name, *blocks):
    shape = jax.ShapeDtypeStruct((BLK, BLK), jnp.float32)
    return pl.pallas_call(
        kernel,
        out_shape=(shape,) * outs,
        in_specs=[VMEM] * len(blocks),
        out_specs=[VMEM] * outs,
        compiler_params=pltpu.CompilerParams(vmem_limit_bytes=32 << 20),
        cost_estimate=pl.CostEstimate(flops=12_000_000_000, bytes_accessed=1 << 20, transcendentals=0),
        name=name,
    )(*blocks)


LEFT = {3: (0, 0, 1, 0, 1, 2), 2: (0, 1, 0)}
RIGHT = {3: (0, 1, 0, 2, 1, 0), 2: (0, 0, 1)}


def split(value, count=3):
    parts = []
    for number in range(count):
        parts.append(value.astype(jnp.bfloat16))
        if number + 1 < count:
            value = value - parts[-1].astype(jnp.float32)
    return parts


def product(left, right, count=3):
    a = jnp.concatenate([left[k] for k in LEFT[count]], axis=1)
    b = jnp.concatenate([right[k] for k in RIGHT[count]], axis=0)
    return jnp.dot(a, b, preferred_element_type=jnp.float32)


def columns_kernel(ids, pattern, y0, y1, inv00, u01, inv11, back0, back1, link, cols):
    for out, value in ((back0, inv00[...].T), (back1, inv11[...].T), (link, u01[...])):
        for number, part in enumerate(split(value)):
            out[number] = part
    q = ids[1]
    swap = ids[2] == 1
    inverse0, inverse1, down = (split(inv00[...]), split(inv11[...]), split(u01[...].T))
    for c in range(2):
        w = pattern[32 * c + q, 1].astype(jnp.float32)
        first = product(inverse0, split(jnp.where(swap, y1[c], y0[c])))
        left = jnp.where(swap, y0[c], y1[c]) - w * product(down, split(first))
        second = product(inverse1, split(left))
        for k, value in enumerate((first, second)):
            for number, part in enumerate(split(value, 2)):
                cols[c, number, k * BLK : (k + 1) * BLK, :] = part


def solve_columns(ids, pattern, y0, y1, inv00, u01, inv11):
    smem = pl.BlockSpec(memory_space=pltpu.SMEM)
    parts = jax.ShapeDtypeStruct((3, BLK, BLK), jnp.bfloat16)
    return pl.pallas_call(
        columns_kernel,
        out_shape=(parts, parts, parts, jax.ShapeDtypeStruct((2, 2, 2 * BLK, BLK), jnp.bfloat16)),
        in_specs=[smem, smem] + [VMEM] * 5,
        out_specs=[VMEM] * 4,
        compiler_params=pltpu.CompilerParams(vmem_limit_bytes=32 << 20),
        cost_estimate=pl.CostEstimate(flops=3_000_000_000, bytes_accessed=4 << 20, transcendentals=0),
        name="solve_columns",
    )(ids, pattern, y0, y1, inv00, u01, inv11)


def update_kernel(ids, pattern, local, g, back0, back1, link, cols, out):
    j = pl.program_id(0)
    p, q = (ids[0], ids[1])
    slots = [(ids[3] + 4 - m) % 4 for m in range(4)]
    raw = [jnp.concatenate([g[k, slot] for slot in slots], axis=0) for k in range(2)]
    first = product(split(raw[0]), back0)
    x0 = split(first)
    linked = product(x0, link)
    w = [pattern[(j + 4 * h) * 8 + p, 1].astype(jnp.float32) for h in range(2)]
    left = [raw[1][h * BLK : (h + 1) * BLK] - w[h] * linked[h * BLK : (h + 1) * BLK] for h in range(2)]
    second = product(split(jnp.concatenate(left, axis=0)), back1)
    x1 = split(second, 2)
    solved = [jnp.concatenate([x0[k], x1[k]], axis=1) for k in range(2)]
    for h in range(2):
        row_id = (j + 4 * h) * 8 + p
        rows = slice(h * BLK, (h + 1) * BLK)
        for c in range(2):
            col_id = 32 * c + q
            places = [pl.ds(2 * c + side, BLK, stride=4) for side in range(2)]
            halves = [slice(side * HALF, (side + 1) * HALF) for side in range(2)]
            panel = col_id < 2
            lower = row_id >= col_id
            changed = lower & ~panel & (pattern[row_id, col_id] != 0)

            @pl.when(panel)
            def _():
                r = lax.broadcasted_iota(jnp.int32, (BLK, BLK), 0)
                s = lax.broadcasted_iota(jnp.int32, (BLK, BLK), 1)
                kept = (row_id > col_id) | ((row_id == col_id) & (s <= r))
                value = jnp.where(kept, jnp.where(col_id == 0, first[rows], second[rows]), 0.0)
                for side in range(2):
                    out[h, 0, places[side], :] = value[:, halves[side]]

            @pl.when(~panel & ~lower)
            def _():
                for side in range(2):
                    out[h, 0, places[side], :] = jnp.zeros((BLK, HALF), jnp.float32)

            @pl.when(changed)
            def _():
                change = product([part[rows] for part in solved], cols[c], 2)
                for side in range(2):
                    out[h, 0, places[side], :] = local[h, 0, places[side], :] - change[:, halves[side]]

            @pl.when(lower & ~panel & ~changed)
            def _():
                for side in range(2):
                    out[h, 0, places[side], :] = local[h, 0, places[side], :]


def update(ids, pattern, local, g, back0, back1, link, cols):
    whole = lambda *shape: pl.BlockSpec(shape, lambda j, *_: (0,) * len(shape))
    block = pl.BlockSpec((2, 1, 4 * BLK, HALF), lambda j, *_: (0, j, 0, 0))
    return pl.pallas_call(
        update_kernel,
        out_shape=jax.ShapeDtypeStruct(local.shape, jnp.float32),
        grid_spec=pltpu.PrefetchScalarGridSpec(
            num_scalar_prefetch=2,
            grid=(4,),
            in_specs=[
                block,
                pl.BlockSpec((2, 4, HALF, BLK), lambda j, *_: (j, 0, 0, 0)),
                *[whole(3, BLK, BLK)] * 3,
                whole(2, 2, 2 * BLK, BLK),
            ],
            out_specs=block,
        ),
        compiler_params=pltpu.CompilerParams(vmem_limit_bytes=40 << 20),
        cost_estimate=pl.CostEstimate(flops=12_000_000_000, bytes_accessed=14 << 20, transcendentals=0),
        name="update",
    )(ids, pattern, local, g, back0, back1, link, cols)


def shifted(value, x=0, core=0, z=0, y=0, where=None):
    pairs = []
    for place in np.ndindex(NX, NCORE, NZ, NY):
        if where is None or where(*place):
            a, b, c, d = place
            to = ((a + x) % NX, (b + core) % NCORE, (c + z) % NZ, (d + y) % NY)
            pairs.append((int(DEVICE[place]), int(DEVICE[to])))
    return lax.ppermute(value, AXES, pairs)


def pick(index, choices):
    value = choices[0]
    for number, choice in enumerate(choices[1:], 1):
        value = jnp.where(index == number, choice, value)
    return value


def per_device(matrix, pattern):
    tie = lambda *arrays: lax.optimization_barrier(arrays)
    p = lax.axis_index("row")
    q = lax.axis_index("col")
    x, core, z, y = (p // NCORE, p % NCORE, q // NY, q % NY)
    local = matrix.reshape(2, 4, 4 * BLK, HALF)
    head = matrix[0, 0, :, :, 0, :].transpose(1, 0, 2)
    quarters = head.transpose(0, 2, 1).reshape(4, HALF, BLK)

    parts = []
    for m in range(4):
        pairs = [(32 * c + s, (s % 8) * 32 + 8 * (s // 8) + 4 * c + m) for c in range(2) for s in range(32)]
        parts.append(lax.ppermute(quarters[m], AXES, pairs))
    mine = parts[0] + parts[1] + parts[2] + parts[3]
    mine, own = tie(mine, head[0])

    roots = ((0, 0, 0, 0), (0, 0, 0, 1), (0, 1, 0, 1))
    root = (x == 0) & (z == 0) & ((core == 0) & (y == 0) | (y == 1))
    g = jnp.stack([mine] + [shifted(mine, y=k) for k in (1, 2, 3)])
    along = [shifted(own, z=k, where=lambda *a: a in roots) for k in (2, 6, 4)]
    pivot = jnp.where(root, own, 0.0) + along[0] + along[1] + along[2]
    g, pivot = tie(g, pivot)

    groups = [[NY * b + a for b in range(NZ)] for a in range(NY)]
    g = lax.all_gather(g, "col", axis=0, axis_index_groups=groups)
    carries = lambda a, b, c, d: a == 0 and (d == 1 or (b == 0 and d == 0))
    pivot = pivot + shifted(pivot, z=1, where=lambda a, b, c, d: carries(a, b, c, d) and c % 2 == 0)
    got = [pivot] + [shifted(pivot, y=k, where=carries) for k in (1, 2, 3)]
    a00, rest = tie(pick(y, got), pick((y + 3) % 4, got))
    got = [a00] + [shifted(a00, x=k, where=lambda a, b, *_: a == 0 and b == 0) for k in (1, 2, 3)]
    a00, rest = tie(pick(x, got), rest)
    a00 = jnp.where(core == 0, a00, shifted(a00, core=1, where=lambda a, b, *_: b == 0))
    rest = pick(x, [rest] + [shifted(rest, x=k, where=lambda a, *_: a == 0) for k in (1, 2, 3)])
    a00, head = tie(a00, head)

    cols = pick(x, [head] + [shifted(head, x=k, where=lambda a, *_: a == 0) for k in (1, 2, 3)])
    (inv00,) = on_blocks(first_kernel, 1, "factor_first", a00)
    inv00, rest = tie(inv00, rest)
    swapped = shifted(rest, core=1)
    a01 = jnp.where(core == 0, rest, swapped)
    a11 = jnp.where(core == 0, swapped, rest)
    u01, inv11 = on_blocks(second_kernel, 2, "factor_second", inv00, a01, a11)
    u01, inv11, cols = tie(u01, inv11, cols)
    other = shifted(cols, core=1)
    ids = jnp.stack([p, q, core, y]).astype(jnp.int32)
    solved = solve_columns(ids, pattern, cols, other, inv00, u01, inv11)
    solved, g = tie(solved, g)
    out = update(ids, pattern, local, g, *solved)
    return out.reshape(matrix.shape)


def solution(mesh):
    return jax.shard_map(
        per_device,
        mesh=mesh,
        in_specs=(P(None, "row", None, None, "col", None), P()),
        out_specs=P(None, "row", None, None, "col", None),
        check_vma=False,
    )
```

time: 197 us -> 166 us (0.84)
  waiting for transfers between devices: 98.1 us -> 83 us
  Pallas kernels: 45.9 us -> 38.3 us
  starting transfers between devices: 27.5 us -> 19.9 us
    ppermute x30 -> x22, waiting for transfers between devices: 87.3 us -> 72.2 us  [shifted(): return lax.ppermute(value, AXES, pairs)]
    pallas_call x1, Pallas kernels: 24.3 us -> 13.3 us  [update(): pl.pallas_call(update_kernel, out_shape=jax.ShapeDtypeStruct(local.shape,...]
    ppermute x30 -> x22, starting transfers between devices: 24.2 us -> 16.6 us  [shifted(): return lax.ppermute(value, AXES, pairs)]
    pallas_call x1 -> x3, Pallas kernels: 21.6 us -> 25 us  [the longest x2 21.3 us: on_blocks(): pl.pallas_call(kernel, out_shape=(shape,) * outs, in_specs=[VMEM] * len(b...]
  transfers between devices with their start and end apart: 35 -> 27, of which waited for: 8 -> 8; matrix products, arithmetic and copies ran while one was open for 1% -> 1% of each run, Pallas kernels for 11% -> 15%
where the time goes in v2:
time: 166 us; the launch traced here: 163 us
  waiting for transfers between devices  83 us (50%)
  Pallas kernels  38.3 us (23%)
  starting transfers between devices  19.9 us (12%)
  between operations  13.8 us (8%)
  local copies, waits for them, and re-layouts  6.36 us (4%)
    ppermute x22, waiting for transfers between devices, shifted(): return lax.ppermute(value, AXES, pairs)  72.2 us
    pallas_call x2, Pallas kernels, on_blocks(): pl.pallas_call(kernel, out_shape=(shape,) * outs, in_specs=[VMEM] * len(b...  21.3 us
    ppermute x22, starting transfers between devices, shifted(): return lax.ppermute(value, AXES, pairs)  16.6 us
    pallas_call x1, Pallas kernels, update(): pl.pallas_call(update_kernel, out_shape=jax.ShapeDtypeStruct(local.shape,...  13.3 us
    ppermute x4, waiting for transfers between devices, per_device(): parts.append(lax.ppermute(quarters[m], AXES, pairs))  10.7 us
    unnamed x7, local copies, waits for them, and re-layouts  4.41 us
    pallas_call x1, Pallas kernels, solve_columns(): pl.pallas_call(columns_kernel, out_shape=(parts, parts, parts, jax.ShapeD...  3.7 us
  transfers between devices with their start and end apart: 27, of which 8 were waited for; matrix products, arithmetic and copies ran while one was open for 1% of the time, Pallas kernels for 15%

profile of v2, /device:TPU:36, one launch (start us, length us, event | category | flops | bytes accessed | tf_op | source)
XLA Modules:
  0.0 162.8 jit_solution(15986019200617893142)
XLA Ops:
  6.5 1.4 slice.18
  7.9 0.5 copy.12
  8.5 0.7 collective-permute-start.1
  9.2 0.7 collective-permute-start.3
  9.8 0.7 collective-permute-start.2
  10.5 1.3 collective-permute-start
  11.9 0.0 collective-permute-done.2
  11.9 10.7 %collective-permute-done = f32[128,256]{1,0:T(8,128)S(1)} collective-permute-done((f32[128,256]{1,0:T(8,128)S(1)}, f32[128,256]{1,0:T(8,128)S(1)}, u32[]{:S(2)}, u32[]{:S(2)}) %collective-permute-start) | collective-permute-done | bytes 131104 | tf_op jit(solution)/shard_map/ppermute | solution.py:261
  22.7 0.7 collective-permute-start.6
  23.3 0.7 collective-permute-start.9
  24.0 0.7 collective-permute-start.8
  24.7 0.7 collective-permute-start.7
  25.4 1.1 collective-permute-start.5
  26.4 2.4 %collective-permute-done.6 = f32[128,256]{1,0:T(8,128)S(1)} collective-permute-done((f32[128,256]{1,0:T(8,128)S(1)}, f32[128,256]{1,0:T(8,128)S(1)}, u32[]{:S(2)}, u32[]{:S(2)}) %collective-permute-start.6) | collective-permute-done | bytes 131104 | tf_op jit(solution)/shard_map/ppermute | solution.py:239
  28.9 0.0 collective-permute-start.4
  28.9 4.2 %collective-permute-done.5 = f32[128,256]{1,0:T(8,128)S(1)} collective-permute-done((f32[128,256]{1,0:T(8,128)S(1)}, f32[128,256]{1,0:T(8,128)S(1)}, u32[]{:S(2)}, u32[]{:S(2)}) %collective-permute-start.5) | collective-permute-done | bytes 131104 | tf_op jit(solution)/shard_map/ppermute | solution.py:239
  33.1 2.0 %collective-permute-done.4 = f32[128,256]{1,0:T(8,128)S(1)} collective-permute-done((f32[128,256]{1,0:T(8,128)S(1)}, f32[128,256]{1,0:T(8,128)S(1)}, u32[]{:S(2)}, u32[]{:S(2)}) %collective-permute-start.4) | collective-permute-done | bytes 131104 | tf_op jit(solution)/shard_map/ppermute | solution.py:239
  35.0 0.8 pad_maximum_fusion
  35.9 0.0 collective-permute-done.9
  35.9 0.0 collective-permute-done.8
  35.9 0.0 collective-permute-done.7
  35.9 0.1 add_add_fusion
  36.0 0.0 all-gather.3.cloned.1.call-update
  36.0 0.7 collective-permute-start.10
  36.7 0.7 collective-permute-start.13
  37.4 0.7 collective-permute-start.12
  38.1 0.7 collective-permute-start.11
  38.8 0.0 collective-permute-done.13
  38.8 0.0 collective-permute-done.12
  38.8 0.1 select_select_fusion.3
  38.9 0.7 collective-permute-start.16
  39.6 1.3 collective-permute-start.15
  40.9 0.7 collective-permute-start.14
  41.6 0.0 collective-permute-done.16
  41.6 42.4 %collective-permute-done.15 = f32[256,256]{1,0:T(8,128)S(1)} collective-permute-done((f32[256,256]{1,0:T(8,128)S(1)}, f32[256,256]{1,0:T(8,128)S(1)}, u32[]{:S(2)}, u32[]{:S(2)}) %collective-permute-start.15) | collective-permute-done | bytes 262176 | tf_op jit(solution)/shard_map/ppermute | solution.py:239
  84.0 0.1 select_select_fusion.2
  84.1 1.3 collective-permute-start.17
  85.4 0.7 collective-permute-start.20
  86.1 1.3 collective-permute-start.19
  87.4 0.9 collective-permute-start.18
  88.3 0.0 collective-permute-done.17
  88.3 0.0 collective-permute-done.20
  88.3 7.5 %collective-permute-done.19 = f32[256,256]{1,0:T(8,128)S(1)} collective-permute-done((f32[256,256]{1,0:T(8,128)S(1)}, f32[256,256]{1,0:T(8,128)S(1)}, u32[]{:S(2)}, u32[]{:S(2)}) %collective-permute-start.19) | collective-permute-done | bytes 262176 | tf_op jit(solution)/shard_map/ppermute | solution.py:239
  95.9 0.0 collective-permute-done.18
  95.9 0.1 select_select_fusion.1
  95.9 10.2 %factor_first.1.inv00 = f32[256,256]{1,0:T(8,128)S(1)} custom-call(f32[256,256]{1,0:T(8,128)S(1)} %broadcast_select_fusion.2.a00), custom_call_target="tpu_custom_call" | custom-call | flops 12000000000 | bytes 1048576 | tf_op jit(solution)/shard_map/factor_first/pallas_call | solution.py:98
  106.1 0.1 collective-permute-start.21
  106.2 0.7 collective-permute-start.24
  106.9 1.3 collective-permute-start.23
  108.2 0.9 collective-permute-start.22
  109.2 0.0 collective-permute-done.21
  109.2 0.0 copy-start.2
  109.2 11.1 %factor_second.1 = (f32[256,256]{1,0:T(8,128)S(1)}, f32[256,256]{1,0:T(8,128)S(1)}) custom-call(f32[256,256]{1,0:T(8,128)S(1)} %factor_first.1.inv00, f32[256,256]{1,0:T(8,128)S(1)} %get-tuple-element.60.a01, f32[256,256]{1,0:T(8,128)S(1)} %get-tuple-element.59.a11), custom_call_target="tpu_custom_call" | custom-call | flops 12000000000 | bytes 1048576 | tf_op jit(solution)/shard_map/factor_second/pallas_call | solution.py:98
  120.3 11.8 %collective-permute-done.23 = f32[2,256,256]{2,1,0:T(8,128)S(1)} collective-permute-done((f32[2,256,256]{2,1,0:T(8,128)S(1)}, f32[2,256,256]{2,1,0:T(8,128)S(1)}, u32[]{:S(2)}, u32[]{:S(2)}) %collective-permute-start.23) | collective-permute-done | bytes 524320 | tf_op jit(solution)/shard_map/ppermute | solution.py:239
  132.2 0.1 select_select_fusion.y0
  132.3 0.4 collective-permute-start.25
  132.7 0.1 pad_add_fusion.ids
  132.7 1.8 %collective-permute-done.25.y1 = f32[2,256,256]{2,1,0:T(8,128)S(1)} collective-permute-done((f32[2,256,256]{2,1,0:T(8,128)S(1)}, f32[2,256,256]{2,1,0:T(8,128)S(1)}, u32[]{:S(2)}, u32[]{:S(2)}) %collective-permute-start.25) | collective-permute-done | bytes 524320 | tf_op jit(solution)/shard_map/ppermute | solution.py:239
  134.6 3.7 %solve_columns.1 = (bf16[3,256,256]{2,1,0:T(8,128)(2,1)S(1)}, bf16[3,256,256]{2,1,0:T(8,128)(2,1)S(1)}, bf16[3,256,256]{2,1,0:T(8,128)(2,1)S(1)}, bf16[2,2,512,256]{3,2,1,0:T(8,128)(2,1)S(1)}) custom-call(s32[4]{0:T(128)S(1)} %pad_add_fusion.ids, s32[64,64]{1,0:T(8,128)S(1)} %copy-done.2, f32[2,256,256]{2,1,0:T(8,128)S(1)} %select_select_fusion.y0, ...), custom_call_target="tpu_custom_call" | custom-call | flops 3000000000 | bytes 4194304 | tf_op jit(solution)/shard_map/solve_columns/pallas_call | solution.py:148
  138.3 0.0 all-gather.3.cloned.1.call-done
  138.3 0.0 copy-start
  138.3 2.2 %copy-done = f32[8,1,256,2,1,256]{5,4,3,2,1,0:T(1,128)S(1)} copy-done((f32[8,1,256,2,1,256]{5,4,3,2,1,0:T(1,128)S(1)}, f32[8,1,256,2,1,256]{5,4,3,2,1,0:T(1,128)}, u32[]{:S(2)}) %copy-start) | copy-done | bytes 4194328
  140.5 2.2 %copy-done.1 = f32[32,128,256]{2,1,0:T(8,128)S(1)} copy-done((f32[32,128,256]{2,1,0:T(8,128)S(1)}, f32[32,128,256]{2,1,0:T(8,128)}, u32[]{:S(2)}) %copy-start.1) | copy-done | bytes 4194328
  142.7 13.3 %update.1 = f32[2,4,1024,128]{3,2,1,0:T(8,128)} custom-call(s32[4]{0:T(128)S(1)} %pad_add_fusion.ids, s32[64,64]{1,0:T(8,128)S(1)} %copy-done.2, f32[2,4,1024,128]{3,2,1,0:T(8,128)S(1)} %bitcast.31, f32[8,4,128,256]{3,2,1,0:T(8,128)S(1)} %bitcast.32, bf16[3,256,256]{2,1,0:T(8,128)(2,1)S(1)} %get-tuple-element.53.back0, ...), custom_call_target="tpu_custom_call" | custom-call | flops 12000000000 | bytes 14680064 | tf_op jit(solution)/shard_map/update/pallas_call | solution.py:212
  (17 shorter events, 0.3 us)
Async XLA Ops:
  6.5 131.8 %all-gather.3.cloned.1.call-start = ((), (), s32[]{:S(2)}) async-start(), calls=%async_computation | async-start | bytes 4718592 | tf_op jit(solution)/shard_map/all_gather | solution.py:273
  8.5 3.4 %collective-permute-start.1 = (f32[128,256]{1,0:T(8,128)S(1)}, f32[128,256]{1,0:T(8,128)S(1)}, u32[]{:S(2)}, u32[]{:S(2)}) collective-permute-start(f32[128,256]{1,0:T(8,128)S(1)} %get-tuple-element.61), channel_id=1, source_target_pairs={{0,1},{1,33},{2,65},{3,97},{4,129},{5,161},{6,193},{7,225},{8,9},{... | collective-permute-start | bytes 393224 | tf_op jit(solution)/shard_map/ppermute | solution.py:261
  9.2 2.7 %collective-permute-start.3 = (f32[128,256]{1,0:T(8,128)S(1)}, f32[128,256]{1,0:T(8,128)S(1)}, u32[]{:S(2)}, u32[]{:S(2)}) collective-permute-start(f32[128,256]{1,0:T(8,128)S(1)} %get-tuple-element.62), channel_id=1, source_target_pairs={{0,3},{1,35},{2,67},{3,99},{4,131},{5,163},{6,195},{7,227},{8,11},... | collective-permute-start | bytes 393224 | tf_op jit(solution)/shard_map/ppermute | solution.py:261
  9.8 2.1 %collective-permute-start.2 = (f32[128,256]{1,0:T(8,128)S(1)}, f32[128,256]{1,0:T(8,128)S(1)}, u32[]{:S(2)}, u32[]{:S(2)}) collective-permute-start(f32[128,256]{1,0:T(8,128)S(1)} %get-tuple-element.63), channel_id=1, source_target_pairs={{0,2},{1,34},{2,66},{3,98},{4,130},{5,162},{6,194},{7,226},{8,10},... | collective-permute-start | bytes 393224 | tf_op jit(solution)/shard_map/ppermute | solution.py:261
  10.5 12.1 %collective-permute-start = (f32[128,256]{1,0:T(8,128)S(1)}, f32[128,256]{1,0:T(8,128)S(1)}, u32[]{:S(2)}, u32[]{:S(2)}) collective-permute-start(f32[128,256]{1,0:T(8,128)S(1)} %get-tuple-element.64), channel_id=1, source_target_pairs={{0,0},{1,32},{2,64},{3,96},{4,128},{5,160},{6,192},{7,224},{8,8},{... | collective-permute-start | bytes 393224 | tf_op jit(solution)/shard_map/ppermute | solution.py:261
  22.7 6.2 %collective-permute-start.6 = (f32[128,256]{1,0:T(8,128)S(1)}, f32[128,256]{1,0:T(8,128)S(1)}, u32[]{:S(2)}, u32[]{:S(2)}) collective-permute-start(f32[128,256]{1,0:T(8,128)S(1)} %add_add_fusion.1), channel_id=1, source_target_pairs={{0,3},{1,0},{2,1},{3,2},{4,7},{5,4},{6,5},{7,6},{8,11},{9,8},{10,9... | collective-permute-start | bytes 393224 | tf_op jit(solution)/shard_map/ppermute | solution.py:239
  23.3 12.5 %collective-permute-start.9 = (f32[256,256]{1,0:T(8,128)S(1)}, f32[256,256]{1,0:T(8,128)S(1)}, u32[]{:S(2)}, u32[]{:S(2)}) collective-permute-start(f32[256,256]{1,0:T(8,128)S(1)} %slice_bitcast_fusion), channel_id=1, source_target_pairs={{0,16},{1,17},{33,49}} | collective-permute-start | bytes 786440 | tf_op jit(solution)/shard_map/ppermute | solution.py:239
  24.0 11.9 %collective-permute-start.8 = (f32[256,256]{1,0:T(8,128)S(1)}, f32[256,256]{1,0:T(8,128)S(1)}, u32[]{:S(2)}, u32[]{:S(2)}) collective-permute-start(f32[256,256]{1,0:T(8,128)S(1)} %slice_bitcast_fusion), channel_id=1, source_target_pairs={{0,24},{1,25},{33,57}} | collective-permute-start | bytes 786440 | tf_op jit(solution)/shard_map/ppermute | solution.py:239
  24.7 11.2 %collective-permute-start.7 = (f32[256,256]{1,0:T(8,128)S(1)}, f32[256,256]{1,0:T(8,128)S(1)}, u32[]{:S(2)}, u32[]{:S(2)}) collective-permute-start(f32[256,256]{1,0:T(8,128)S(1)} %slice_bitcast_fusion), channel_id=1, source_target_pairs={{0,8},{1,9},{33,41}} | collective-permute-start | bytes 786440 | tf_op jit(solution)/shard_map/ppermute | solution.py:239
  25.4 7.7 %collective-permute-start.5 = (f32[128,256]{1,0:T(8,128)S(1)}, f32[128,256]{1,0:T(8,128)S(1)}, u32[]{:S(2)}, u32[]{:S(2)}) collective-permute-start(f32[128,256]{1,0:T(8,128)S(1)} %add_add_fusion.1), channel_id=1, source_target_pairs={{0,2},{1,3},{2,0},{3,1},{4,6},{5,7},{6,4},{7,5},{8,10},{9,11},{10,... | collective-permute-start | bytes 393224 | tf_op jit(solution)/shard_map/ppermute | solution.py:239
  28.9 6.2 %collective-permute-start.4 = (f32[128,256]{1,0:T(8,128)S(1)}, f32[128,256]{1,0:T(8,128)S(1)}, u32[]{:S(2)}, u32[]{:S(2)}) collective-permute-start(f32[128,256]{1,0:T(8,128)S(1)} %add_add_fusion.1), channel_id=1, source_target_pairs={{0,1},{1,2},{2,3},{3,0},{4,5},{5,6},{6,7},{7,4},{8,9},{9,10},{10,1... | collective-permute-start | bytes 393224 | tf_op jit(solution)/shard_map/ppermute | solution.py:239
  36.0 0.7 collective-permute-start.10
  36.7 2.1 %collective-permute-start.13 = (f32[256,256]{1,0:T(8,128)S(1)}, f32[256,256]{1,0:T(8,128)S(1)}, u32[]{:S(2)}, u32[]{:S(2)}) collective-permute-start(f32[256,256]{1,0:T(8,128)S(1)} %add.44), channel_id=1, source_target_pairs={{0,1},{1,2},{4,5},{5,6},{8,9},{9,10},{12,13},{13,14},{16,17},{17,1... | collective-permute-start | bytes 786440 | tf_op jit(solution)/shard_map/ppermute | solution.py:239
  37.4 1.4 collective-permute-start.12
  38.1 0.7 collective-permute-start.11
  38.9 2.7 %collective-permute-start.16 = (f32[256,256]{1,0:T(8,128)S(1)}, f32[256,256]{1,0:T(8,128)S(1)}, u32[]{:S(2)}, u32[]{:S(2)}) collective-permute-start(f32[256,256]{1,0:T(8,128)S(1)} %get-tuple-element.34), channel_id=1, source_target_pairs={{0,64},{1,65},{2,66},{3,67},{4,68},{5,69},{6,70},{7,71},{8,72},{9,... | collective-permute-start | bytes 786440 | tf_op jit(solution)/shard_map/ppermute | solution.py:239
  39.6 44.4 %collective-permute-start.15 = (f32[256,256]{1,0:T(8,128)S(1)}, f32[256,256]{1,0:T(8,128)S(1)}, u32[]{:S(2)}, u32[]{:S(2)}) collective-permute-start(f32[256,256]{1,0:T(8,128)S(1)} %get-tuple-element.34), channel_id=1, source_target_pairs={{0,128},{1,129},{2,130},{3,131},{4,132},{5,133},{6,134},{7,135},{8... | collective-permute-start | bytes 786440 | tf_op jit(solution)/shard_map/ppermute | solution.py:239
  40.9 43.1 %collective-permute-start.14 = (f32[256,256]{1,0:T(8,128)S(1)}, f32[256,256]{1,0:T(8,128)S(1)}, u32[]{:S(2)}, u32[]{:S(2)}) collective-permute-start(f32[256,256]{1,0:T(8,128)S(1)} %get-tuple-element.34), channel_id=1, source_target_pairs={{0,192},{1,193},{2,194},{3,195},{4,196},{5,197},{6,198},{7,199},{8... | collective-permute-start | bytes 786440 | tf_op jit(solution)/shard_map/ppermute | solution.py:239
  84.1 4.2 %collective-permute-start.17 = (f32[256,256]{1,0:T(8,128)S(1)}, f32[256,256]{1,0:T(8,128)S(1)}, u32[]{:S(2)}, u32[]{:S(2)}) collective-permute-start(f32[256,256]{1,0:T(8,128)S(1)} %select_select_fusion.2), channel_id=1, source_target_pairs={{0,32},{1,33},{2,34},{3,35},{4,36},{5,37},{6,38},{7,39},{8,40},{9,... | collective-permute-start | bytes 786440 | tf_op jit(solution)/shard_map/ppermute | solution.py:239
  85.4 2.9 %collective-permute-start.20 = (f32[256,256]{1,0:T(8,128)S(1)}, f32[256,256]{1,0:T(8,128)S(1)}, u32[]{:S(2)}, u32[]{:S(2)}) collective-permute-start(f32[256,256]{1,0:T(8,128)S(1)} %get-tuple-element.38), channel_id=1, source_target_pairs={{0,64},{1,65},{2,66},{3,67},{4,68},{5,69},{6,70},{7,71},{8,72},{9,... | collective-permute-start | bytes 786440 | tf_op jit(solution)/shard_map/ppermute | solution.py:239
  86.1 9.8 %collective-permute-start.19 = (f32[256,256]{1,0:T(8,128)S(1)}, f32[256,256]{1,0:T(8,128)S(1)}, u32[]{:S(2)}, u32[]{:S(2)}) collective-permute-start(f32[256,256]{1,0:T(8,128)S(1)} %get-tuple-element.38), channel_id=1, source_target_pairs={{0,128},{1,129},{2,130},{3,131},{4,132},{5,133},{6,134},{7,135},{8... | collective-permute-start | bytes 786440 | tf_op jit(solution)/shard_map/ppermute | solution.py:239
  87.4 8.5 %collective-permute-start.18 = (f32[256,256]{1,0:T(8,128)S(1)}, f32[256,256]{1,0:T(8,128)S(1)}, u32[]{:S(2)}, u32[]{:S(2)}) collective-permute-start(f32[256,256]{1,0:T(8,128)S(1)} %get-tuple-element.38), channel_id=1, source_target_pairs={{0,192},{1,193},{2,194},{3,195},{4,196},{5,197},{6,198},{7,199},{8... | collective-permute-start | bytes 786440 | tf_op jit(solution)/shard_map/ppermute | solution.py:239
  106.1 3.0 %collective-permute-start.21 = (f32[256,256]{1,0:T(8,128)S(1)}, f32[256,256]{1,0:T(8,128)S(1)}, u32[]{:S(2)}, u32[]{:S(2)}) collective-permute-start(f32[256,256]{1,0:T(8,128)S(1)} %select_select_fusion.1), channel_id=1, source_target_pairs={{0,32},{1,33},{2,34},{3,35},{4,36},{5,37},{6,38},{7,39},{8,40},{9,... | collective-permute-start | bytes 786440 | tf_op jit(solution)/shard_map/ppermute | solution.py:239
  106.2 14.1 %collective-permute-start.24 = (f32[2,256,256]{2,1,0:T(8,128)S(1)}, f32[2,256,256]{2,1,0:T(8,128)S(1)}, u32[]{:S(2)}, u32[]{:S(2)}) collective-permute-start(f32[2,256,256]{2,1,0:T(8,128)S(1)} %bitcast.34), channel_id=1, source_target_pairs={{0,64},{1,65},{2,66},{3,67},{4,68},{5,69},{6,70},{7,71},{8,72},{9,... | collective-permute-start | bytes 1572872 | tf_op jit(solution)/shard_map/ppermute | solution.py:239
  106.9 25.2 %collective-permute-start.23 = (f32[2,256,256]{2,1,0:T(8,128)S(1)}, f32[2,256,256]{2,1,0:T(8,128)S(1)}, u32[]{:S(2)}, u32[]{:S(2)}) collective-permute-start(f32[2,256,256]{2,1,0:T(8,128)S(1)} %bitcast.35), channel_id=1, source_target_pairs={{0,128},{1,129},{2,130},{3,131},{4,132},{5,133},{6,134},{7,135},{8... | collective-permute-start | bytes 1572872 | tf_op jit(solution)/shard_map/ppermute | solution.py:239
  108.2 23.9 %collective-permute-start.22 = (f32[2,256,256]{2,1,0:T(8,128)S(1)}, f32[2,256,256]{2,1,0:T(8,128)S(1)}, u32[]{:S(2)}, u32[]{:S(2)}) collective-permute-start(f32[2,256,256]{2,1,0:T(8,128)S(1)} %bitcast.36), channel_id=1, source_target_pairs={{0,192},{1,193},{2,194},{3,195},{4,196},{5,197},{6,198},{7,199},{8... | collective-permute-start | bytes 1572872 | tf_op jit(solution)/shard_map/ppermute | solution.py:239
  109.2 25.4 %copy-start.2 = (s32[64,64]{1,0:T(8,128)S(1)}, s32[64,64]{1,0:T(8,128)}, u32[]{:S(2)}) copy-start(s32[64,64]{1,0:T(8,128)} %pattern.3) | copy-start | bytes 49156
  132.3 2.3 %collective-permute-start.25 = (f32[2,256,256]{2,1,0:T(8,128)S(1)}, f32[2,256,256]{2,1,0:T(8,128)S(1)}, u32[]{:S(2)}, u32[]{:S(2)}) collective-permute-start(f32[2,256,256]{2,1,0:T(8,128)S(1)} %select_select_fusion.y0), channel_id=1, source_target_pairs={{0,32},{1,33},{2,34},{3,35},{4,36},{5,37},{6,38},{7,39},{8,40},{9,... | collective-permute-start | bytes 1572872 | tf_op jit(solution)/shard_map/ppermute | solution.py:239
  138.3 2.2 %copy-start = (f32[8,1,256,2,1,256]{5,4,3,2,1,0:T(1,128)S(1)}, f32[8,1,256,2,1,256]{5,4,3,2,1,0:T(1,128)}, u32[]{:S(2)}) copy-start(f32[8,1,256,2,1,256]{5,4,3,2,1,0:T(1,128)} %param.2) | copy-start | bytes 12582916
  140.5 2.2 %copy-start.1 = (f32[32,128,256]{2,1,0:T(8,128)S(1)}, f32[32,128,256]{2,1,0:T(8,128)}, u32[]{:S(2)}) copy-start(f32[32,128,256]{2,1,0:T(8,128)} %all-gather.3.cloned.1.call-done) | copy-start | bytes 12582916
Sparse Core Ops, SparseCore 0:
  36.1 57.9 all-gather.2

commit v3 on v2

--- a/solution.py
+++ b/solution.py
@@ -83,27 +83,24 @@
     out[h:, h:] = low
 
 
-def first_kernel(a00, inv00):
+def pivots_kernel(a00, a01, a11, inv00, u01, inv11):
     invert_pair(a00[...], inv00)
-
-
-def second_kernel(inv00, a01, a11, u01, inv11):
     link = dot(inv00[...], a01[...])
     u01[...] = link
     invert_pair(a11[...] - dot(link, link, ((0,), (0,))), inv11)
 
 
-def on_blocks(kernel, outs, name, *blocks):
+def factor_pivots(a00, a01, a11):
     shape = jax.ShapeDtypeStruct((BLK, BLK), jnp.float32)
     return pl.pallas_call(
-        kernel,
-        out_shape=(shape,) * outs,
-        in_specs=[VMEM] * len(blocks),
-        out_specs=[VMEM] * outs,
+        pivots_kernel,
+        out_shape=(shape, shape, shape),
+        in_specs=[VMEM] * 3,
+        out_specs=[VMEM] * 3,
         compiler_params=pltpu.CompilerParams(vmem_limit_bytes=32 << 20),
-        cost_estimate=pl.CostEstimate(flops=12_000_000_000, bytes_accessed=1 << 20, transcendentals=0),
-        name=name,
-    )(*blocks)
+        cost_estimate=pl.CostEstimate(flops=25_000_000_000, bytes_accessed=1 << 20, transcendentals=0),
+        name="factor_pivots",
+    )(a00, a01, a11)
 
 
 LEFT = {3: (0, 0, 1, 0, 1, 2), 2: (0, 1, 0)}
@@ -223,7 +220,7 @@
             ],
             out_specs=block,
         ),
-        compiler_params=pltpu.CompilerParams(vmem_limit_bytes=40 << 20),
+        compiler_params=pltpu.CompilerParams(vmem_limit_bytes=60 << 20),
         cost_estimate=pl.CostEstimate(flops=12_000_000_000, bytes_accessed=14 << 20, transcendentals=0),
         name="update",
     )(ids, pattern, local, g, back0, back1, link, cols)
@@ -255,40 +252,39 @@
     head = matrix[0, 0, :, :, 0, :].transpose(1, 0, 2)
     quarters = head.transpose(0, 2, 1).reshape(4, HALF, BLK)
 
+    own = head[0]
+    starts = lambda b, d: d == 1 or (b == 0 and d == 0)
+    carrier = (y == 1) | ((core == 0) & (y == 0))
+    along = [shifted(own, x=k, where=lambda a, b, c, d: a == 0 and c == 0 and starts(b, d)) for k in (1, 3, 2)]
     parts = []
     for m in range(4):
         pairs = [(32 * c + s, (s % 8) * 32 + 8 * (s // 8) + 4 * c + m) for c in range(2) for s in range(32)]
         parts.append(lax.ppermute(quarters[m], AXES, pairs))
+    pivot = jnp.where((x == 0) & (z == 0) & carrier, own, 0.0) + along[0] + along[1] + along[2]
+    along = [shifted(pivot, z=k, where=lambda a, b, c, d: c == 0 and starts(b, d)) for k in (2, 6, 4)]
+    pivot = pivot + along[0] + along[1] + along[2]
     mine = parts[0] + parts[1] + parts[2] + parts[3]
-    mine, own = tie(mine, head[0])
-
-    roots = ((0, 0, 0, 0), (0, 0, 0, 1), (0, 1, 0, 1))
-    root = (x == 0) & (z == 0) & ((core == 0) & (y == 0) | (y == 1))
+    mine, pivot = tie(mine, pivot)
+
     g = jnp.stack([mine] + [shifted(mine, y=k) for k in (1, 2, 3)])
-    along = [shifted(own, z=k, where=lambda *a: a in roots) for k in (2, 6, 4)]
-    pivot = jnp.where(root, own, 0.0) + along[0] + along[1] + along[2]
+    pivot = pivot + shifted(pivot, z=1, where=lambda a, b, c, d: c % 2 == 0 and starts(b, d))
     g, pivot = tie(g, pivot)
 
     groups = [[NY * b + a for b in range(NZ)] for a in range(NY)]
     g = lax.all_gather(g, "col", axis=0, axis_index_groups=groups)
-    carries = lambda a, b, c, d: a == 0 and (d == 1 or (b == 0 and d == 0))
-    pivot = pivot + shifted(pivot, z=1, where=lambda a, b, c, d: carries(a, b, c, d) and c % 2 == 0)
-    got = [pivot] + [shifted(pivot, y=k, where=carries) for k in (1, 2, 3)]
-    a00, rest = tie(pick(y, got), pick((y + 3) % 4, got))
-    got = [a00] + [shifted(a00, x=k, where=lambda a, b, *_: a == 0 and b == 0) for k in (1, 2, 3)]
-    a00, rest = tie(pick(x, got), rest)
-    a00 = jnp.where(core == 0, a00, shifted(a00, core=1, where=lambda a, b, *_: b == 0))
-    rest = pick(x, [rest] + [shifted(rest, x=k, where=lambda a, *_: a == 0) for k in (1, 2, 3)])
-    a00, head = tie(a00, head)
-
-    cols = pick(x, [head] + [shifted(head, x=k, where=lambda a, *_: a == 0) for k in (1, 2, 3)])
-    (inv00,) = on_blocks(first_kernel, 1, "factor_first", a00)
-    inv00, rest = tie(inv00, rest)
+    got = [pivot] + [shifted(pivot, y=k, where=lambda a, b, c, d: starts(b, d)) for k in (1, 2, 3)]
+    first = pick(y, got)
+    rest = pick((y + 3) % 4, got)
     swapped = shifted(rest, core=1)
+    a00 = jnp.where(core == 0, first, shifted(first, core=1, where=lambda a, b, *_: b == 0))
     a01 = jnp.where(core == 0, rest, swapped)
     a11 = jnp.where(core == 0, swapped, rest)
-    u01, inv11 = on_blocks(second_kernel, 2, "factor_second", inv00, a01, a11)
-    u01, inv11, cols = tie(u01, inv11, cols)
+    a00, a01, a11, head = tie(a00, a01, a11, head)
+
+    cols = [head] + [shifted(head, x=k, where=lambda a, *_: a == 0) for k in (1, 2, 3)]
+    inv00, u01, inv11 = factor_pivots(a00, a01, a11)
+    inv00, u01, inv11, cols[0] = tie(inv00, u01, inv11, cols[0])
+    cols = pick(x, cols)
     other = shifted(cols, core=1)
     ids = jnp.stack([p, q, core, y]).astype(jnp.int32)
     solved = solve_columns(ids, pattern, cols, other, inv00, u01, inv11)

time: 166 us -> 135 us (0.81)
  the two profiles are of different devices: /device:TPU:36 before, /device:TPU:65 now
where the time goes in v3:
time: 135 us; the launch traced here: 134 us
  starting transfers between devices  54.4 us (40%)
  Pallas kernels  42.3 us (31%)
  waiting for transfers between devices  17 us (13%)
  between operations  13.9 us (10%)
  local copies, waits for them, and re-layouts  5.3 us (4%)
  other arithmetic  1.4 us (1%)
    ppermute x19, starting transfers between devices, shifted(): return lax.ppermute(value, AXES, pairs)  40.1 us
    pallas_call x1, Pallas kernels, factor_pivots(): pl.pallas_call(pivots_kernel, out_shape=(shape, shape, shape), in_specs=[...  21.6 us
    pallas_call x1, Pallas kernels, update(): pl.pallas_call(update_kernel, out_shape=jax.ShapeDtypeStruct(local.shape,...  17 us
    ppermute x19, waiting for transfers between devices, shifted(): return lax.ppermute(value, AXES, pairs)  14.8 us
    ppermute x4, starting transfers between devices, per_device(): parts.append(lax.ppermute(quarters[m], AXES, pairs))  14.3 us
    pallas_call x1, Pallas kernels, solve_columns(): pl.pallas_call(columns_kernel, out_shape=(parts, parts, parts, jax.ShapeD...  3.7 us
    unnamed x13, local copies, waits for them, and re-layouts  3.35 us
  transfers between devices with their start and end apart: 24, of which 8 were waited for; matrix products, arithmetic and copies ran while one was open for 1% of the time, Pallas kernels for 19%

profile of v3, /device:TPU:65, one launch (start us, length us, event | category | flops | bytes accessed | tf_op | source)
XLA Modules:
  0.0 134.3 jit_solution(16122298121496182874)
XLA Ops:
  6.5 1.4 %slice.18 = f32[1,1,256,2,1,256]{5,4,3,2,1,0:T(1,128)S(1)} slice(f32[8,1,256,2,1,256]{5,4,3,2,1,0:T(1,128)} %param.2), slice={[0:1], [0:1], [0:256], [0:2], [0:1], [0:256]} | slice | bytes 1048576 | tf_op jit(solution)/shard_map/slice | solution.py:252
  8.0 0.7 collective-permute-start.5
  8.7 0.7 collective-permute-start.4
  9.4 0.7 collective-permute-start.6
  10.1 0.5 copy.12
  10.6 5.1 %collective-permute-start.1 = (f32[128,256]{1,0:T(8,128)S(1)}, f32[128,256]{1,0:T(8,128)S(1)}, u32[]{:S(2)}, u32[]{:S(2)}) collective-permute-start(f32[128,256]{1,0:T(8,128)S(1)} %get-tuple-element.57), channel_id=1, source_target_pairs={{0,1},{1,33},{2,65},{3,97},{4,129},{5,161},{6,193},{7,225},{8,9},{... | collective-permute-start | bytes 393224 | tf_op jit(solution)/shard_map/ppermute | solution.py:262
  15.7 5.8 %collective-permute-start.3 = (f32[128,256]{1,0:T(8,128)S(1)}, f32[128,256]{1,0:T(8,128)S(1)}, u32[]{:S(2)}, u32[]{:S(2)}) collective-permute-start(f32[128,256]{1,0:T(8,128)S(1)} %get-tuple-element.58), channel_id=1, source_target_pairs={{0,3},{1,35},{2,67},{3,99},{4,131},{5,163},{6,195},{7,227},{8,11},... | collective-permute-start | bytes 393224 | tf_op jit(solution)/shard_map/ppermute | solution.py:262
  21.6 0.0 collective-permute-done.5
  21.6 1.5 %collective-permute-start.2 = (f32[128,256]{1,0:T(8,128)S(1)}, f32[128,256]{1,0:T(8,128)S(1)}, u32[]{:S(2)}, u32[]{:S(2)}) collective-permute-start(f32[128,256]{1,0:T(8,128)S(1)} %get-tuple-element.59), channel_id=1, source_target_pairs={{0,2},{1,34},{2,66},{3,98},{4,130},{5,162},{6,194},{7,226},{8,10},... | collective-permute-start | bytes 393224 | tf_op jit(solution)/shard_map/ppermute | solution.py:262
  23.1 0.0 collective-permute-done.4
  23.1 1.9 %collective-permute-start = (f32[128,256]{1,0:T(8,128)S(1)}, f32[128,256]{1,0:T(8,128)S(1)}, u32[]{:S(2)}, u32[]{:S(2)}) collective-permute-start(f32[128,256]{1,0:T(8,128)S(1)} %get-tuple-element.60), channel_id=1, source_target_pairs={{0,0},{1,32},{2,64},{3,96},{4,128},{5,160},{6,192},{7,224},{8,8},{... | collective-permute-start | bytes 393224 | tf_op jit(solution)/shard_map/ppermute | solution.py:262
  25.0 0.0 collective-permute-done.6
  25.0 0.1 add_add_fusion.1
  25.1 0.7 collective-permute-start.9
  25.8 0.0 collective-permute-done.1
  25.8 0.7 collective-permute-start.8
  26.5 0.0 collective-permute-done.3
  26.5 0.7 collective-permute-start.7
  27.2 0.0 collective-permute-done.2
  27.2 2.2 %collective-permute-done = f32[128,256]{1,0:T(8,128)S(1)} collective-permute-done((f32[128,256]{1,0:T(8,128)S(1)}, f32[128,256]{1,0:T(8,128)S(1)}, u32[]{:S(2)}, u32[]{:S(2)}) %collective-permute-start) | collective-permute-done | bytes 131104 | tf_op jit(solution)/shard_map/ppermute | solution.py:262
  29.4 0.0 collective-permute-done.9
  29.4 0.0 collective-permute-done.8
  29.4 0.0 collective-permute-done.7
  29.4 0.1 add_add_fusion
  29.5 0.7 collective-permute-start.13
  30.2 0.1 collective-permute-start.12
  30.3 14.4 %collective-permute-start.11 = (f32[128,256]{1,0:T(8,128)S(1)}, f32[128,256]{1,0:T(8,128)S(1)}, u32[]{:S(2)}, u32[]{:S(2)}) collective-permute-start(f32[128,256]{1,0:T(8,128)S(1)} %add_add_fusion.2), channel_id=1, source_target_pairs={{0,2},{1,3},{2,0},{3,1},{4,6},{5,7},{6,4},{7,5},{8,10},{9,11},{10,... | collective-permute-start | bytes 393224 | tf_op jit(solution)/shard_map/ppermute | solution.py:236
  44.7 0.0 collective-permute-start.10
  44.7 0.6 collective-permute-done.12
  45.3 1.8 %collective-permute-done.11 = f32[128,256]{1,0:T(8,128)S(1)} collective-permute-done((f32[128,256]{1,0:T(8,128)S(1)}, f32[128,256]{1,0:T(8,128)S(1)}, u32[]{:S(2)}, u32[]{:S(2)}) %collective-permute-start.11) | collective-permute-done | bytes 131104 | tf_op jit(solution)/shard_map/ppermute | solution.py:236
  47.1 2.7 %collective-permute-done.10 = f32[128,256]{1,0:T(8,128)S(1)} collective-permute-done((f32[128,256]{1,0:T(8,128)S(1)}, f32[128,256]{1,0:T(8,128)S(1)}, u32[]{:S(2)}, u32[]{:S(2)}) %collective-permute-start.10) | collective-permute-done | bytes 131104 | tf_op jit(solution)/shard_map/ppermute | solution.py:236
  49.7 0.8 pad_maximum_fusion
  50.6 0.0 collective-permute-done.13
  50.6 0.0 all-gather.3.cloned.1.call-update
  50.6 0.7 collective-permute-start.16
  51.3 0.7 collective-permute-start.15
  52.0 1.3 collective-permute-start.14
  53.3 0.0 collective-permute-done.16
  53.3 0.0 collective-permute-done.15
  53.4 7.0 %collective-permute-done.14 = f32[256,256]{1,0:T(8,128)S(1)} collective-permute-done((f32[256,256]{1,0:T(8,128)S(1)}, f32[256,256]{1,0:T(8,128)S(1)}, u32[]{:S(2)}, u32[]{:S(2)}) %collective-permute-start.14) | collective-permute-done | bytes 262176 | tf_op jit(solution)/shard_map/ppermute | solution.py:236
  60.4 0.1 select_select_fusion.1
  60.5 1.3 collective-permute-start.17
  61.8 9.0 %collective-permute-start.18 = (f32[256,256]{1,0:T(8,128)S(1)}, f32[256,256]{1,0:T(8,128)S(1)}, u32[]{:S(2)}, u32[]{:S(2)}) collective-permute-start(f32[256,256]{1,0:T(8,128)S(1)} %get-tuple-element.53), channel_id=1, source_target_pairs={{0,32},{1,33},{2,34},{3,35},{4,36},{5,37},{6,38},{7,39},{8,40},{9,... | collective-permute-start | bytes 786440 | tf_op jit(solution)/shard_map/ppermute | solution.py:236
  70.8 0.9 collective-permute-done.17
  71.7 0.3 collective-permute-done.18
  72.1 0.0 copy-start.1
  72.1 1.3 collective-permute-start.21
  73.5 4.5 %collective-permute-start.20 = (f32[2,256,256]{2,1,0:T(8,128)S(1)}, f32[2,256,256]{2,1,0:T(8,128)S(1)}, u32[]{:S(2)}, u32[]{:S(2)}) collective-permute-start(f32[2,256,256]{2,1,0:T(8,128)S(1)} %bitcast.36), channel_id=1, source_target_pairs={{0,128},{1,129},{2,130},{3,131},{4,132},{5,133},{6,134},{7,135},{8... | collective-permute-start | bytes 1572872 | tf_op jit(solution)/shard_map/ppermute | solution.py:236
  77.9 1.5 %collective-permute-start.19 = (f32[2,256,256]{2,1,0:T(8,128)S(1)}, f32[2,256,256]{2,1,0:T(8,128)S(1)}, u32[]{:S(2)}, u32[]{:S(2)}) collective-permute-start(f32[2,256,256]{2,1,0:T(8,128)S(1)} %bitcast.37), channel_id=1, source_target_pairs={{0,192},{1,193},{2,194},{3,195},{4,196},{5,197},{6,198},{7,199},{8... | collective-permute-start | bytes 1572872 | tf_op jit(solution)/shard_map/ppermute | solution.py:236
  79.4 21.6 %factor_pivots.1 = (f32[256,256]{1,0:T(8,128)S(1)}, f32[256,256]{1,0:T(8,128)S(1)}, f32[256,256]{1,0:T(8,128)S(1)}) custom-call(f32[256,256]{1,0:T(8,128)S(1)} %broadcast_select_fusion.2.a00, f32[256,256]{1,0:T(8,128)S(1)} %get-tuple-element.34.a01, f32[256,256]{1,0:T(8,128)S(1)} %get-tuple-element.35.a11), custom_call_target="tpu_custom_call" | custom-call | flops 24999999488 | bytes 1048576 | tf_op jit(solution)/shard_map/factor_pivots/pallas_call | solution.py:95
  101.1 0.0 collective-permute-done.21
  101.1 0.0 collective-permute-done.20
  101.1 0.0 collective-permute-done.19
  101.1 0.1 select_select_fusion.y0
  101.2 0.6 collective-permute-start.22
  101.9 0.1 pad_add_fusion.ids
  101.9 1.5 %collective-permute-done.22.y1 = f32[2,256,256]{2,1,0:T(8,128)S(1)} collective-permute-done((f32[2,256,256]{2,1,0:T(8,128)S(1)}, f32[2,256,256]{2,1,0:T(8,128)S(1)}, u32[]{:S(2)}, u32[]{:S(2)}) %collective-permute-start.22) | collective-permute-done | bytes 524320 | tf_op jit(solution)/shard_map/ppermute | solution.py:236
  103.4 3.7 %solve_columns.1 = (bf16[3,256,256]{2,1,0:T(8,128)(2,1)S(1)}, bf16[3,256,256]{2,1,0:T(8,128)(2,1)S(1)}, bf16[3,256,256]{2,1,0:T(8,128)(2,1)S(1)}, bf16[2,2,512,256]{3,2,1,0:T(8,128)(2,1)S(1)}) custom-call(s32[4]{0:T(128)S(1)} %pad_add_fusion.ids, s32[64,64]{1,0:T(8,128)S(1)} %copy-done.1, f32[2,256,256]{2,1,0:T(8,128)S(1)} %select_select_fusion.y0, ...), custom_call_target="tpu_custom_call" | custom-call | flops 3000000000 | bytes 4194304 | tf_op jit(solution)/shard_map/solve_columns/pallas_call | solution.py:145
  107.1 0.0 copy-done
  107.1 1.0 copy-done.2
  108.1 0.8 copy-done.3
  108.9 0.8 copy-done.4
  109.7 0.8 copy-done.5
  110.4 17.0 %update.1 = f32[2,4,1024,128]{3,2,1,0:T(8,128)} custom-call(s32[4]{0:T(128)} %copy-done, s32[64,64]{1,0:T(8,128)} %pattern.3, f32[2,4,1024,128]{3,2,1,0:T(8,128)} %bitcast.44, f32[8,4,128,256]{3,2,1,0:T(8,128)} %bitcast.45, bf16[3,256,256]{2,1,0:T(8,128)(2,1)} %copy-done.3, bf16[3,256,256]{2,1,0:T(8,128)(2,1)} %copy-done.4, bf16[3,256,256]{2,1,0:T(8,128)(2,1)} %copy-done.5, ...), custom_call_target="tpu_custom_call" | custom-call | flops 12000000000 | bytes 14680064 | tf_op jit(solution)/shard_map/update/pallas_call | solution.py:209
  (15 shorter events, 0.2 us)
Async XLA Ops:
  6.5 103.9 %all-gather.3.cloned.1.call-start = ((), (), s32[]{:S(2)}) async-start(), calls=%async_computation | async-start | bytes 4718592 | tf_op jit(solution)/shard_map/all_gather | solution.py:274
  8.0 13.6 %collective-permute-start.5 = (f32[256,256]{1,0:T(8,128)S(1)}, f32[256,256]{1,0:T(8,128)S(1)}, u32[]{:S(2)}, u32[]{:S(2)}) collective-permute-start(f32[256,256]{1,0:T(8,128)S(1)} %slice_bitcast_fusion), channel_id=1, source_target_pairs={{0,192},{1,193},{33,225}} | collective-permute-start | bytes 786440 | tf_op jit(solution)/shard_map/ppermute | solution.py:236
  8.7 14.4 %collective-permute-start.4 = (f32[256,256]{1,0:T(8,128)S(1)}, f32[256,256]{1,0:T(8,128)S(1)}, u32[]{:S(2)}, u32[]{:S(2)}) collective-permute-start(f32[256,256]{1,0:T(8,128)S(1)} %slice_bitcast_fusion), channel_id=1, source_target_pairs={{0,64},{1,65},{33,97}} | collective-permute-start | bytes 786440 | tf_op jit(solution)/shard_map/ppermute | solution.py:236
  9.4 15.6 %collective-permute-start.6 = (f32[256,256]{1,0:T(8,128)S(1)}, f32[256,256]{1,0:T(8,128)S(1)}, u32[]{:S(2)}, u32[]{:S(2)}) collective-permute-start(f32[256,256]{1,0:T(8,128)S(1)} %slice_bitcast_fusion), channel_id=1, source_target_pairs={{0,128},{1,129},{33,161}} | collective-permute-start | bytes 786440 | tf_op jit(solution)/shard_map/ppermute | solution.py:236
  10.6 15.2 %collective-permute-start.1 = (f32[128,256]{1,0:T(8,128)S(1)}, f32[128,256]{1,0:T(8,128)S(1)}, u32[]{:S(2)}, u32[]{:S(2)}) collective-permute-start(f32[128,256]{1,0:T(8,128)S(1)} %get-tuple-element.57), channel_id=1, source_target_pairs={{0,1},{1,33},{2,65},{3,97},{4,129},{5,161},{6,193},{7,225},{8,9},{... | collective-permute-start | bytes 393224 | tf_op jit(solution)/shard_map/ppermute | solution.py:262
  15.7 10.7 %collective-permute-start.3 = (f32[128,256]{1,0:T(8,128)S(1)}, f32[128,256]{1,0:T(8,128)S(1)}, u32[]{:S(2)}, u32[]{:S(2)}) collective-permute-start(f32[128,256]{1,0:T(8,128)S(1)} %get-tuple-element.58), channel_id=1, source_target_pairs={{0,3},{1,35},{2,67},{3,99},{4,131},{5,163},{6,195},{7,227},{8,11},... | collective-permute-start | bytes 393224 | tf_op jit(solution)/shard_map/ppermute | solution.py:262
  21.6 5.6 %collective-permute-start.2 = (f32[128,256]{1,0:T(8,128)S(1)}, f32[128,256]{1,0:T(8,128)S(1)}, u32[]{:S(2)}, u32[]{:S(2)}) collective-permute-start(f32[128,256]{1,0:T(8,128)S(1)} %get-tuple-element.59), channel_id=1, source_target_pairs={{0,2},{1,34},{2,66},{3,98},{4,130},{5,162},{6,194},{7,226},{8,10},... | collective-permute-start | bytes 393224 | tf_op jit(solution)/shard_map/ppermute | solution.py:262
  23.1 6.3 %collective-permute-start = (f32[128,256]{1,0:T(8,128)S(1)}, f32[128,256]{1,0:T(8,128)S(1)}, u32[]{:S(2)}, u32[]{:S(2)}) collective-permute-start(f32[128,256]{1,0:T(8,128)S(1)} %get-tuple-element.60), channel_id=1, source_target_pairs={{0,0},{1,32},{2,64},{3,96},{4,128},{5,160},{6,192},{7,224},{8,8},{... | collective-permute-start | bytes 393224 | tf_op jit(solution)/shard_map/ppermute | solution.py:262
  25.1 4.3 %collective-permute-start.9 = (f32[256,256]{1,0:T(8,128)S(1)}, f32[256,256]{1,0:T(8,128)S(1)}, u32[]{:S(2)}, u32[]{:S(2)}) collective-permute-start(f32[256,256]{1,0:T(8,128)S(1)} %add_add_fusion.1), channel_id=1, source_target_pairs={{0,16},{1,17},{33,49},{64,80},{65,81},{97,113},{128,144},{129,145}... | collective-permute-start | bytes 786440 | tf_op jit(solution)/shard_map/ppermute | solution.py:236
  25.8 3.6 %collective-permute-start.8 = (f32[256,256]{1,0:T(8,128)S(1)}, f32[256,256]{1,0:T(8,128)S(1)}, u32[]{:S(2)}, u32[]{:S(2)}) collective-permute-start(f32[256,256]{1,0:T(8,128)S(1)} %add_add_fusion.1), channel_id=1, source_target_pairs={{0,24},{1,25},{33,57},{64,88},{65,89},{97,121},{128,152},{129,153}... | collective-permute-start | bytes 786440 | tf_op jit(solution)/shard_map/ppermute | solution.py:236
  26.5 2.9 %collective-permute-start.7 = (f32[256,256]{1,0:T(8,128)S(1)}, f32[256,256]{1,0:T(8,128)S(1)}, u32[]{:S(2)}, u32[]{:S(2)}) collective-permute-start(f32[256,256]{1,0:T(8,128)S(1)} %add_add_fusion.1), channel_id=1, source_target_pairs={{0,8},{1,9},{33,41},{64,72},{65,73},{97,105},{128,136},{129,137},{... | collective-permute-start | bytes 786440 | tf_op jit(solution)/shard_map/ppermute | solution.py:236
  29.5 21.1 %collective-permute-start.13 = (f32[256,256]{1,0:T(8,128)S(1)}, f32[256,256]{1,0:T(8,128)S(1)}, u32[]{:S(2)}, u32[]{:S(2)}) collective-permute-start(f32[256,256]{1,0:T(8,128)S(1)} %add_add_fusion), channel_id=1, source_target_pairs={{0,4},{1,5},{8,12},{9,13},{16,20},{17,21},{24,28},{25,29},{33,37},... | collective-permute-start | bytes 786440 | tf_op jit(solution)/shard_map/ppermute | solution.py:236
  30.2 15.1 %collective-permute-start.12 = (f32[128,256]{1,0:T(8,128)S(1)}, f32[128,256]{1,0:T(8,128)S(1)}, u32[]{:S(2)}, u32[]{:S(2)}) collective-permute-start(f32[128,256]{1,0:T(8,128)S(1)} %add_add_fusion.2), channel_id=1, source_target_pairs={{0,3},{1,0},{2,1},{3,2},{4,7},{5,4},{6,5},{7,6},{8,11},{9,8},{10,9... | collective-permute-start | bytes 393224 | tf_op jit(solution)/shard_map/ppermute | solution.py:236
  30.3 16.8 %collective-permute-start.11 = (f32[128,256]{1,0:T(8,128)S(1)}, f32[128,256]{1,0:T(8,128)S(1)}, u32[]{:S(2)}, u32[]{:S(2)}) collective-permute-start(f32[128,256]{1,0:T(8,128)S(1)} %add_add_fusion.2), channel_id=1, source_target_pairs={{0,2},{1,3},{2,0},{3,1},{4,6},{5,7},{6,4},{7,5},{8,10},{9,11},{10,... | collective-permute-start | bytes 393224 | tf_op jit(solution)/shard_map/ppermute | solution.py:236
  44.7 5.0 %collective-permute-start.10 = (f32[128,256]{1,0:T(8,128)S(1)}, f32[128,256]{1,0:T(8,128)S(1)}, u32[]{:S(2)}, u32[]{:S(2)}) collective-permute-start(f32[128,256]{1,0:T(8,128)S(1)} %add_add_fusion.2), channel_id=1, source_target_pairs={{0,1},{1,2},{2,3},{3,0},{4,5},{5,6},{6,7},{7,4},{8,9},{9,10},{10,1... | collective-permute-start | bytes 393224 | tf_op jit(solution)/shard_map/ppermute | solution.py:236
  50.6 2.7 %collective-permute-start.16 = (f32[256,256]{1,0:T(8,128)S(1)}, f32[256,256]{1,0:T(8,128)S(1)}, u32[]{:S(2)}, u32[]{:S(2)}) collective-permute-start(f32[256,256]{1,0:T(8,128)S(1)} %add.56), channel_id=1, source_target_pairs={{0,1},{1,2},{4,5},{5,6},{8,9},{9,10},{12,13},{13,14},{16,17},{17,1... | collective-permute-start | bytes 786440 | tf_op jit(solution)/shard_map/ppermute | solution.py:236
  51.3 2.0 %collective-permute-start.15 = (f32[256,256]{1,0:T(8,128)S(1)}, f32[256,256]{1,0:T(8,128)S(1)}, u32[]{:S(2)}, u32[]{:S(2)}) collective-permute-start(f32[256,256]{1,0:T(8,128)S(1)} %add.56), channel_id=1, source_target_pairs={{0,2},{1,3},{4,6},{5,7},{8,10},{9,11},{12,14},{13,15},{16,18},{17,... | collective-permute-start | bytes 786440 | tf_op jit(solution)/shard_map/ppermute | solution.py:236
  52.0 8.4 %collective-permute-start.14 = (f32[256,256]{1,0:T(8,128)S(1)}, f32[256,256]{1,0:T(8,128)S(1)}, u32[]{:S(2)}, u32[]{:S(2)}) collective-permute-start(f32[256,256]{1,0:T(8,128)S(1)} %add.56), channel_id=1, source_target_pairs={{0,3},{1,0},{4,7},{5,4},{8,11},{9,8},{12,15},{13,12},{16,19},{17,1... | collective-permute-start | bytes 786440 | tf_op jit(solution)/shard_map/ppermute | solution.py:236
  60.5 11.2 %collective-permute-start.17 = (f32[256,256]{1,0:T(8,128)S(1)}, f32[256,256]{1,0:T(8,128)S(1)}, u32[]{:S(2)}, u32[]{:S(2)}) collective-permute-start(f32[256,256]{1,0:T(8,128)S(1)} %get-tuple-element.54), channel_id=1, source_target_pairs={{0,32},{1,33},{2,34},{3,35},{4,36},{5,37},{6,38},{7,39},{8,40},{9,... | collective-permute-start | bytes 786440 | tf_op jit(solution)/shard_map/ppermute | solution.py:236
  61.8 10.3 %collective-permute-start.18 = (f32[256,256]{1,0:T(8,128)S(1)}, f32[256,256]{1,0:T(8,128)S(1)}, u32[]{:S(2)}, u32[]{:S(2)}) collective-permute-start(f32[256,256]{1,0:T(8,128)S(1)} %get-tuple-element.53), channel_id=1, source_target_pairs={{0,32},{1,33},{2,34},{3,35},{4,36},{5,37},{6,38},{7,39},{8,40},{9,... | collective-permute-start | bytes 786440 | tf_op jit(solution)/shard_map/ppermute | solution.py:236
  72.1 31.3 %copy-start.1 = (s32[64,64]{1,0:T(8,128)S(1)}, s32[64,64]{1,0:T(8,128)}, u32[]{:S(2)}) copy-start(s32[64,64]{1,0:T(8,128)} %pattern.3) | copy-start | bytes 49156
  72.1 28.9 %collective-permute-start.21 = (f32[2,256,256]{2,1,0:T(8,128)S(1)}, f32[2,256,256]{2,1,0:T(8,128)S(1)}, u32[]{:S(2)}, u32[]{:S(2)}) collective-permute-start(f32[2,256,256]{2,1,0:T(8,128)S(1)} %bitcast.35), channel_id=1, source_target_pairs={{0,64},{1,65},{2,66},{3,67},{4,68},{5,69},{6,70},{7,71},{8,72},{9,... | collective-permute-start | bytes 1572872 | tf_op jit(solution)/shard_map/ppermute | solution.py:236
  73.5 27.6 %collective-permute-start.20 = (f32[2,256,256]{2,1,0:T(8,128)S(1)}, f32[2,256,256]{2,1,0:T(8,128)S(1)}, u32[]{:S(2)}, u32[]{:S(2)}) collective-permute-start(f32[2,256,256]{2,1,0:T(8,128)S(1)} %bitcast.36), channel_id=1, source_target_pairs={{0,128},{1,129},{2,130},{3,131},{4,132},{5,133},{6,134},{7,135},{8... | collective-permute-start | bytes 1572872 | tf_op jit(solution)/shard_map/ppermute | solution.py:236
  77.9 23.2 %collective-permute-start.19 = (f32[2,256,256]{2,1,0:T(8,128)S(1)}, f32[2,256,256]{2,1,0:T(8,128)S(1)}, u32[]{:S(2)}, u32[]{:S(2)}) collective-permute-start(f32[2,256,256]{2,1,0:T(8,128)S(1)} %bitcast.37), channel_id=1, source_target_pairs={{0,192},{1,193},{2,194},{3,195},{4,196},{5,197},{6,198},{7,199},{8... | collective-permute-start | bytes 1572872 | tf_op jit(solution)/shard_map/ppermute | solution.py:236
  101.2 2.2 %collective-permute-start.22 = (f32[2,256,256]{2,1,0:T(8,128)S(1)}, f32[2,256,256]{2,1,0:T(8,128)S(1)}, u32[]{:S(2)}, u32[]{:S(2)}) collective-permute-start(f32[2,256,256]{2,1,0:T(8,128)S(1)} %select_select_fusion.y0), channel_id=1, source_target_pairs={{0,32},{1,33},{2,34},{3,35},{4,36},{5,37},{6,38},{7,39},{8,40},{9,... | collective-permute-start | bytes 1572872 | tf_op jit(solution)/shard_map/ppermute | solution.py:236
  101.9 5.2 %copy-start = (s32[4]{0:T(128)}, s32[4]{0:T(128)S(1)}, u32[]{:S(2)}) copy-start(s32[4]{0:T(128)S(1)} %pad_add_fusion.ids) | copy-start | bytes 52
  107.1 1.0 copy-start.2
  108.1 0.8 copy-start.3
  108.9 0.8 copy-start.4
  109.7 0.8 copy-start.5
Sparse Core Ops, SparseCore 0:
  50.8 53.7 all-gather.2

commit v4 on v3

--- a/solution.py
+++ b/solution.py
@@ -17,8 +17,27 @@
 VMEM = pl.BlockSpec(memory_space=pltpu.VMEM)
 
 
-def dot(a, b, contract=((1,), (0,))):
-    return lax.dot_general(a, b, (contract, ((), ())), precision=lax.Precision.HIGHEST, preferred_element_type=jnp.float32)
+LEFT = {3: (0, 0, 1, 0, 1, 2), 2: (0, 1, 0)}
+RIGHT = {3: (0, 1, 0, 2, 1, 0), 2: (0, 0, 1)}
+
+
+def split(value, count=3):
+    parts = []
+    for number in range(count):
+        parts.append(value.astype(jnp.bfloat16))
+        if number + 1 < count:
+            value = value - parts[-1].astype(jnp.float32)
+    return parts
+
+
+def product(left, right, count=3):
+    a = jnp.concatenate([left[k] for k in LEFT[count]], axis=1)
+    b = jnp.concatenate([right[k] for k in RIGHT[count]], axis=0)
+    return jnp.dot(a, b, preferred_element_type=jnp.float32)
+
+
+def dot(a, b):
+    return product(split(a), split(b))
 
 
 def invert_factor(block):
@@ -76,10 +95,10 @@
     h = HALF
     top = invert_factor(block[:h, :h])
     link = dot(top, block[:h, h:])
-    low = invert_factor(block[h:, h:] - dot(link, link, ((0,), (0,))))
+    low = invert_factor(block[h:, h:] - dot(link.T, link))
     out[:h, :h] = top
     out[:h, h:] = jnp.zeros((h, h), jnp.float32)
-    out[h:, :h] = -dot(dot(low, link, ((1,), (1,))), top)
+    out[h:, :h] = -dot(dot(low, link.T), top)
     out[h:, h:] = low
 
 
@@ -87,7 +106,7 @@
     invert_pair(a00[...], inv00)
     link = dot(inv00[...], a01[...])
     u01[...] = link
-    invert_pair(a11[...] - dot(link, link, ((0,), (0,))), inv11)
+    invert_pair(a11[...] - dot(link.T, link), inv11)
 
 
 def factor_pivots(a00, a01, a11):
@@ -103,28 +122,9 @@
     )(a00, a01, a11)
 
 
-LEFT = {3: (0, 0, 1, 0, 1, 2), 2: (0, 1, 0)}
-RIGHT = {3: (0, 1, 0, 2, 1, 0), 2: (0, 0, 1)}
-
-
-def split(value, count=3):
-    parts = []
-    for number in range(count):
-        parts.append(value.astype(jnp.bfloat16))
-        if number + 1 < count:
-            value = value - parts[-1].astype(jnp.float32)
-    return parts
-
-
-def product(left, right, count=3):
-    a = jnp.concatenate([left[k] for k in LEFT[count]], axis=1)
-    b = jnp.concatenate([right[k] for k in RIGHT[count]], axis=0)
-    return jnp.dot(a, b, preferred_element_type=jnp.float32)
-
-
 def columns_kernel(ids, pattern, y0, y1, inv00, u01, inv11, back0, back1, link, cols):
     for out, value in ((back0, inv00[...].T), (back1, inv11[...].T), (link, u01[...])):
-        for number, part in enumerate(split(value)):
+        for number, part in enumerate(split(value, 2)):
             out[number] = part
     q = ids[1]
     swap = ids[2] == 1
@@ -141,7 +141,7 @@
 
 def solve_columns(ids, pattern, y0, y1, inv00, u01, inv11):
     smem = pl.BlockSpec(memory_space=pltpu.SMEM)
-    parts = jax.ShapeDtypeStruct((3, BLK, BLK), jnp.bfloat16)
+    parts = jax.ShapeDtypeStruct((2, BLK, BLK), jnp.bfloat16)
     return pl.pallas_call(
         columns_kernel,
         out_shape=(parts, parts, parts, jax.ShapeDtypeStruct((2, 2, 2 * BLK, BLK), jnp.bfloat16)),
@@ -158,12 +158,12 @@
     p, q = (ids[0], ids[1])
     slots = [(ids[3] + 4 - m) % 4 for m in range(4)]
     raw = [jnp.concatenate([g[k, slot] for slot in slots], axis=0) for k in range(2)]
-    first = product(split(raw[0]), back0)
-    x0 = split(first)
-    linked = product(x0, link)
+    first = product(split(raw[0], 2), back0, 2)
+    x0 = split(first, 2)
+    linked = product(x0, link, 2)
     w = [pattern[(j + 4 * h) * 8 + p, 1].astype(jnp.float32) for h in range(2)]
     left = [raw[1][h * BLK : (h + 1) * BLK] - w[h] * linked[h * BLK : (h + 1) * BLK] for h in range(2)]
-    second = product(split(jnp.concatenate(left, axis=0)), back1)
+    second = product(split(jnp.concatenate(left, axis=0), 2), back1, 2)
     x1 = split(second, 2)
     solved = [jnp.concatenate([x0[k], x1[k]], axis=1) for k in range(2)]
     for h in range(2):
@@ -215,12 +215,12 @@
             in_specs=[
                 block,
                 pl.BlockSpec((2, 4, HALF, BLK), lambda j, *_: (j, 0, 0, 0)),
-                *[whole(3, BLK, BLK)] * 3,
+                *[whole(2, BLK, BLK)] * 3,
                 whole(2, 2, 2 * BLK, BLK),
             ],
             out_specs=block,
         ),
-        compiler_params=pltpu.CompilerParams(vmem_limit_bytes=60 << 20),
+        compiler_params=pltpu.CompilerParams(vmem_limit_bytes=50 << 20),
         cost_estimate=pl.CostEstimate(flops=12_000_000_000, bytes_accessed=14 << 20, transcendentals=0),
         name="update",
     )(ids, pattern, local, g, back0, back1, link, cols)
@@ -255,23 +255,22 @@
     own = head[0]
     starts = lambda b, d: d == 1 or (b == 0 and d == 0)
     carrier = (y == 1) | ((core == 0) & (y == 0))
-    along = [shifted(own, x=k, where=lambda a, b, c, d: a == 0 and c == 0 and starts(b, d)) for k in (1, 3, 2)]
     parts = []
     for m in range(4):
         pairs = [(32 * c + s, (s % 8) * 32 + 8 * (s // 8) + 4 * c + m) for c in range(2) for s in range(32)]
         parts.append(lax.ppermute(quarters[m], AXES, pairs))
+    along = [shifted(own, x=k, where=lambda a, b, c, d: a == 0 and c == 0 and starts(b, d)) for k in (1, 3, 2)]
     pivot = jnp.where((x == 0) & (z == 0) & carrier, own, 0.0) + along[0] + along[1] + along[2]
+    mine = parts[0] + parts[1] + parts[2] + parts[3]
+    mine, pivot = tie(mine, pivot)
+
+    groups = [[NY * b + a for b in range(NZ)] for a in range(NY)]
+    g = jnp.stack([mine] + [shifted(mine, y=k) for k in (1, 2, 3)])
+    g = lax.all_gather(g, "col", axis=0, axis_index_groups=groups)
     along = [shifted(pivot, z=k, where=lambda a, b, c, d: c == 0 and starts(b, d)) for k in (2, 6, 4)]
     pivot = pivot + along[0] + along[1] + along[2]
-    mine = parts[0] + parts[1] + parts[2] + parts[3]
-    mine, pivot = tie(mine, pivot)
-
-    g = jnp.stack([mine] + [shifted(mine, y=k) for k in (1, 2, 3)])
     pivot = pivot + shifted(pivot, z=1, where=lambda a, b, c, d: c % 2 == 0 and starts(b, d))
-    g, pivot = tie(g, pivot)
-
-    groups = [[NY * b + a for b in range(NZ)] for a in range(NY)]
-    g = lax.all_gather(g, "col", axis=0, axis_index_groups=groups)
+
     got = [pivot] + [shifted(pivot, y=k, where=lambda a, b, c, d: starts(b, d)) for k in (1, 2, 3)]
     first = pick(y, got)
     rest = pick((y + 3) % 4, got)

time: 135 us -> 147 us (1.089)
  the two profiles are of different devices: /device:TPU:65 before, /device:TPU:33 now
where the time goes in v4:
time: 147 us
  waiting for transfers between devices  47 us (32%)
  starting transfers between devices  45.9 us (31%)
  Pallas kernels  36.4 us (25%)
  between operations  13.8 us (9%)
  local copies, waits for them, and re-layouts  1.99 us (1%)
    ppermute x19, waiting for transfers between devices, shifted(): return lax.ppermute(value, AXES, pairs)  44.5 us
    ppermute x19, starting transfers between devices, shifted(): return lax.ppermute(value, AXES, pairs)  34.4 us
    pallas_call x1, Pallas kernels, factor_pivots(): pl.pallas_call(pivots_kernel, out_shape=(shape, shape, shape), in_specs=[...  20.6 us
    pallas_call x1, Pallas kernels, update(): pl.pallas_call(update_kernel, out_shape=jax.ShapeDtypeStruct(local.shape,...  12.1 us
    ppermute x4, starting transfers between devices, per_device(): parts.append(lax.ppermute(quarters[m], AXES, pairs))  11.6 us
    pallas_call x1, Pallas kernels, solve_columns(): pl.pallas_call(columns_kernel, out_shape=(parts, parts, parts, jax.ShapeD...  3.66 us
  transfers between devices with their start and end apart: 24, of which 8 were waited for; matrix products, arithmetic and copies ran while one was open for 0% of the time, Pallas kernels for 17%

profile of v4, /device:TPU:33, one launch (start us, length us, event | category | flops | bytes accessed | tf_op | source)
XLA Modules:
  0.0 146.6 jit_solution(10957010683146667834)
XLA Ops:
  6.5 0.0 all-gather.3.cloned.1.call-start
  6.5 1.4 slice.18
  7.9 0.5 copy.12
  8.5 6.2 %collective-permute-start.1 = (f32[128,256]{1,0:T(8,128)S(1)}, f32[128,256]{1,0:T(8,128)S(1)}, u32[]{:S(2)}, u32[]{:S(2)}) collective-permute-start(f32[128,256]{1,0:T(8,128)S(1)} %get-tuple-element.53), channel_id=1, source_target_pairs={{0,1},{1,33},{2,65},{3,97},{4,129},{5,161},{6,193},{7,225},{8,9},{... | collective-permute-start | bytes 393224 | tf_op jit(solution)/shard_map/ppermute | solution.py:261
  14.7 2.1 %collective-permute-start.3 = (f32[128,256]{1,0:T(8,128)S(1)}, f32[128,256]{1,0:T(8,128)S(1)}, u32[]{:S(2)}, u32[]{:S(2)}) collective-permute-start(f32[128,256]{1,0:T(8,128)S(1)} %get-tuple-element.54), channel_id=1, source_target_pairs={{0,3},{1,35},{2,67},{3,99},{4,131},{5,163},{6,195},{7,227},{8,11},... | collective-permute-start | bytes 393224 | tf_op jit(solution)/shard_map/ppermute | solution.py:261
  16.8 1.3 collective-permute-start.2
  18.1 1.9 %collective-permute-start = (f32[128,256]{1,0:T(8,128)S(1)}, f32[128,256]{1,0:T(8,128)S(1)}, u32[]{:S(2)}, u32[]{:S(2)}) collective-permute-start(f32[128,256]{1,0:T(8,128)S(1)} %get-tuple-element.56), channel_id=1, source_target_pairs={{0,0},{1,32},{2,64},{3,96},{4,128},{5,160},{6,192},{7,224},{8,8},{... | collective-permute-start | bytes 393224 | tf_op jit(solution)/shard_map/ppermute | solution.py:261
  20.1 0.7 collective-permute-start.5
  20.8 0.0 collective-permute-done.1
  20.8 0.7 collective-permute-start.4
  21.5 0.0 collective-permute-done.3
  21.5 0.7 collective-permute-start.6
  22.3 0.0 collective-permute-done.2
  22.3 2.5 %collective-permute-done = f32[128,256]{1,0:T(8,128)S(1)} collective-permute-done((f32[128,256]{1,0:T(8,128)S(1)}, f32[128,256]{1,0:T(8,128)S(1)}, u32[]{:S(2)}, u32[]{:S(2)}) %collective-permute-start) | collective-permute-done | bytes 131104 | tf_op jit(solution)/shard_map/ppermute | solution.py:261
  24.9 0.0 collective-permute-done.5
  24.9 0.0 collective-permute-done.4
  24.9 0.0 collective-permute-done.6
  24.9 0.1 add_add_fusion.1
  25.0 1.4 collective-permute-start.22
  26.3 0.1 collective-permute-start.21
  26.4 0.8 collective-permute-start.20
  27.2 2.1 %collective-permute-done.22 = f32[128,256]{1,0:T(8,128)S(1)} collective-permute-done((f32[128,256]{1,0:T(8,128)S(1)}, f32[128,256]{1,0:T(8,128)S(1)}, u32[]{:S(2)}, u32[]{:S(2)}) %collective-permute-start.22) | collective-permute-done | bytes 131104 | tf_op jit(solution)/shard_map/ppermute | solution.py:236
  29.3 3.2 %collective-permute-done.21 = f32[128,256]{1,0:T(8,128)S(1)} collective-permute-done((f32[128,256]{1,0:T(8,128)S(1)}, f32[128,256]{1,0:T(8,128)S(1)}, u32[]{:S(2)}, u32[]{:S(2)}) %collective-permute-start.21) | collective-permute-done | bytes 131104 | tf_op jit(solution)/shard_map/ppermute | solution.py:236
  32.4 3.3 %collective-permute-done.20 = f32[128,256]{1,0:T(8,128)S(1)} collective-permute-done((f32[128,256]{1,0:T(8,128)S(1)}, f32[128,256]{1,0:T(8,128)S(1)}, u32[]{:S(2)}, u32[]{:S(2)}) %collective-permute-start.20) | collective-permute-done | bytes 131104 | tf_op jit(solution)/shard_map/ppermute | solution.py:236
  35.7 0.8 pad_maximum_fusion
  36.5 0.0 all-gather.3.cloned.1.call-update
  36.6 0.7 collective-permute-start.9
  37.2 0.7 collective-permute-start.8
  37.9 0.7 collective-permute-start.7
  38.6 0.0 collective-permute-done.9
  38.6 0.0 collective-permute-done.8
  38.6 0.0 collective-permute-done.7
  38.6 0.1 add_add_fusion
  38.7 0.7 collective-permute-start.10
  39.4 0.0 collective-permute-done.10
  39.5 0.7 collective-permute-start.13
  40.1 0.7 collective-permute-start.12
  40.8 1.3 collective-permute-start.11
  42.2 0.0 collective-permute-done.13
  42.2 0.0 collective-permute-done.12
  42.2 33.2 %collective-permute-done.11 = f32[256,256]{1,0:T(8,128)S(1)} collective-permute-done((f32[256,256]{1,0:T(8,128)S(1)}, f32[256,256]{1,0:T(8,128)S(1)}, u32[]{:S(2)}, u32[]{:S(2)}) %collective-permute-start.11) | collective-permute-done | bytes 262176 | tf_op jit(solution)/shard_map/ppermute | solution.py:236
  75.4 0.1 select_select_fusion.1
  75.5 1.3 collective-permute-start.14
  76.8 12.7 %collective-permute-start.15 = (f32[256,256]{1,0:T(8,128)S(1)}, f32[256,256]{1,0:T(8,128)S(1)}, u32[]{:S(2)}, u32[]{:S(2)}) collective-permute-start(f32[256,256]{1,0:T(8,128)S(1)} %get-tuple-element.49), channel_id=1, source_target_pairs={{0,32},{1,33},{2,34},{3,35},{4,36},{5,37},{6,38},{7,39},{8,40},{9,... | collective-permute-start | bytes 786440 | tf_op jit(solution)/shard_map/ppermute | solution.py:236
  89.5 0.9 collective-permute-done.14
  90.4 0.3 collective-permute-done.15
  90.8 0.0 copy-start
  90.8 1.3 collective-permute-start.18
  92.2 7.3 %collective-permute-start.17 = (f32[2,256,256]{2,1,0:T(8,128)S(1)}, f32[2,256,256]{2,1,0:T(8,128)S(1)}, u32[]{:S(2)}, u32[]{:S(2)}) collective-permute-start(f32[2,256,256]{2,1,0:T(8,128)S(1)} %bitcast.36), channel_id=1, source_target_pairs={{0,128},{1,129},{2,130},{3,131},{4,132},{5,133},{6,134},{7,135},{8... | collective-permute-start | bytes 1572872 | tf_op jit(solution)/shard_map/ppermute | solution.py:236
  99.4 1.5 %collective-permute-start.16 = (f32[2,256,256]{2,1,0:T(8,128)S(1)}, f32[2,256,256]{2,1,0:T(8,128)S(1)}, u32[]{:S(2)}, u32[]{:S(2)}) collective-permute-start(f32[2,256,256]{2,1,0:T(8,128)S(1)} %bitcast.37), channel_id=1, source_target_pairs={{0,192},{1,193},{2,194},{3,195},{4,196},{5,197},{6,198},{7,199},{8... | collective-permute-start | bytes 1572872 | tf_op jit(solution)/shard_map/ppermute | solution.py:236
  101.0 20.6 %factor_pivots.1 = (f32[256,256]{1,0:T(8,128)S(1)}, f32[256,256]{1,0:T(8,128)S(1)}, f32[256,256]{1,0:T(8,128)S(1)}) custom-call(f32[256,256]{1,0:T(8,128)S(1)} %broadcast_select_fusion.2.a00, f32[256,256]{1,0:T(8,128)S(1)} %get-tuple-element.30.a01, f32[256,256]{1,0:T(8,128)S(1)} %get-tuple-element.31.a11), custom_call_target="tpu_custom_call" | custom-call | flops 24999999488 | bytes 1048576 | tf_op jit(solution)/shard_map/factor_pivots/pallas_call | solution.py:114
  121.6 0.0 collective-permute-done.18
  121.6 0.0 collective-permute-done.17
  121.6 0.0 collective-permute-done.16
  121.6 0.1 select_select_fusion.y0
  121.8 0.6 collective-permute-start.19
  122.4 0.1 pad_add_fusion.ids
  122.5 1.5 collective-permute-done.19.y1
  123.9 0.0 copy-done
  123.9 3.7 %solve_columns.1 = (bf16[2,256,256]{2,1,0:T(8,128)(2,1)S(1)}, bf16[2,256,256]{2,1,0:T(8,128)(2,1)S(1)}, bf16[2,256,256]{2,1,0:T(8,128)(2,1)S(1)}, bf16[2,2,512,256]{3,2,1,0:T(8,128)(2,1)S(1)}) custom-call(s32[4]{0:T(128)S(1)} %pad_add_fusion.ids, s32[64,64]{1,0:T(8,128)S(1)} %copy-done, f32[2,256,256]{2,1,0:T(8,128)S(1)} %select_select_fusion.y0, ...), custom_call_target="tpu_custom_call" | custom-call | flops 3000000000 | bytes 4194304 | tf_op jit(solution)/shard_map/solve_columns/pallas_call | solution.py:145
  127.6 0.0 all-gather.3.cloned.1.call-done
  127.6 12.1 %update.1 = f32[2,4,1024,128]{3,2,1,0:T(8,128)} custom-call(s32[4]{0:T(128)S(1)} %pad_add_fusion.ids, s32[64,64]{1,0:T(8,128)S(1)} %copy-done, f32[2,4,1024,128]{3,2,1,0:T(8,128)} %bitcast.44, f32[8,4,128,256]{3,2,1,0:T(8,128)} %bitcast.45, bf16[2,256,256]{2,1,0:T(8,128)(2,1)S(1)} %get-tuple-element.45.back0, ...), custom_call_target="tpu_custom_call" | custom-call | flops 12000000000 | bytes 14680064 | tf_op jit(solution)/shard_map/update/pallas_call | solution.py:209
  (7 shorter events, 0.2 us)
Async XLA Ops:
  6.5 121.1 %all-gather.3.cloned.1.call-start = ((), (), s32[]{:S(2)}) async-start(), calls=%async_computation | async-start | bytes 4718592 | tf_op jit(solution)/shard_map/all_gather | solution.py:269
  8.5 12.3 %collective-permute-start.1 = (f32[128,256]{1,0:T(8,128)S(1)}, f32[128,256]{1,0:T(8,128)S(1)}, u32[]{:S(2)}, u32[]{:S(2)}) collective-permute-start(f32[128,256]{1,0:T(8,128)S(1)} %get-tuple-element.53), channel_id=1, source_target_pairs={{0,1},{1,33},{2,65},{3,97},{4,129},{5,161},{6,193},{7,225},{8,9},{... | collective-permute-start | bytes 393224 | tf_op jit(solution)/shard_map/ppermute | solution.py:261
  14.7 6.8 %collective-permute-start.3 = (f32[128,256]{1,0:T(8,128)S(1)}, f32[128,256]{1,0:T(8,128)S(1)}, u32[]{:S(2)}, u32[]{:S(2)}) collective-permute-start(f32[128,256]{1,0:T(8,128)S(1)} %get-tuple-element.54), channel_id=1, source_target_pairs={{0,3},{1,35},{2,67},{3,99},{4,131},{5,163},{6,195},{7,227},{8,11},... | collective-permute-start | bytes 393224 | tf_op jit(solution)/shard_map/ppermute | solution.py:261
  16.8 5.4 %collective-permute-start.2 = (f32[128,256]{1,0:T(8,128)S(1)}, f32[128,256]{1,0:T(8,128)S(1)}, u32[]{:S(2)}, u32[]{:S(2)}) collective-permute-start(f32[128,256]{1,0:T(8,128)S(1)} %get-tuple-element.55), channel_id=1, source_target_pairs={{0,2},{1,34},{2,66},{3,98},{4,130},{5,162},{6,194},{7,226},{8,10},... | collective-permute-start | bytes 393224 | tf_op jit(solution)/shard_map/ppermute | solution.py:261
  18.1 6.7 %collective-permute-start = (f32[128,256]{1,0:T(8,128)S(1)}, f32[128,256]{1,0:T(8,128)S(1)}, u32[]{:S(2)}, u32[]{:S(2)}) collective-permute-start(f32[128,256]{1,0:T(8,128)S(1)} %get-tuple-element.56), channel_id=1, source_target_pairs={{0,0},{1,32},{2,64},{3,96},{4,128},{5,160},{6,192},{7,224},{8,8},{... | collective-permute-start | bytes 393224 | tf_op jit(solution)/shard_map/ppermute | solution.py:261
  20.1 4.7 %collective-permute-start.5 = (f32[256,256]{1,0:T(8,128)S(1)}, f32[256,256]{1,0:T(8,128)S(1)}, u32[]{:S(2)}, u32[]{:S(2)}) collective-permute-start(f32[256,256]{1,0:T(8,128)S(1)} %slice_bitcast_fusion), channel_id=1, source_target_pairs={{0,192},{1,193},{33,225}} | collective-permute-start | bytes 786440 | tf_op jit(solution)/shard_map/ppermute | solution.py:236
  20.8 4.0 %collective-permute-start.4 = (f32[256,256]{1,0:T(8,128)S(1)}, f32[256,256]{1,0:T(8,128)S(1)}, u32[]{:S(2)}, u32[]{:S(2)}) collective-permute-start(f32[256,256]{1,0:T(8,128)S(1)} %slice_bitcast_fusion), channel_id=1, source_target_pairs={{0,64},{1,65},{33,97}} | collective-permute-start | bytes 786440 | tf_op jit(solution)/shard_map/ppermute | solution.py:236
  21.5 3.3 %collective-permute-start.6 = (f32[256,256]{1,0:T(8,128)S(1)}, f32[256,256]{1,0:T(8,128)S(1)}, u32[]{:S(2)}, u32[]{:S(2)}) collective-permute-start(f32[256,256]{1,0:T(8,128)S(1)} %slice_bitcast_fusion), channel_id=1, source_target_pairs={{0,128},{1,129},{33,161}} | collective-permute-start | bytes 786440 | tf_op jit(solution)/shard_map/ppermute | solution.py:236
  25.0 4.3 %collective-permute-start.22 = (f32[128,256]{1,0:T(8,128)S(1)}, f32[128,256]{1,0:T(8,128)S(1)}, u32[]{:S(2)}, u32[]{:S(2)}) collective-permute-start(f32[128,256]{1,0:T(8,128)S(1)} %add_add_fusion.2), channel_id=1, source_target_pairs={{0,3},{1,0},{2,1},{3,2},{4,7},{5,4},{6,5},{7,6},{8,11},{9,8},{10,9... | collective-permute-start | bytes 393224 | tf_op jit(solution)/shard_map/ppermute | solution.py:236
  26.3 6.1 %collective-permute-start.21 = (f32[128,256]{1,0:T(8,128)S(1)}, f32[128,256]{1,0:T(8,128)S(1)}, u32[]{:S(2)}, u32[]{:S(2)}) collective-permute-start(f32[128,256]{1,0:T(8,128)S(1)} %add_add_fusion.2), channel_id=1, source_target_pairs={{0,2},{1,3},{2,0},{3,1},{4,6},{5,7},{6,4},{7,5},{8,10},{9,11},{10,... | collective-permute-start | bytes 393224 | tf_op jit(solution)/shard_map/ppermute | solution.py:236
  26.4 9.3 %collective-permute-start.20 = (f32[128,256]{1,0:T(8,128)S(1)}, f32[128,256]{1,0:T(8,128)S(1)}, u32[]{:S(2)}, u32[]{:S(2)}) collective-permute-start(f32[128,256]{1,0:T(8,128)S(1)} %add_add_fusion.2), channel_id=1, source_target_pairs={{0,1},{1,2},{2,3},{3,0},{4,5},{5,6},{6,7},{7,4},{8,9},{9,10},{10,1... | collective-permute-start | bytes 393224 | tf_op jit(solution)/shard_map/ppermute | solution.py:236
  36.6 2.1 %collective-permute-start.9 = (f32[256,256]{1,0:T(8,128)S(1)}, f32[256,256]{1,0:T(8,128)S(1)}, u32[]{:S(2)}, u32[]{:S(2)}) collective-permute-start(f32[256,256]{1,0:T(8,128)S(1)} %add_add_fusion.1), channel_id=1, source_target_pairs={{0,16},{1,17},{33,49},{64,80},{65,81},{97,113},{128,144},{129,145}... | collective-permute-start | bytes 786440 | tf_op jit(solution)/shard_map/ppermute | solution.py:236
  37.2 1.4 collective-permute-start.8
  37.9 0.7 collective-permute-start.7
  38.7 0.7 collective-permute-start.10
  39.5 2.7 %collective-permute-start.13 = (f32[256,256]{1,0:T(8,128)S(1)}, f32[256,256]{1,0:T(8,128)S(1)}, u32[]{:S(2)}, u32[]{:S(2)}) collective-permute-start(f32[256,256]{1,0:T(8,128)S(1)} %add.56), channel_id=1, source_target_pairs={{0,1},{1,2},{4,5},{5,6},{8,9},{9,10},{12,13},{13,14},{16,17},{17,1... | collective-permute-start | bytes 786440 | tf_op jit(solution)/shard_map/ppermute | solution.py:236
  40.1 2.0 %collective-permute-start.12 = (f32[256,256]{1,0:T(8,128)S(1)}, f32[256,256]{1,0:T(8,128)S(1)}, u32[]{:S(2)}, u32[]{:S(2)}) collective-permute-start(f32[256,256]{1,0:T(8,128)S(1)} %add.56), channel_id=1, source_target_pairs={{0,2},{1,3},{4,6},{5,7},{8,10},{9,11},{12,14},{13,15},{16,18},{17,... | collective-permute-start | bytes 786440 | tf_op jit(solution)/shard_map/ppermute | solution.py:236
  40.8 34.6 %collective-permute-start.11 = (f32[256,256]{1,0:T(8,128)S(1)}, f32[256,256]{1,0:T(8,128)S(1)}, u32[]{:S(2)}, u32[]{:S(2)}) collective-permute-start(f32[256,256]{1,0:T(8,128)S(1)} %add.56), channel_id=1, source_target_pairs={{0,3},{1,0},{4,7},{5,4},{8,11},{9,8},{12,15},{13,12},{16,19},{17,1... | collective-permute-start | bytes 786440 | tf_op jit(solution)/shard_map/ppermute | solution.py:236
  75.5 14.9 %collective-permute-start.14 = (f32[256,256]{1,0:T(8,128)S(1)}, f32[256,256]{1,0:T(8,128)S(1)}, u32[]{:S(2)}, u32[]{:S(2)}) collective-permute-start(f32[256,256]{1,0:T(8,128)S(1)} %get-tuple-element.50), channel_id=1, source_target_pairs={{0,32},{1,33},{2,34},{3,35},{4,36},{5,37},{6,38},{7,39},{8,40},{9,... | collective-permute-start | bytes 786440 | tf_op jit(solution)/shard_map/ppermute | solution.py:236
  76.8 14.0 %collective-permute-start.15 = (f32[256,256]{1,0:T(8,128)S(1)}, f32[256,256]{1,0:T(8,128)S(1)}, u32[]{:S(2)}, u32[]{:S(2)}) collective-permute-start(f32[256,256]{1,0:T(8,128)S(1)} %get-tuple-element.49), channel_id=1, source_target_pairs={{0,32},{1,33},{2,34},{3,35},{4,36},{5,37},{6,38},{7,39},{8,40},{9,... | collective-permute-start | bytes 786440 | tf_op jit(solution)/shard_map/ppermute | solution.py:236
  90.8 33.1 %copy-start = (s32[64,64]{1,0:T(8,128)S(1)}, s32[64,64]{1,0:T(8,128)}, u32[]{:S(2)}) copy-start(s32[64,64]{1,0:T(8,128)} %pattern.3) | copy-start | bytes 49156
  90.8 30.8 %collective-permute-start.18 = (f32[2,256,256]{2,1,0:T(8,128)S(1)}, f32[2,256,256]{2,1,0:T(8,128)S(1)}, u32[]{:S(2)}, u32[]{:S(2)}) collective-permute-start(f32[2,256,256]{2,1,0:T(8,128)S(1)} %bitcast.35), channel_id=1, source_target_pairs={{0,64},{1,65},{2,66},{3,67},{4,68},{5,69},{6,70},{7,71},{8,72},{9,... | collective-permute-start | bytes 1572872 | tf_op jit(solution)/shard_map/ppermute | solution.py:236
  92.2 29.4 %collective-permute-start.17 = (f32[2,256,256]{2,1,0:T(8,128)S(1)}, f32[2,256,256]{2,1,0:T(8,128)S(1)}, u32[]{:S(2)}, u32[]{:S(2)}) collective-permute-start(f32[2,256,256]{2,1,0:T(8,128)S(1)} %bitcast.36), channel_id=1, source_target_pairs={{0,128},{1,129},{2,130},{3,131},{4,132},{5,133},{6,134},{7,135},{8... | collective-permute-start | bytes 1572872 | tf_op jit(solution)/shard_map/ppermute | solution.py:236
  99.4 22.2 %collective-permute-start.16 = (f32[2,256,256]{2,1,0:T(8,128)S(1)}, f32[2,256,256]{2,1,0:T(8,128)S(1)}, u32[]{:S(2)}, u32[]{:S(2)}) collective-permute-start(f32[2,256,256]{2,1,0:T(8,128)S(1)} %bitcast.37), channel_id=1, source_target_pairs={{0,192},{1,193},{2,194},{3,195},{4,196},{5,197},{6,198},{7,199},{8... | collective-permute-start | bytes 1572872 | tf_op jit(solution)/shard_map/ppermute | solution.py:236
  121.8 2.2 %collective-permute-start.19 = (f32[2,256,256]{2,1,0:T(8,128)S(1)}, f32[2,256,256]{2,1,0:T(8,128)S(1)}, u32[]{:S(2)}, u32[]{:S(2)}) collective-permute-start(f32[2,256,256]{2,1,0:T(8,128)S(1)} %select_select_fusion.y0), channel_id=1, source_target_pairs={{0,32},{1,33},{2,34},{3,35},{4,36},{5,37},{6,38},{7,39},{8,40},{9,... | collective-permute-start | bytes 1572872 | tf_op jit(solution)/shard_map/ppermute | solution.py:236
Sparse Core Ops, SparseCore 0:
  36.7 61.0 all-gather.2

commit v5 on v4

--- a/solution.py
+++ b/solution.py
@@ -255,22 +255,21 @@
     own = head[0]
     starts = lambda b, d: d == 1 or (b == 0 and d == 0)
     carrier = (y == 1) | ((core == 0) & (y == 0))
+    along = [shifted(own, z=k, where=lambda a, b, c, d: a == 0 and c == 0 and starts(b, d)) for k in (2, 6, 4)]
     parts = []
     for m in range(4):
         pairs = [(32 * c + s, (s % 8) * 32 + 8 * (s // 8) + 4 * c + m) for c in range(2) for s in range(32)]
         parts.append(lax.ppermute(quarters[m], AXES, pairs))
-    along = [shifted(own, x=k, where=lambda a, b, c, d: a == 0 and c == 0 and starts(b, d)) for k in (1, 3, 2)]
     pivot = jnp.where((x == 0) & (z == 0) & carrier, own, 0.0) + along[0] + along[1] + along[2]
+    pivot = pivot + shifted(pivot, z=1, where=lambda a, b, c, d: a == 0 and c % 2 == 0 and starts(b, d))
     mine = parts[0] + parts[1] + parts[2] + parts[3]
     mine, pivot = tie(mine, pivot)
 
     groups = [[NY * b + a for b in range(NZ)] for a in range(NY)]
     g = jnp.stack([mine] + [shifted(mine, y=k) for k in (1, 2, 3)])
     g = lax.all_gather(g, "col", axis=0, axis_index_groups=groups)
-    along = [shifted(pivot, z=k, where=lambda a, b, c, d: c == 0 and starts(b, d)) for k in (2, 6, 4)]
+    along = [shifted(pivot, x=k, where=lambda a, b, c, d: a == 0 and starts(b, d)) for k in (1, 3, 2)]
     pivot = pivot + along[0] + along[1] + along[2]
-    pivot = pivot + shifted(pivot, z=1, where=lambda a, b, c, d: c % 2 == 0 and starts(b, d))
-
     got = [pivot] + [shifted(pivot, y=k, where=lambda a, b, c, d: starts(b, d)) for k in (1, 2, 3)]
     first = pick(y, got)
     rest = pick((y + 3) % 4, got)

time: 147 us -> 137 us (0.932)
  the two profiles are of different devices: /device:TPU:33 before, /device:TPU:36 now
where the time goes in v5:
time: 137 us
  waiting for transfers between devices  57.1 us (42%)
  Pallas kernels  37.5 us (27%)
  starting transfers between devices  25.1 us (18%)
  between operations  13.8 us (10%)
  local copies, waits for them, and re-layouts  1.99 us (1%)
  other arithmetic  1.4 us (1%)
    ppermute x19, waiting for transfers between devices, shifted(): return lax.ppermute(value, AXES, pairs)  47 us
    ppermute x19, starting transfers between devices, shifted(): return lax.ppermute(value, AXES, pairs)  21.8 us
    pallas_call x1, Pallas kernels, factor_pivots(): pl.pallas_call(pivots_kernel, out_shape=(shape, shape, shape), in_specs=[...  20.6 us
    pallas_call x1, Pallas kernels, update(): pl.pallas_call(update_kernel, out_shape=jax.ShapeDtypeStruct(local.shape,...  13.2 us
    ppermute x4, waiting for transfers between devices, per_device(): parts.append(lax.ppermute(quarters[m], AXES, pairs))  10 us
    pallas_call x1, Pallas kernels, solve_columns(): pl.pallas_call(columns_kernel, out_shape=(parts, parts, parts, jax.ShapeD...  3.66 us
    ppermute x4, starting transfers between devices, per_device(): parts.append(lax.ppermute(quarters[m], AXES, pairs))  3.3 us
  transfers between devices with their start and end apart: 24, of which 12 were waited for; matrix products, arithmetic and copies ran while one was open for 1% of the time, Pallas kernels for 18%

profile of v5, /device:TPU:36, one launch (start us, length us, event | category | flops | bytes accessed | tf_op | source)
XLA Modules:
  0.0 136.9 jit_solution(8864581746552351852)
XLA Ops:
  6.5 0.0 all-gather.3.cloned.1.call-start
  6.5 1.4 %slice.18 = f32[1,1,256,2,1,256]{5,4,3,2,1,0:T(1,128)S(1)} slice(f32[8,1,256,2,1,256]{5,4,3,2,1,0:T(1,128)} %param.2), slice={[0:1], [0:1], [0:256], [0:2], [0:1], [0:256]} | slice | bytes 1048576 | tf_op jit(solution)/shard_map/slice | solution.py:252
  8.0 0.7 collective-permute-start.5
  8.7 0.7 collective-permute-start.4
  9.4 0.7 collective-permute-start.6
  10.1 0.5 copy.12
  10.6 0.7 collective-permute-start.1
  11.3 0.7 collective-permute-start.3
  12.0 0.0 collective-permute-done.5
  12.0 0.7 collective-permute-start.2
  12.7 0.0 collective-permute-done.4
  12.7 1.3 collective-permute-start
  14.0 0.0 collective-permute-done.6
  14.0 0.1 add_add_fusion.1
  14.1 0.7 collective-permute-start.7
  14.8 0.0 collective-permute-done.1
  14.8 0.0 collective-permute-done.3
  14.8 0.0 collective-permute-done.2
  14.8 10.0 %collective-permute-done = f32[128,256]{1,0:T(8,128)S(1)} collective-permute-done((f32[128,256]{1,0:T(8,128)S(1)}, f32[128,256]{1,0:T(8,128)S(1)}, u32[]{:S(2)}, u32[]{:S(2)}) %collective-permute-start) | collective-permute-done | bytes 131104 | tf_op jit(solution)/shard_map/ppermute | solution.py:262
  24.9 0.0 collective-permute-done.7
  24.9 0.6 collective-permute-start.22
  25.5 1.0 collective-permute-start.21
  26.6 1.3 collective-permute-start.20
  27.9 3.0 %collective-permute-done.22 = f32[128,256]{1,0:T(8,128)S(1)} collective-permute-done((f32[128,256]{1,0:T(8,128)S(1)}, f32[128,256]{1,0:T(8,128)S(1)}, u32[]{:S(2)}, u32[]{:S(2)}) %collective-permute-start.22) | collective-permute-done | bytes 131104 | tf_op jit(solution)/shard_map/ppermute | solution.py:236
  30.9 2.3 %collective-permute-done.21 = f32[128,256]{1,0:T(8,128)S(1)} collective-permute-done((f32[128,256]{1,0:T(8,128)S(1)}, f32[128,256]{1,0:T(8,128)S(1)}, u32[]{:S(2)}, u32[]{:S(2)}) %collective-permute-start.21) | collective-permute-done | bytes 131104 | tf_op jit(solution)/shard_map/ppermute | solution.py:236
  33.1 1.4 collective-permute-done.20
  34.5 0.8 pad_maximum_fusion
  35.3 0.0 all-gather.3.cloned.1.call-update
  35.4 1.3 collective-permute-start.10
  36.7 0.7 collective-permute-start.9
  37.4 0.7 collective-permute-start.8
  38.0 18.7 %collective-permute-done.10 = f32[256,256]{1,0:T(8,128)S(1)} collective-permute-done((f32[256,256]{1,0:T(8,128)S(1)}, f32[256,256]{1,0:T(8,128)S(1)}, u32[]{:S(2)}, u32[]{:S(2)}) %collective-permute-start.10) | collective-permute-done | bytes 262176 | tf_op jit(solution)/shard_map/ppermute | solution.py:236
  56.8 0.0 collective-permute-done.9
  56.8 0.0 collective-permute-done.8
  56.8 0.1 add_add_fusion
  56.8 5.9 %collective-permute-start.13 = (f32[256,256]{1,0:T(8,128)S(1)}, f32[256,256]{1,0:T(8,128)S(1)}, u32[]{:S(2)}, u32[]{:S(2)}) collective-permute-start(f32[256,256]{1,0:T(8,128)S(1)} %add_add_fusion), channel_id=1, source_target_pairs={{0,1},{1,2},{4,5},{5,6},{8,9},{9,10},{12,13},{13,14},{16,17},{17,1... | collective-permute-start | bytes 786440 | tf_op jit(solution)/shard_map/ppermute | solution.py:236
  62.7 1.3 collective-permute-start.12
  64.1 1.9 %collective-permute-start.11 = (f32[256,256]{1,0:T(8,128)S(1)}, f32[256,256]{1,0:T(8,128)S(1)}, u32[]{:S(2)}, u32[]{:S(2)}) collective-permute-start(f32[256,256]{1,0:T(8,128)S(1)} %add_add_fusion), channel_id=1, source_target_pairs={{0,3},{1,0},{4,7},{5,4},{8,11},{9,8},{12,15},{13,12},{16,19},{17,1... | collective-permute-start | bytes 786440 | tf_op jit(solution)/shard_map/ppermute | solution.py:236
  66.0 0.6 collective-permute-done.13
  66.6 2.8 %collective-permute-done.12 = f32[256,256]{1,0:T(8,128)S(1)} collective-permute-done((f32[256,256]{1,0:T(8,128)S(1)}, f32[256,256]{1,0:T(8,128)S(1)}, u32[]{:S(2)}, u32[]{:S(2)}) %collective-permute-start.12) | collective-permute-done | bytes 262176 | tf_op jit(solution)/shard_map/ppermute | solution.py:236
  69.4 5.6 %collective-permute-done.11 = f32[256,256]{1,0:T(8,128)S(1)} collective-permute-done((f32[256,256]{1,0:T(8,128)S(1)}, f32[256,256]{1,0:T(8,128)S(1)}, u32[]{:S(2)}, u32[]{:S(2)}) %collective-permute-start.11) | collective-permute-done | bytes 262176 | tf_op jit(solution)/shard_map/ppermute | solution.py:236
  75.0 0.1 select_select_fusion.1
  75.1 1.3 collective-permute-start.14
  76.4 0.1 collective-permute-start.15
  76.5 1.0 collective-permute-done.14
  77.6 0.5 collective-permute-done.15
  78.1 0.0 copy-start
  78.1 0.7 collective-permute-start.18
  78.8 1.3 collective-permute-start.17
  80.1 0.9 collective-permute-start.16
  81.0 20.6 %factor_pivots.1 = (f32[256,256]{1,0:T(8,128)S(1)}, f32[256,256]{1,0:T(8,128)S(1)}, f32[256,256]{1,0:T(8,128)S(1)}) custom-call(f32[256,256]{1,0:T(8,128)S(1)} %broadcast_select_fusion.2.a00, f32[256,256]{1,0:T(8,128)S(1)} %get-tuple-element.30.a01, f32[256,256]{1,0:T(8,128)S(1)} %get-tuple-element.31.a11), custom_call_target="tpu_custom_call" | custom-call | flops 24999999488 | bytes 1048576 | tf_op jit(solution)/shard_map/factor_pivots/pallas_call | solution.py:114
  101.6 0.0 collective-permute-done.18
  101.6 9.4 %collective-permute-done.17 = f32[2,256,256]{2,1,0:T(8,128)S(1)} collective-permute-done((f32[2,256,256]{2,1,0:T(8,128)S(1)}, f32[2,256,256]{2,1,0:T(8,128)S(1)}, u32[]{:S(2)}, u32[]{:S(2)}) %collective-permute-start.17) | collective-permute-done | bytes 524320 | tf_op jit(solution)/shard_map/ppermute | solution.py:236
  111.0 0.0 collective-permute-done.16
  111.0 0.1 select_select_fusion.y0
  111.1 0.1 collective-permute-start.19
  111.2 0.1 pad_add_fusion.ids
  111.3 1.8 %collective-permute-done.19.y1 = f32[2,256,256]{2,1,0:T(8,128)S(1)} collective-permute-done((f32[2,256,256]{2,1,0:T(8,128)S(1)}, f32[2,256,256]{2,1,0:T(8,128)S(1)}, u32[]{:S(2)}, u32[]{:S(2)}) %collective-permute-start.19) | collective-permute-done | bytes 524320 | tf_op jit(solution)/shard_map/ppermute | solution.py:236
  113.1 0.0 copy-done
  113.1 3.7 %solve_columns.1 = (bf16[2,256,256]{2,1,0:T(8,128)(2,1)S(1)}, bf16[2,256,256]{2,1,0:T(8,128)(2,1)S(1)}, bf16[2,256,256]{2,1,0:T(8,128)(2,1)S(1)}, bf16[2,2,512,256]{3,2,1,0:T(8,128)(2,1)S(1)}) custom-call(s32[4]{0:T(128)S(1)} %pad_add_fusion.ids, s32[64,64]{1,0:T(8,128)S(1)} %copy-done, f32[2,256,256]{2,1,0:T(8,128)S(1)} %select_select_fusion.y0, ...), custom_call_target="tpu_custom_call" | custom-call | flops 3000000000 | bytes 4194304 | tf_op jit(solution)/shard_map/solve_columns/pallas_call | solution.py:145
  116.8 0.0 all-gather.3.cloned.1.call-done
  116.8 13.2 %update.1 = f32[2,4,1024,128]{3,2,1,0:T(8,128)} custom-call(s32[4]{0:T(128)S(1)} %pad_add_fusion.ids, s32[64,64]{1,0:T(8,128)S(1)} %copy-done, f32[2,4,1024,128]{3,2,1,0:T(8,128)} %bitcast.44, f32[8,4,128,256]{3,2,1,0:T(8,128)} %bitcast.45, bf16[2,256,256]{2,1,0:T(8,128)(2,1)S(1)} %get-tuple-element.45.back0, ...), custom_call_target="tpu_custom_call" | custom-call | flops 12000000000 | bytes 14680064 | tf_op jit(solution)/shard_map/update/pallas_call | solution.py:209
  (7 shorter events, 0.2 us)
Async XLA Ops:
  6.5 110.3 %all-gather.3.cloned.1.call-start = ((), (), s32[]{:S(2)}) async-start(), calls=%async_computation | async-start | bytes 4718592 | tf_op jit(solution)/shard_map/all_gather | solution.py:270
  8.0 4.0 %collective-permute-start.5 = (f32[256,256]{1,0:T(8,128)S(1)}, f32[256,256]{1,0:T(8,128)S(1)}, u32[]{:S(2)}, u32[]{:S(2)}) collective-permute-start(f32[256,256]{1,0:T(8,128)S(1)} %slice_bitcast_fusion), channel_id=1, source_target_pairs={{0,24},{1,25},{33,57}} | collective-permute-start | bytes 786440 | tf_op jit(solution)/shard_map/ppermute | solution.py:236
  8.7 4.0 %collective-permute-start.4 = (f32[256,256]{1,0:T(8,128)S(1)}, f32[256,256]{1,0:T(8,128)S(1)}, u32[]{:S(2)}, u32[]{:S(2)}) collective-permute-start(f32[256,256]{1,0:T(8,128)S(1)} %slice_bitcast_fusion), channel_id=1, source_target_pairs={{0,8},{1,9},{33,41}} | collective-permute-start | bytes 786440 | tf_op jit(solution)/shard_map/ppermute | solution.py:236
  9.4 4.6 %collective-permute-start.6 = (f32[256,256]{1,0:T(8,128)S(1)}, f32[256,256]{1,0:T(8,128)S(1)}, u32[]{:S(2)}, u32[]{:S(2)}) collective-permute-start(f32[256,256]{1,0:T(8,128)S(1)} %slice_bitcast_fusion), channel_id=1, source_target_pairs={{0,16},{1,17},{33,49}} | collective-permute-start | bytes 786440 | tf_op jit(solution)/shard_map/ppermute | solution.py:236
  10.6 4.2 %collective-permute-start.1 = (f32[128,256]{1,0:T(8,128)S(1)}, f32[128,256]{1,0:T(8,128)S(1)}, u32[]{:S(2)}, u32[]{:S(2)}) collective-permute-start(f32[128,256]{1,0:T(8,128)S(1)} %get-tuple-element.53), channel_id=1, source_target_pairs={{0,1},{1,33},{2,65},{3,97},{4,129},{5,161},{6,193},{7,225},{8,9},{... | collective-permute-start | bytes 393224 | tf_op jit(solution)/shard_map/ppermute | solution.py:262
  11.3 3.5 %collective-permute-start.3 = (f32[128,256]{1,0:T(8,128)S(1)}, f32[128,256]{1,0:T(8,128)S(1)}, u32[]{:S(2)}, u32[]{:S(2)}) collective-permute-start(f32[128,256]{1,0:T(8,128)S(1)} %get-tuple-element.54), channel_id=1, source_target_pairs={{0,3},{1,35},{2,67},{3,99},{4,131},{5,163},{6,195},{7,227},{8,11},... | collective-permute-start | bytes 393224 | tf_op jit(solution)/shard_map/ppermute | solution.py:262
  12.0 2.8 %collective-permute-start.2 = (f32[128,256]{1,0:T(8,128)S(1)}, f32[128,256]{1,0:T(8,128)S(1)}, u32[]{:S(2)}, u32[]{:S(2)}) collective-permute-start(f32[128,256]{1,0:T(8,128)S(1)} %get-tuple-element.55), channel_id=1, source_target_pairs={{0,2},{1,34},{2,66},{3,98},{4,130},{5,162},{6,194},{7,226},{8,10},... | collective-permute-start | bytes 393224 | tf_op jit(solution)/shard_map/ppermute | solution.py:262
  12.7 12.1 %collective-permute-start = (f32[128,256]{1,0:T(8,128)S(1)}, f32[128,256]{1,0:T(8,128)S(1)}, u32[]{:S(2)}, u32[]{:S(2)}) collective-permute-start(f32[128,256]{1,0:T(8,128)S(1)} %get-tuple-element.56), channel_id=1, source_target_pairs={{0,0},{1,32},{2,64},{3,96},{4,128},{5,160},{6,192},{7,224},{8,8},{... | collective-permute-start | bytes 393224 | tf_op jit(solution)/shard_map/ppermute | solution.py:262
  14.1 10.8 %collective-permute-start.7 = (f32[256,256]{1,0:T(8,128)S(1)}, f32[256,256]{1,0:T(8,128)S(1)}, u32[]{:S(2)}, u32[]{:S(2)}) collective-permute-start(f32[256,256]{1,0:T(8,128)S(1)} %add_add_fusion.1), channel_id=1, source_target_pairs={{0,4},{1,5},{8,12},{9,13},{16,20},{17,21},{24,28},{25,29},{33,37},... | collective-permute-start | bytes 786440 | tf_op jit(solution)/shard_map/ppermute | solution.py:236
  24.9 5.9 %collective-permute-start.22 = (f32[128,256]{1,0:T(8,128)S(1)}, f32[128,256]{1,0:T(8,128)S(1)}, u32[]{:S(2)}, u32[]{:S(2)}) collective-permute-start(f32[128,256]{1,0:T(8,128)S(1)} %add_add_fusion.2), channel_id=1, source_target_pairs={{0,3},{1,0},{2,1},{3,2},{4,7},{5,4},{6,5},{7,6},{8,11},{9,8},{10,9... | collective-permute-start | bytes 393224 | tf_op jit(solution)/shard_map/ppermute | solution.py:236
  25.5 7.6 %collective-permute-start.21 = (f32[128,256]{1,0:T(8,128)S(1)}, f32[128,256]{1,0:T(8,128)S(1)}, u32[]{:S(2)}, u32[]{:S(2)}) collective-permute-start(f32[128,256]{1,0:T(8,128)S(1)} %add_add_fusion.2), channel_id=1, source_target_pairs={{0,2},{1,3},{2,0},{3,1},{4,6},{5,7},{6,4},{7,5},{8,10},{9,11},{10,... | collective-permute-start | bytes 393224 | tf_op jit(solution)/shard_map/ppermute | solution.py:236
  26.6 7.9 %collective-permute-start.20 = (f32[128,256]{1,0:T(8,128)S(1)}, f32[128,256]{1,0:T(8,128)S(1)}, u32[]{:S(2)}, u32[]{:S(2)}) collective-permute-start(f32[128,256]{1,0:T(8,128)S(1)} %add_add_fusion.2), channel_id=1, source_target_pairs={{0,1},{1,2},{2,3},{3,0},{4,5},{5,6},{6,7},{7,4},{8,9},{9,10},{10,1... | collective-permute-start | bytes 393224 | tf_op jit(solution)/shard_map/ppermute | solution.py:236
  35.4 21.4 %collective-permute-start.10 = (f32[256,256]{1,0:T(8,128)S(1)}, f32[256,256]{1,0:T(8,128)S(1)}, u32[]{:S(2)}, u32[]{:S(2)}) collective-permute-start(f32[256,256]{1,0:T(8,128)S(1)} %add.53), channel_id=1, source_target_pairs={{0,128},{1,129},{4,132},{5,133},{8,136},{9,137},{12,140},{13,141},... | collective-permute-start | bytes 786440 | tf_op jit(solution)/shard_map/ppermute | solution.py:236
  36.7 20.1 %collective-permute-start.9 = (f32[256,256]{1,0:T(8,128)S(1)}, f32[256,256]{1,0:T(8,128)S(1)}, u32[]{:S(2)}, u32[]{:S(2)}) collective-permute-start(f32[256,256]{1,0:T(8,128)S(1)} %add.53), channel_id=1, source_target_pairs={{0,192},{1,193},{4,196},{5,197},{8,200},{9,201},{12,204},{13,205},... | collective-permute-start | bytes 786440 | tf_op jit(solution)/shard_map/ppermute | solution.py:236
  37.4 19.4 %collective-permute-start.8 = (f32[256,256]{1,0:T(8,128)S(1)}, f32[256,256]{1,0:T(8,128)S(1)}, u32[]{:S(2)}, u32[]{:S(2)}) collective-permute-start(f32[256,256]{1,0:T(8,128)S(1)} %add.53), channel_id=1, source_target_pairs={{0,64},{1,65},{4,68},{5,69},{8,72},{9,73},{12,76},{13,77},{16,80},... | collective-permute-start | bytes 786440 | tf_op jit(solution)/shard_map/ppermute | solution.py:236
  56.8 9.8 %collective-permute-start.13 = (f32[256,256]{1,0:T(8,128)S(1)}, f32[256,256]{1,0:T(8,128)S(1)}, u32[]{:S(2)}, u32[]{:S(2)}) collective-permute-start(f32[256,256]{1,0:T(8,128)S(1)} %add_add_fusion), channel_id=1, source_target_pairs={{0,1},{1,2},{4,5},{5,6},{8,9},{9,10},{12,13},{13,14},{16,17},{17,1... | collective-permute-start | bytes 786440 | tf_op jit(solution)/shard_map/ppermute | solution.py:236
  62.7 6.7 %collective-permute-start.12 = (f32[256,256]{1,0:T(8,128)S(1)}, f32[256,256]{1,0:T(8,128)S(1)}, u32[]{:S(2)}, u32[]{:S(2)}) collective-permute-start(f32[256,256]{1,0:T(8,128)S(1)} %add_add_fusion), channel_id=1, source_target_pairs={{0,2},{1,3},{4,6},{5,7},{8,10},{9,11},{12,14},{13,15},{16,18},{17,... | collective-permute-start | bytes 786440 | tf_op jit(solution)/shard_map/ppermute | solution.py:236
  64.1 11.0 %collective-permute-start.11 = (f32[256,256]{1,0:T(8,128)S(1)}, f32[256,256]{1,0:T(8,128)S(1)}, u32[]{:S(2)}, u32[]{:S(2)}) collective-permute-start(f32[256,256]{1,0:T(8,128)S(1)} %add_add_fusion), channel_id=1, source_target_pairs={{0,3},{1,0},{4,7},{5,4},{8,11},{9,8},{12,15},{13,12},{16,19},{17,1... | collective-permute-start | bytes 786440 | tf_op jit(solution)/shard_map/ppermute | solution.py:236
  75.1 2.4 %collective-permute-start.14 = (f32[256,256]{1,0:T(8,128)S(1)}, f32[256,256]{1,0:T(8,128)S(1)}, u32[]{:S(2)}, u32[]{:S(2)}) collective-permute-start(f32[256,256]{1,0:T(8,128)S(1)} %get-tuple-element.50), channel_id=1, source_target_pairs={{0,32},{1,33},{2,34},{3,35},{4,36},{5,37},{6,38},{7,39},{8,40},{9,... | collective-permute-start | bytes 786440 | tf_op jit(solution)/shard_map/ppermute | solution.py:236
  76.4 1.6 %collective-permute-start.15 = (f32[256,256]{1,0:T(8,128)S(1)}, f32[256,256]{1,0:T(8,128)S(1)}, u32[]{:S(2)}, u32[]{:S(2)}) collective-permute-start(f32[256,256]{1,0:T(8,128)S(1)} %get-tuple-element.49), channel_id=1, source_target_pairs={{0,32},{1,33},{2,34},{3,35},{4,36},{5,37},{6,38},{7,39},{8,40},{9,... | collective-permute-start | bytes 786440 | tf_op jit(solution)/shard_map/ppermute | solution.py:236
  78.1 35.1 %copy-start = (s32[64,64]{1,0:T(8,128)S(1)}, s32[64,64]{1,0:T(8,128)}, u32[]{:S(2)}) copy-start(s32[64,64]{1,0:T(8,128)} %pattern.3) | copy-start | bytes 49156
  78.1 23.5 %collective-permute-start.18 = (f32[2,256,256]{2,1,0:T(8,128)S(1)}, f32[2,256,256]{2,1,0:T(8,128)S(1)}, u32[]{:S(2)}, u32[]{:S(2)}) collective-permute-start(f32[2,256,256]{2,1,0:T(8,128)S(1)} %bitcast.35), channel_id=1, source_target_pairs={{0,64},{1,65},{2,66},{3,67},{4,68},{5,69},{6,70},{7,71},{8,72},{9,... | collective-permute-start | bytes 1572872 | tf_op jit(solution)/shard_map/ppermute | solution.py:236
  78.8 32.2 %collective-permute-start.17 = (f32[2,256,256]{2,1,0:T(8,128)S(1)}, f32[2,256,256]{2,1,0:T(8,128)S(1)}, u32[]{:S(2)}, u32[]{:S(2)}) collective-permute-start(f32[2,256,256]{2,1,0:T(8,128)S(1)} %bitcast.36), channel_id=1, source_target_pairs={{0,128},{1,129},{2,130},{3,131},{4,132},{5,133},{6,134},{7,135},{8... | collective-permute-start | bytes 1572872 | tf_op jit(solution)/shard_map/ppermute | solution.py:236
  80.1 30.9 %collective-permute-start.16 = (f32[2,256,256]{2,1,0:T(8,128)S(1)}, f32[2,256,256]{2,1,0:T(8,128)S(1)}, u32[]{:S(2)}, u32[]{:S(2)}) collective-permute-start(f32[2,256,256]{2,1,0:T(8,128)S(1)} %bitcast.37), channel_id=1, source_target_pairs={{0,192},{1,193},{2,194},{3,195},{4,196},{5,197},{6,198},{7,199},{8... | collective-permute-start | bytes 1572872 | tf_op jit(solution)/shard_map/ppermute | solution.py:236
  111.1 2.0 %collective-permute-start.19 = (f32[2,256,256]{2,1,0:T(8,128)S(1)}, f32[2,256,256]{2,1,0:T(8,128)S(1)}, u32[]{:S(2)}, u32[]{:S(2)}) collective-permute-start(f32[2,256,256]{2,1,0:T(8,128)S(1)} %select_select_fusion.y0), channel_id=1, source_target_pairs={{0,32},{1,33},{2,34},{3,35},{4,36},{5,37},{6,38},{7,39},{8,40},{9,... | collective-permute-start | bytes 1572872 | tf_op jit(solution)/shard_map/ppermute | solution.py:236
Sparse Core Ops, SparseCore 0:
  35.5 61.2 all-gather.2

commit v6 on v5

--- a/solution.py
+++ b/solution.py
@@ -91,35 +91,40 @@
     return jnp.where(c <= r, whole, 0.0)
 
 
-def invert_pair(block, out):
+def invert_pair(blocks, out):
     h = HALF
-    top = invert_factor(block[:h, :h])
-    link = dot(top, block[:h, h:])
-    low = invert_factor(block[h:, h:] - dot(link.T, link))
+    top = invert_factor(blocks[0])
+    link = dot(top, blocks[1])
+    low = invert_factor(blocks[2] - dot(link.T, link))
     out[:h, :h] = top
     out[:h, h:] = jnp.zeros((h, h), jnp.float32)
     out[h:, :h] = -dot(dot(low, link.T), top)
     out[h:, h:] = low
 
 
-def pivots_kernel(a00, a01, a11, inv00, u01, inv11):
-    invert_pair(a00[...], inv00)
-    link = dot(inv00[...], a01[...])
+def pivots_kernel(even, odd, inv00, u01, inv11):
+    h = HALF
+    invert_pair([even[0, k] for k in range(3)], inv00)
+    upper = jnp.concatenate([even[1, 0], even[1, 1]], axis=1)
+    lower = jnp.concatenate([odd[0, 1].T, odd[0, 2].T], axis=1)
+    link = dot(inv00[...], jnp.concatenate([upper, lower], axis=0))
     u01[...] = link
-    invert_pair(a11[...] - dot(link.T, link), inv11)
-
-
-def factor_pivots(a00, a01, a11):
+    change = dot(link.T, link)
+    parts = (change[:h, :h], change[:h, h:], change[h:, h:])
+    invert_pair([odd[1, k] - parts[k] for k in range(3)], inv11)
+
+
+def factor_pivots(even, odd):
     shape = jax.ShapeDtypeStruct((BLK, BLK), jnp.float32)
     return pl.pallas_call(
         pivots_kernel,
         out_shape=(shape, shape, shape),
-        in_specs=[VMEM] * 3,
+        in_specs=[VMEM] * 2,
         out_specs=[VMEM] * 3,
         compiler_params=pltpu.CompilerParams(vmem_limit_bytes=32 << 20),
         cost_estimate=pl.CostEstimate(flops=25_000_000_000, bytes_accessed=1 << 20, transcendentals=0),
         name="factor_pivots",
-    )(a00, a01, a11)
+    )(even, odd)
 
 
 def columns_kernel(ids, pattern, y0, y1, inv00, u01, inv11, back0, back1, link, cols):
@@ -128,12 +133,12 @@
             out[number] = part
     q = ids[1]
     swap = ids[2] == 1
-    inverse0, inverse1, down = (split(inv00[...]), split(inv11[...]), split(u01[...].T))
+    inverse0, inverse1, down = (split(inv00[...], 2), split(inv11[...], 2), split(u01[...].T, 2))
     for c in range(2):
         w = pattern[32 * c + q, 1].astype(jnp.float32)
-        first = product(inverse0, split(jnp.where(swap, y1[c], y0[c])))
-        left = jnp.where(swap, y0[c], y1[c]) - w * product(down, split(first))
-        second = product(inverse1, split(left))
+        first = product(inverse0, split(jnp.where(swap, y1[c], y0[c]), 2), 2)
+        left = jnp.where(swap, y0[c], y1[c]) - w * product(down, split(first, 2), 2)
+        second = product(inverse1, split(left, 2), 2)
         for k, value in enumerate((first, second)):
             for number, part in enumerate(split(value, 2)):
                 cols[c, number, k * BLK : (k + 1) * BLK, :] = part
@@ -252,35 +257,34 @@
     head = matrix[0, 0, :, :, 0, :].transpose(1, 0, 2)
     quarters = head.transpose(0, 2, 1).reshape(4, HALF, BLK)
 
-    own = head[0]
-    starts = lambda b, d: d == 1 or (b == 0 and d == 0)
-    carrier = (y == 1) | ((core == 0) & (y == 0))
-    along = [shifted(own, z=k, where=lambda a, b, c, d: a == 0 and c == 0 and starts(b, d)) for k in (2, 6, 4)]
+    corner = head[0]
+    own = jnp.stack([corner[:HALF, :HALF], corner[:HALF, HALF:], corner[HALF:, HALF:]])
+    along = [shifted(own, x=k, where=lambda a, b, c, d: a == 0 and c == 0 and d < 2) for k in (1, 3, 2)]
     parts = []
     for m in range(4):
         pairs = [(32 * c + s, (s % 8) * 32 + 8 * (s // 8) + 4 * c + m) for c in range(2) for s in range(32)]
         parts.append(lax.ppermute(quarters[m], AXES, pairs))
-    pivot = jnp.where((x == 0) & (z == 0) & carrier, own, 0.0) + along[0] + along[1] + along[2]
-    pivot = pivot + shifted(pivot, z=1, where=lambda a, b, c, d: a == 0 and c % 2 == 0 and starts(b, d))
+    pivot = jnp.where((x == 0) & (z == 0) & (y < 2), own, 0.0) + along[0] + along[1] + along[2]
+    along = [shifted(pivot, z=k, where=lambda a, b, c, d: c == 0 and d < 2) for k in (2, 6, 4)]
+    pivot = pivot + along[0] + along[1] + along[2]
     mine = parts[0] + parts[1] + parts[2] + parts[3]
     mine, pivot = tie(mine, pivot)
 
+    g = jnp.stack([mine] + [shifted(mine, y=k) for k in (1, 2, 3)])
+    pivot = pivot + shifted(pivot, z=1, where=lambda a, b, c, d: c % 2 == 0 and d < 2)
+    g, pivot = tie(g, pivot)
+
     groups = [[NY * b + a for b in range(NZ)] for a in range(NY)]
-    g = jnp.stack([mine] + [shifted(mine, y=k) for k in (1, 2, 3)])
     g = lax.all_gather(g, "col", axis=0, axis_index_groups=groups)
-    along = [shifted(pivot, x=k, where=lambda a, b, c, d: a == 0 and starts(b, d)) for k in (1, 3, 2)]
-    pivot = pivot + along[0] + along[1] + along[2]
-    got = [pivot] + [shifted(pivot, y=k, where=lambda a, b, c, d: starts(b, d)) for k in (1, 2, 3)]
-    first = pick(y, got)
-    rest = pick((y + 3) % 4, got)
-    swapped = shifted(rest, core=1)
-    a00 = jnp.where(core == 0, first, shifted(first, core=1, where=lambda a, b, *_: b == 0))
-    a01 = jnp.where(core == 0, rest, swapped)
-    a11 = jnp.where(core == 0, swapped, rest)
-    a00, a01, a11, head = tie(a00, a01, a11, head)
+    got = [pivot] + [shifted(pivot, y=k, where=lambda a, b, c, d: d < 2) for k in (1, 2, 3)]
+    both = jnp.stack([pick(y, got), pick((y + 3) % 4, got)])
+    swapped = shifted(both, core=1)
+    even = jnp.where(core == 0, both, swapped)
+    odd = jnp.where(core == 0, swapped, both)
+    even, odd, head = tie(even, odd, head)
 
     cols = [head] + [shifted(head, x=k, where=lambda a, *_: a == 0) for k in (1, 2, 3)]
-    inv00, u01, inv11 = factor_pivots(a00, a01, a11)
+    inv00, u01, inv11 = factor_pivots(even, odd)
     inv00, u01, inv11, cols[0] = tie(inv00, u01, inv11, cols[0])
     cols = pick(x, cols)
     other = shifted(cols, core=1)

time: 137 us -> 122 us (0.89); the launches traced: 137 us -> 120 us
  waiting for transfers between devices: 57.1 us -> 46 us
  starting transfers between devices: 25.1 us -> 20 us
    ppermute x19 -> x18, waiting for transfers between devices: 47 us -> 31 us  [shifted(): return lax.ppermute(value, AXES, pairs)]
    all_gather x1, waiting for transfers between devices: 0.02 us -> 6.25 us  [per_device(): g = lax.all_gather(g, 'col', axis=0, axis_index_groups=groups)]
    ppermute x19 -> x18, starting transfers between devices: 21.8 us -> 16.7 us  [shifted(): return lax.ppermute(value, AXES, pairs)]
  transfers between devices with their start and end apart: 24 -> 23, of which waited for: 12 -> 12; matrix products, arithmetic and copies ran while one was open for 1% -> 1% of each run, Pallas kernels for 18% -> 19%
where the time goes in v6:
time: 122 us; the launch traced here: 120 us
  waiting for transfers between devices  46 us (38%)
  Pallas kernels  36.3 us (30%)
  starting transfers between devices  20 us (16%)
  between operations  13.8 us (11%)
  local copies, waits for them, and re-layouts  2.01 us (2%)
  other arithmetic  1.36 us (1%)
    ppermute x18, waiting for transfers between devices, shifted(): return lax.ppermute(value, AXES, pairs)  31 us
    pallas_call x1, Pallas kernels, factor_pivots(): pl.pallas_call(pivots_kernel, out_shape=(shape, shape, shape), in_specs=[...  20.5 us
    ppermute x18, starting transfers between devices, shifted(): return lax.ppermute(value, AXES, pairs)  16.7 us
    pallas_call x1, Pallas kernels, update(): pl.pallas_call(update_kernel, out_shape=jax.ShapeDtypeStruct(local.shape,...  13.2 us
    ppermute x4, waiting for transfers between devices, per_device(): parts.append(lax.ppermute(quarters[m], AXES, pairs))  8.7 us
    all_gather x1, waiting for transfers between devices, per_device(): g = lax.all_gather(g, 'col', axis=0, axis_index_groups=groups)  6.25 us
    ppermute x4, starting transfers between devices, per_device(): parts.append(lax.ppermute(quarters[m], AXES, pairs))  3.3 us
    pallas_call x1, Pallas kernels, solve_columns(): pl.pallas_call(columns_kernel, out_shape=(parts, parts, parts, jax.ShapeD...  2.66 us
  transfers between devices with their start and end apart: 23, of which 12 were waited for; matrix products, arithmetic and copies ran while one was open for 1% of the time, Pallas kernels for 19%

profile of v6, /device:TPU:36, one launch (start us, length us, event | category | flops | bytes accessed | tf_op | source)
XLA Modules:
  0.0 119.6 jit_solution(2603772931783598759)
XLA Ops:
  6.5 0.0 all-gather.3.cloned.1.call-start
  6.5 1.4 %slice.27 = f32[1,1,256,2,1,256]{5,4,3,2,1,0:T(1,128)S(1)} slice(f32[8,1,256,2,1,256]{5,4,3,2,1,0:T(1,128)} %param.2), slice={[0:1], [0:1], [0:256], [0:2], [0:1], [0:256]} | slice | bytes 1048576 | tf_op jit(solution)/shard_map/slice | solution.py:257
  8.1 0.7 collective-permute-start.5
  8.7 0.7 collective-permute-start.4
  9.4 0.7 collective-permute-start.6
  10.1 0.5 copy.12
  10.6 0.7 collective-permute-start.1
  11.3 0.7 collective-permute-start.3
  12.0 0.0 collective-permute-done.5
  12.1 0.7 collective-permute-start.2
  12.7 0.0 collective-permute-done.4
  12.7 1.3 %collective-permute-start = (f32[128,256]{1,0:T(8,128)S(1)}, f32[128,256]{1,0:T(8,128)S(1)}, u32[]{:S(2)}, u32[]{:S(2)}) collective-permute-start(f32[128,256]{1,0:T(8,128)S(1)} %get-tuple-element.58), channel_id=1, source_target_pairs={{0,0},{1,32},{2,64},{3,96},{4,128},{5,160},{6,192},{7,224},{8,8},{... | collective-permute-start | bytes 393224 | tf_op jit(solution)/shard_map/ppermute | solution.py:266
  14.0 0.0 collective-permute-done.6
  14.1 0.7 collective-permute-start.9
  14.8 0.0 collective-permute-done.1
  14.8 0.7 collective-permute-start.8
  15.5 0.0 collective-permute-done.3
  15.5 0.7 collective-permute-start.7
  16.2 0.0 collective-permute-done.2
  16.2 8.7 %collective-permute-done = f32[128,256]{1,0:T(8,128)S(1)} collective-permute-done((f32[128,256]{1,0:T(8,128)S(1)}, f32[128,256]{1,0:T(8,128)S(1)}, u32[]{:S(2)}, u32[]{:S(2)}) %collective-permute-start) | collective-permute-done | bytes 131104 | tf_op jit(solution)/shard_map/ppermute | solution.py:266
  24.9 0.0 collective-permute-done.9
  24.9 0.0 collective-permute-done.8
  24.9 0.0 collective-permute-done.7
  24.9 0.1 add_add_fusion
  25.0 1.3 %collective-permute-start.12 = (f32[128,256]{1,0:T(8,128)S(1)}, f32[128,256]{1,0:T(8,128)S(1)}, u32[]{:S(2)}, u32[]{:S(2)}) collective-permute-start(f32[128,256]{1,0:T(8,128)S(1)} %add_add_fusion.2), channel_id=1, source_target_pairs={{0,3},{1,0},{2,1},{3,2},{4,7},{5,4},{6,5},{7,6},{8,11},{9,8},{10,9... | collective-permute-start | bytes 393224 | tf_op jit(solution)/shard_map/ppermute | solution.py:241
  26.3 0.4 collective-permute-start.11
  26.6 1.3 %collective-permute-start.10 = (f32[128,256]{1,0:T(8,128)S(1)}, f32[128,256]{1,0:T(8,128)S(1)}, u32[]{:S(2)}, u32[]{:S(2)}) collective-permute-start(f32[128,256]{1,0:T(8,128)S(1)} %add_add_fusion.2), channel_id=1, source_target_pairs={{0,1},{1,2},{2,3},{3,0},{4,5},{5,6},{6,7},{7,4},{8,9},{9,10},{10,1... | collective-permute-start | bytes 393224 | tf_op jit(solution)/shard_map/ppermute | solution.py:241
  28.0 1.3 %collective-permute-start.13 = (f32[3,128,128]{2,1,0:T(8,128)S(1)}, f32[3,128,128]{2,1,0:T(8,128)S(1)}, u32[]{:S(2)}, u32[]{:S(2)}) collective-permute-start(f32[3,128,128]{2,1,0:T(8,128)S(1)} %add_add_fusion), channel_id=1, source_target_pairs={{0,4},{1,5},{8,12},{9,13},{16,20},{17,21},{24,28},{25,29},{32,36},... | collective-permute-start | bytes 589832 | tf_op jit(solution)/shard_map/ppermute | solution.py:241
  29.3 1.7 %collective-permute-done.12 = f32[128,256]{1,0:T(8,128)S(1)} collective-permute-done((f32[128,256]{1,0:T(8,128)S(1)}, f32[128,256]{1,0:T(8,128)S(1)}, u32[]{:S(2)}, u32[]{:S(2)}) %collective-permute-start.12) | collective-permute-done | bytes 131104 | tf_op jit(solution)/shard_map/ppermute | solution.py:241
  30.9 3.0 %collective-permute-done.11 = f32[128,256]{1,0:T(8,128)S(1)} collective-permute-done((f32[128,256]{1,0:T(8,128)S(1)}, f32[128,256]{1,0:T(8,128)S(1)}, u32[]{:S(2)}, u32[]{:S(2)}) %collective-permute-start.11) | collective-permute-done | bytes 131104 | tf_op jit(solution)/shard_map/ppermute | solution.py:241
  33.9 1.0 collective-permute-done.10
  35.0 0.8 pad_maximum_fusion
  35.8 11.1 %collective-permute-done.13 = f32[3,128,128]{2,1,0:T(8,128)S(1)} collective-permute-done((f32[3,128,128]{2,1,0:T(8,128)S(1)}, f32[3,128,128]{2,1,0:T(8,128)S(1)}, u32[]{:S(2)}, u32[]{:S(2)}) %collective-permute-start.13) | collective-permute-done | bytes 196640 | tf_op jit(solution)/shard_map/ppermute | solution.py:241
  46.9 0.0 all-gather.3.cloned.1.call-update
  46.9 2.2 %collective-permute-start.16 = (f32[3,128,128]{2,1,0:T(8,128)S(1)}, f32[3,128,128]{2,1,0:T(8,128)S(1)}, u32[]{:S(2)}, u32[]{:S(2)}) collective-permute-start(f32[3,128,128]{2,1,0:T(8,128)S(1)} %add.56), channel_id=1, source_target_pairs={{0,1},{1,2},{4,5},{5,6},{8,9},{9,10},{12,13},{13,14},{16,17},{17,1... | collective-permute-start | bytes 589832 | tf_op jit(solution)/shard_map/ppermute | solution.py:241
  49.1 1.3 %collective-permute-start.15 = (f32[3,128,128]{2,1,0:T(8,128)S(1)}, f32[3,128,128]{2,1,0:T(8,128)S(1)}, u32[]{:S(2)}, u32[]{:S(2)}) collective-permute-start(f32[3,128,128]{2,1,0:T(8,128)S(1)} %add.56), channel_id=1, source_target_pairs={{0,2},{1,3},{4,6},{5,7},{8,10},{9,11},{12,14},{13,15},{16,18},{17,... | collective-permute-start | bytes 589832 | tf_op jit(solution)/shard_map/ppermute | solution.py:241
  50.4 1.9 %collective-permute-start.14 = (f32[3,128,128]{2,1,0:T(8,128)S(1)}, f32[3,128,128]{2,1,0:T(8,128)S(1)}, u32[]{:S(2)}, u32[]{:S(2)}) collective-permute-start(f32[3,128,128]{2,1,0:T(8,128)S(1)} %add.56), channel_id=1, source_target_pairs={{0,3},{1,0},{4,7},{5,4},{8,11},{9,8},{12,15},{13,12},{16,19},{17,1... | collective-permute-start | bytes 589832 | tf_op jit(solution)/shard_map/ppermute | solution.py:241
  52.4 0.2 collective-permute-done.16
  52.6 2.1 %collective-permute-done.15 = f32[3,128,128]{2,1,0:T(8,128)S(1)} collective-permute-done((f32[3,128,128]{2,1,0:T(8,128)S(1)}, f32[3,128,128]{2,1,0:T(8,128)S(1)}, u32[]{:S(2)}, u32[]{:S(2)}) %collective-permute-start.15) | collective-permute-done | bytes 196640 | tf_op jit(solution)/shard_map/ppermute | solution.py:241
  54.7 3.3 %collective-permute-done.14 = f32[3,128,128]{2,1,0:T(8,128)S(1)} collective-permute-done((f32[3,128,128]{2,1,0:T(8,128)S(1)}, f32[3,128,128]{2,1,0:T(8,128)S(1)}, u32[]{:S(2)}, u32[]{:S(2)}) %collective-permute-start.14) | collective-permute-done | bytes 196640 | tf_op jit(solution)/shard_map/ppermute | solution.py:241
  58.1 0.1 collective-permute-start.17
  58.3 1.7 %collective-permute-done.17 = f32[2,3,128,128]{3,2,1,0:T(8,128)S(1)} collective-permute-done((f32[2,3,128,128]{3,2,1,0:T(8,128)S(1)}, f32[2,3,128,128]{3,2,1,0:T(8,128)S(1)}, u32[]{:S(2)}, u32[]{:S(2)}) %collective-permute-start.17) | collective-permute-done | bytes 393248 | tf_op jit(solution)/shard_map/ppermute | solution.py:241
  60.0 0.1 broadcast_select_fusion
  60.0 0.0 copy-start
  60.0 0.7 collective-permute-start.20
  60.7 1.3 %collective-permute-start.19 = (f32[2,256,256]{2,1,0:T(8,128)S(1)}, f32[2,256,256]{2,1,0:T(8,128)S(1)}, u32[]{:S(2)}, u32[]{:S(2)}) collective-permute-start(f32[2,256,256]{2,1,0:T(8,128)S(1)} %bitcast.43), channel_id=1, source_target_pairs={{0,128},{1,129},{2,130},{3,131},{4,132},{5,133},{6,134},{7,135},{8... | collective-permute-start | bytes 1572872 | tf_op jit(solution)/shard_map/ppermute | solution.py:241
  62.0 0.9 collective-permute-start.18
  62.9 20.5 %factor_pivots.1 = (f32[256,256]{1,0:T(8,128)S(1)}, f32[256,256]{1,0:T(8,128)S(1)}, f32[256,256]{1,0:T(8,128)S(1)}) custom-call(f32[2,3,128,128]{3,2,1,0:T(8,128)S(1)} %get-tuple-element.32.even, f32[2,3,128,128]{3,2,1,0:T(8,128)S(1)} %get-tuple-element.33.odd), custom_call_target="tpu_custom_call" | custom-call | flops 24999999488 | bytes 1048576 | tf_op jit(solution)/shard_map/factor_pivots/pallas_call | solution.py:119
  83.4 0.0 collective-permute-done.20
  83.5 5.1 %collective-permute-done.19 = f32[2,256,256]{2,1,0:T(8,128)S(1)} collective-permute-done((f32[2,256,256]{2,1,0:T(8,128)S(1)}, f32[2,256,256]{2,1,0:T(8,128)S(1)}, u32[]{:S(2)}, u32[]{:S(2)}) %collective-permute-start.19) | collective-permute-done | bytes 524320 | tf_op jit(solution)/shard_map/ppermute | solution.py:241
  88.5 0.0 collective-permute-done.18
  88.5 0.1 select_select_fusion.y0
  88.7 0.1 collective-permute-start.21
  88.8 0.1 pad_add_fusion.ids
  88.8 1.8 %collective-permute-done.21.y1 = f32[2,256,256]{2,1,0:T(8,128)S(1)} collective-permute-done((f32[2,256,256]{2,1,0:T(8,128)S(1)}, f32[2,256,256]{2,1,0:T(8,128)S(1)}, u32[]{:S(2)}, u32[]{:S(2)}) %collective-permute-start.21) | collective-permute-done | bytes 524320 | tf_op jit(solution)/shard_map/ppermute | solution.py:241
  90.7 0.0 copy-done
  90.7 2.7 %solve_columns.1 = (bf16[2,256,256]{2,1,0:T(8,128)(2,1)S(1)}, bf16[2,256,256]{2,1,0:T(8,128)(2,1)S(1)}, bf16[2,256,256]{2,1,0:T(8,128)(2,1)S(1)}, bf16[2,2,512,256]{3,2,1,0:T(8,128)(2,1)S(1)}) custom-call(s32[4]{0:T(128)S(1)} %pad_add_fusion.ids, s32[64,64]{1,0:T(8,128)S(1)} %copy-done, f32[2,256,256]{2,1,0:T(8,128)S(1)} %select_select_fusion.y0, ...), custom_call_target="tpu_custom_call" | custom-call | flops 3000000000 | bytes 4194304 | tf_op jit(solution)/shard_map/solve_columns/pallas_call | solution.py:150
  93.3 6.2 %all-gather.3.cloned.1.call-done = f32[32,128,256]{2,1,0:T(8,128)} async-done(((f32[4,128,256]{2,1,0:T(8,128)}), f32[32,128,256]{2,1,0:T(8,128)}) %all-gather.3.cloned.1.call-update) | async-done | bytes 4194320 | tf_op jit(solution)/shard_map/all_gather | solution.py:278
  99.6 13.2 %update.1 = f32[2,4,1024,128]{3,2,1,0:T(8,128)} custom-call(s32[4]{0:T(128)S(1)} %pad_add_fusion.ids, s32[64,64]{1,0:T(8,128)S(1)} %copy-done, f32[2,4,1024,128]{3,2,1,0:T(8,128)} %bitcast.51, f32[8,4,128,256]{3,2,1,0:T(8,128)} %bitcast.52, bf16[2,256,256]{2,1,0:T(8,128)(2,1)S(1)} %get-tuple-element.47.back0, ...), custom_call_target="tpu_custom_call" | custom-call | flops 12000000000 | bytes 14680064 | tf_op jit(solution)/shard_map/update/pallas_call | solution.py:214
  (10 shorter events, 0.3 us)
Async XLA Ops:
  6.5 93.0 %all-gather.3.cloned.1.call-start = ((), (), s32[]{:S(2)}) async-start(), calls=%async_computation | async-start | bytes 4718592 | tf_op jit(solution)/shard_map/all_gather | solution.py:278
  8.1 4.0 %collective-permute-start.5 = (f32[3,128,128]{2,1,0:T(8,128)S(1)}, f32[3,128,128]{2,1,0:T(8,128)S(1)}, u32[]{:S(2)}, u32[]{:S(2)}) collective-permute-start(f32[3,128,128]{2,1,0:T(8,128)S(1)} %pad_maximum_fusion.2), channel_id=1, source_target_pairs={{0,192},{1,193},{32,224},{33,225}} | collective-permute-start | bytes 589832 | tf_op jit(solution)/shard_map/ppermute | solution.py:241
  8.7 4.0 %collective-permute-start.4 = (f32[3,128,128]{2,1,0:T(8,128)S(1)}, f32[3,128,128]{2,1,0:T(8,128)S(1)}, u32[]{:S(2)}, u32[]{:S(2)}) collective-permute-start(f32[3,128,128]{2,1,0:T(8,128)S(1)} %pad_maximum_fusion.2), channel_id=1, source_target_pairs={{0,64},{1,65},{32,96},{33,97}} | collective-permute-start | bytes 589832 | tf_op jit(solution)/shard_map/ppermute | solution.py:241
  9.4 4.6 %collective-permute-start.6 = (f32[3,128,128]{2,1,0:T(8,128)S(1)}, f32[3,128,128]{2,1,0:T(8,128)S(1)}, u32[]{:S(2)}, u32[]{:S(2)}) collective-permute-start(f32[3,128,128]{2,1,0:T(8,128)S(1)} %pad_maximum_fusion.2), channel_id=1, source_target_pairs={{0,128},{1,129},{32,160},{33,161}} | collective-permute-start | bytes 589832 | tf_op jit(solution)/shard_map/ppermute | solution.py:241
  10.6 4.1 %collective-permute-start.1 = (f32[128,256]{1,0:T(8,128)S(1)}, f32[128,256]{1,0:T(8,128)S(1)}, u32[]{:S(2)}, u32[]{:S(2)}) collective-permute-start(f32[128,256]{1,0:T(8,128)S(1)} %get-tuple-element.55), channel_id=1, source_target_pairs={{0,1},{1,33},{2,65},{3,97},{4,129},{5,161},{6,193},{7,225},{8,9},{... | collective-permute-start | bytes 393224 | tf_op jit(solution)/shard_map/ppermute | solution.py:266
  11.3 4.2 %collective-permute-start.3 = (f32[128,256]{1,0:T(8,128)S(1)}, f32[128,256]{1,0:T(8,128)S(1)}, u32[]{:S(2)}, u32[]{:S(2)}) collective-permute-start(f32[128,256]{1,0:T(8,128)S(1)} %get-tuple-element.56), channel_id=1, source_target_pairs={{0,3},{1,35},{2,67},{3,99},{4,131},{5,163},{6,195},{7,227},{8,11},... | collective-permute-start | bytes 393224 | tf_op jit(solution)/shard_map/ppermute | solution.py:266
  12.1 4.1 %collective-permute-start.2 = (f32[128,256]{1,0:T(8,128)S(1)}, f32[128,256]{1,0:T(8,128)S(1)}, u32[]{:S(2)}, u32[]{:S(2)}) collective-permute-start(f32[128,256]{1,0:T(8,128)S(1)} %get-tuple-element.57), channel_id=1, source_target_pairs={{0,2},{1,34},{2,66},{3,98},{4,130},{5,162},{6,194},{7,226},{8,10},... | collective-permute-start | bytes 393224 | tf_op jit(solution)/shard_map/ppermute | solution.py:266
  12.7 12.1 %collective-permute-start = (f32[128,256]{1,0:T(8,128)S(1)}, f32[128,256]{1,0:T(8,128)S(1)}, u32[]{:S(2)}, u32[]{:S(2)}) collective-permute-start(f32[128,256]{1,0:T(8,128)S(1)} %get-tuple-element.58), channel_id=1, source_target_pairs={{0,0},{1,32},{2,64},{3,96},{4,128},{5,160},{6,192},{7,224},{8,8},{... | collective-permute-start | bytes 393224 | tf_op jit(solution)/shard_map/ppermute | solution.py:266
  14.1 10.8 %collective-permute-start.9 = (f32[3,128,128]{2,1,0:T(8,128)S(1)}, f32[3,128,128]{2,1,0:T(8,128)S(1)}, u32[]{:S(2)}, u32[]{:S(2)}) collective-permute-start(f32[3,128,128]{2,1,0:T(8,128)S(1)} %add_add_fusion.1), channel_id=1, source_target_pairs={{0,16},{1,17},{32,48},{33,49},{64,80},{65,81},{96,112},{97,113},{1... | collective-permute-start | bytes 589832 | tf_op jit(solution)/shard_map/ppermute | solution.py:241
  14.8 10.1 %collective-permute-start.8 = (f32[3,128,128]{2,1,0:T(8,128)S(1)}, f32[3,128,128]{2,1,0:T(8,128)S(1)}, u32[]{:S(2)}, u32[]{:S(2)}) collective-permute-start(f32[3,128,128]{2,1,0:T(8,128)S(1)} %add_add_fusion.1), channel_id=1, source_target_pairs={{0,24},{1,25},{32,56},{33,57},{64,88},{65,89},{96,120},{97,121},{1... | collective-permute-start | bytes 589832 | tf_op jit(solution)/shard_map/ppermute | solution.py:241
  15.5 9.4 %collective-permute-start.7 = (f32[3,128,128]{2,1,0:T(8,128)S(1)}, f32[3,128,128]{2,1,0:T(8,128)S(1)}, u32[]{:S(2)}, u32[]{:S(2)}) collective-permute-start(f32[3,128,128]{2,1,0:T(8,128)S(1)} %add_add_fusion.1), channel_id=1, source_target_pairs={{0,8},{1,9},{32,40},{33,41},{64,72},{65,73},{96,104},{97,105},{128... | collective-permute-start | bytes 589832 | tf_op jit(solution)/shard_map/ppermute | solution.py:241
  25.0 5.9 %collective-permute-start.12 = (f32[128,256]{1,0:T(8,128)S(1)}, f32[128,256]{1,0:T(8,128)S(1)}, u32[]{:S(2)}, u32[]{:S(2)}) collective-permute-start(f32[128,256]{1,0:T(8,128)S(1)} %add_add_fusion.2), channel_id=1, source_target_pairs={{0,3},{1,0},{2,1},{3,2},{4,7},{5,4},{6,5},{7,6},{8,11},{9,8},{10,9... | collective-permute-start | bytes 393224 | tf_op jit(solution)/shard_map/ppermute | solution.py:241
  26.3 7.7 %collective-permute-start.11 = (f32[128,256]{1,0:T(8,128)S(1)}, f32[128,256]{1,0:T(8,128)S(1)}, u32[]{:S(2)}, u32[]{:S(2)}) collective-permute-start(f32[128,256]{1,0:T(8,128)S(1)} %add_add_fusion.2), channel_id=1, source_target_pairs={{0,2},{1,3},{2,0},{3,1},{4,6},{5,7},{6,4},{7,5},{8,10},{9,11},{10,... | collective-permute-start | bytes 393224 | tf_op jit(solution)/shard_map/ppermute | solution.py:241
  26.6 8.3 %collective-permute-start.10 = (f32[128,256]{1,0:T(8,128)S(1)}, f32[128,256]{1,0:T(8,128)S(1)}, u32[]{:S(2)}, u32[]{:S(2)}) collective-permute-start(f32[128,256]{1,0:T(8,128)S(1)} %add_add_fusion.2), channel_id=1, source_target_pairs={{0,1},{1,2},{2,3},{3,0},{4,5},{5,6},{6,7},{7,4},{8,9},{9,10},{10,1... | collective-permute-start | bytes 393224 | tf_op jit(solution)/shard_map/ppermute | solution.py:241
  28.0 18.9 %collective-permute-start.13 = (f32[3,128,128]{2,1,0:T(8,128)S(1)}, f32[3,128,128]{2,1,0:T(8,128)S(1)}, u32[]{:S(2)}, u32[]{:S(2)}) collective-permute-start(f32[3,128,128]{2,1,0:T(8,128)S(1)} %add_add_fusion), channel_id=1, source_target_pairs={{0,4},{1,5},{8,12},{9,13},{16,20},{17,21},{24,28},{25,29},{32,36},... | collective-permute-start | bytes 589832 | tf_op jit(solution)/shard_map/ppermute | solution.py:241
  46.9 5.7 %collective-permute-start.16 = (f32[3,128,128]{2,1,0:T(8,128)S(1)}, f32[3,128,128]{2,1,0:T(8,128)S(1)}, u32[]{:S(2)}, u32[]{:S(2)}) collective-permute-start(f32[3,128,128]{2,1,0:T(8,128)S(1)} %add.56), channel_id=1, source_target_pairs={{0,1},{1,2},{4,5},{5,6},{8,9},{9,10},{12,13},{13,14},{16,17},{17,1... | collective-permute-start | bytes 589832 | tf_op jit(solution)/shard_map/ppermute | solution.py:241
  49.1 5.6 %collective-permute-start.15 = (f32[3,128,128]{2,1,0:T(8,128)S(1)}, f32[3,128,128]{2,1,0:T(8,128)S(1)}, u32[]{:S(2)}, u32[]{:S(2)}) collective-permute-start(f32[3,128,128]{2,1,0:T(8,128)S(1)} %add.56), channel_id=1, source_target_pairs={{0,2},{1,3},{4,6},{5,7},{8,10},{9,11},{12,14},{13,15},{16,18},{17,... | collective-permute-start | bytes 589832 | tf_op jit(solution)/shard_map/ppermute | solution.py:241
  50.4 7.6 %collective-permute-start.14 = (f32[3,128,128]{2,1,0:T(8,128)S(1)}, f32[3,128,128]{2,1,0:T(8,128)S(1)}, u32[]{:S(2)}, u32[]{:S(2)}) collective-permute-start(f32[3,128,128]{2,1,0:T(8,128)S(1)} %add.56), channel_id=1, source_target_pairs={{0,3},{1,0},{4,7},{5,4},{8,11},{9,8},{12,15},{13,12},{16,19},{17,1... | collective-permute-start | bytes 589832 | tf_op jit(solution)/shard_map/ppermute | solution.py:241
  58.1 1.8 %collective-permute-start.17 = (f32[2,3,128,128]{3,2,1,0:T(8,128)S(1)}, f32[2,3,128,128]{3,2,1,0:T(8,128)S(1)}, u32[]{:S(2)}, u32[]{:S(2)}) collective-permute-start(f32[2,3,128,128]{3,2,1,0:T(8,128)S(1)} %pad_maximum_fusion.1), channel_id=1, source_target_pairs={{0,32},{1,33},{2,34},{3,35},{4,36},{5,37},{6,38},{7,39},{8,40},{9,... | collective-permute-start | bytes 1179656 | tf_op jit(solution)/shard_map/ppermute | solution.py:241
  60.0 30.6 %copy-start = (s32[64,64]{1,0:T(8,128)S(1)}, s32[64,64]{1,0:T(8,128)}, u32[]{:S(2)}) copy-start(s32[64,64]{1,0:T(8,128)} %pattern.3) | copy-start | bytes 49156
  60.0 23.4 %collective-permute-start.20 = (f32[2,256,256]{2,1,0:T(8,128)S(1)}, f32[2,256,256]{2,1,0:T(8,128)S(1)}, u32[]{:S(2)}, u32[]{:S(2)}) collective-permute-start(f32[2,256,256]{2,1,0:T(8,128)S(1)} %bitcast.42), channel_id=1, source_target_pairs={{0,64},{1,65},{2,66},{3,67},{4,68},{5,69},{6,70},{7,71},{8,72},{9,... | collective-permute-start | bytes 1572872 | tf_op jit(solution)/shard_map/ppermute | solution.py:241
  60.7 27.8 %collective-permute-start.19 = (f32[2,256,256]{2,1,0:T(8,128)S(1)}, f32[2,256,256]{2,1,0:T(8,128)S(1)}, u32[]{:S(2)}, u32[]{:S(2)}) collective-permute-start(f32[2,256,256]{2,1,0:T(8,128)S(1)} %bitcast.43), channel_id=1, source_target_pairs={{0,128},{1,129},{2,130},{3,131},{4,132},{5,133},{6,134},{7,135},{8... | collective-permute-start | bytes 1572872 | tf_op jit(solution)/shard_map/ppermute | solution.py:241
  62.0 26.5 %collective-permute-start.18 = (f32[2,256,256]{2,1,0:T(8,128)S(1)}, f32[2,256,256]{2,1,0:T(8,128)S(1)}, u32[]{:S(2)}, u32[]{:S(2)}) collective-permute-start(f32[2,256,256]{2,1,0:T(8,128)S(1)} %bitcast.44), channel_id=1, source_target_pairs={{0,192},{1,193},{2,194},{3,195},{4,196},{5,197},{6,198},{7,199},{8... | collective-permute-start | bytes 1572872 | tf_op jit(solution)/shard_map/ppermute | solution.py:241
  88.7 2.0 %collective-permute-start.21 = (f32[2,256,256]{2,1,0:T(8,128)S(1)}, f32[2,256,256]{2,1,0:T(8,128)S(1)}, u32[]{:S(2)}, u32[]{:S(2)}) collective-permute-start(f32[2,256,256]{2,1,0:T(8,128)S(1)} %select_select_fusion.y0), channel_id=1, source_target_pairs={{0,32},{1,33},{2,34},{3,35},{4,36},{5,37},{6,38},{7,39},{8,40},{9,... | collective-permute-start | bytes 1572872 | tf_op jit(solution)/shard_map/ppermute | solution.py:241
Sparse Core Ops, SparseCore 0:
  47.1 52.4 all-gather.2

commit v7 on v6

--- a/solution.py
+++ b/solution.py
@@ -209,7 +209,6 @@
 
 
 def update(ids, pattern, local, g, back0, back1, link, cols):
-    whole = lambda *shape: pl.BlockSpec(shape, lambda j, *_: (0,) * len(shape))
     block = pl.BlockSpec((2, 1, 4 * BLK, HALF), lambda j, *_: (0, j, 0, 0))
     return pl.pallas_call(
         update_kernel,
@@ -220,8 +219,7 @@
             in_specs=[
                 block,
                 pl.BlockSpec((2, 4, HALF, BLK), lambda j, *_: (j, 0, 0, 0)),
-                *[whole(2, BLK, BLK)] * 3,
-                whole(2, 2, 2 * BLK, BLK),
+                *[VMEM] * 4,
             ],
             out_specs=block,
         ),
@@ -270,9 +268,9 @@
     mine = parts[0] + parts[1] + parts[2] + parts[3]
     mine, pivot = tie(mine, pivot)
 
-    g = jnp.stack([mine] + [shifted(mine, y=k) for k in (1, 2, 3)])
     pivot = pivot + shifted(pivot, z=1, where=lambda a, b, c, d: c % 2 == 0 and d < 2)
-    g, pivot = tie(g, pivot)
+    turns = [shifted(mine, y=k) for k in (1, 2, 3)]
+    g = jnp.stack([mine] + turns)
 
     groups = [[NY * b + a for b in range(NZ)] for a in range(NY)]
     g = lax.all_gather(g, "col", axis=0, axis_index_groups=groups)

time: 122 us -> 122 us (level)
    ppermute x18, waiting for transfers between devices: 31 us -> 37.5 us  [shifted(): return lax.ppermute(value, AXES, pairs)]
    all_gather x1, waiting for transfers between devices: 6.25 us -> 0.02 us  [per_device(): g = lax.all_gather(g, 'col', axis=0, axis_index_groups=groups)]
  transfers between devices with their start and end apart: 23 -> 23, of which waited for: 12 -> 10; matrix products, arithmetic and copies ran while one was open for 1% -> 1% of each run, Pallas kernels for 19% -> 19%
where the time goes in v7:
time: 122 us; the launch traced here: 120 us
  waiting for transfers between devices  46.2 us (38%)
  Pallas kernels  36.3 us (30%)
  starting transfers between devices  20.1 us (16%)
  between operations  13.8 us (11%)
  local copies, waits for them, and re-layouts  2.01 us (2%)
  other arithmetic  1.36 us (1%)
    ppermute x18, waiting for transfers between devices, shifted(): return lax.ppermute(value, AXES, pairs)  37.5 us
    pallas_call x1, Pallas kernels, factor_pivots(): pl.pallas_call(pivots_kernel, out_shape=(shape, shape, shape), in_specs=[...  20.5 us
    ppermute x18, starting transfers between devices, shifted(): return lax.ppermute(value, AXES, pairs)  16.8 us
    pallas_call x1, Pallas kernels, update(): pl.pallas_call(update_kernel, out_shape=jax.ShapeDtypeStruct(local.shape,...  13.2 us
    ppermute x4, waiting for transfers between devices, per_device(): parts.append(lax.ppermute(quarters[m], AXES, pairs))  8.7 us
    ppermute x4, starting transfers between devices, per_device(): parts.append(lax.ppermute(quarters[m], AXES, pairs))  3.3 us
    pallas_call x1, Pallas kernels, solve_columns(): pl.pallas_call(columns_kernel, out_shape=(parts, parts, parts, jax.ShapeD...  2.66 us
  transfers between devices with their start and end apart: 23, of which 10 were waited for; matrix products, arithmetic and copies ran while one was open for 1% of the time, Pallas kernels for 19%

profile of v7, /device:TPU:36, one launch (start us, length us, event | category | flops | bytes accessed | tf_op | source)
XLA Modules:
  0.0 119.9 jit_solution(6490256999227719329)
XLA Ops:
  6.5 0.0 all-gather.3.cloned.1.call-start
  6.5 1.4 %slice.27 = f32[1,1,256,2,1,256]{5,4,3,2,1,0:T(1,128)S(1)} slice(f32[8,1,256,2,1,256]{5,4,3,2,1,0:T(1,128)} %param.2), slice={[0:1], [0:1], [0:256], [0:2], [0:1], [0:256]} | slice | bytes 1048576 | tf_op jit(solution)/shard_map/slice | solution.py:255
  8.1 0.7 collective-permute-start.5
  8.7 0.7 collective-permute-start.4
  9.4 0.7 collective-permute-start.6
  10.1 0.5 copy.12
  10.6 0.7 collective-permute-start.1
  11.3 0.7 collective-permute-start.3
  12.0 0.0 collective-permute-done.5
  12.1 0.7 collective-permute-start.2
  12.7 0.0 collective-permute-done.4
  12.7 1.3 %collective-permute-start = (f32[128,256]{1,0:T(8,128)S(1)}, f32[128,256]{1,0:T(8,128)S(1)}, u32[]{:S(2)}, u32[]{:S(2)}) collective-permute-start(f32[128,256]{1,0:T(8,128)S(1)} %get-tuple-element.54), channel_id=1, source_target_pairs={{0,0},{1,32},{2,64},{3,96},{4,128},{5,160},{6,192},{7,224},{8,8},{... | collective-permute-start | bytes 393224 | tf_op jit(solution)/shard_map/ppermute | solution.py:264
  14.0 0.0 collective-permute-done.6
  14.1 0.7 collective-permute-start.9
  14.8 0.0 collective-permute-done.1
  14.8 0.7 collective-permute-start.8
  15.5 0.0 collective-permute-done.3
  15.5 0.7 collective-permute-start.7
  16.2 0.0 collective-permute-done.2
  16.2 8.7 %collective-permute-done = f32[128,256]{1,0:T(8,128)S(1)} collective-permute-done((f32[128,256]{1,0:T(8,128)S(1)}, f32[128,256]{1,0:T(8,128)S(1)}, u32[]{:S(2)}, u32[]{:S(2)}) %collective-permute-start) | collective-permute-done | bytes 131104 | tf_op jit(solution)/shard_map/ppermute | solution.py:264
  24.9 0.0 collective-permute-done.9
  24.9 0.0 collective-permute-done.8
  24.9 0.0 collective-permute-done.7
  24.9 0.1 add_add_fusion
  25.0 1.3 %collective-permute-start.21 = (f32[128,256]{1,0:T(8,128)S(1)}, f32[128,256]{1,0:T(8,128)S(1)}, u32[]{:S(2)}, u32[]{:S(2)}) collective-permute-start(f32[128,256]{1,0:T(8,128)S(1)} %add_add_fusion.2), channel_id=1, source_target_pairs={{0,3},{1,0},{2,1},{3,2},{4,7},{5,4},{6,5},{7,6},{8,11},{9,8},{10,9... | collective-permute-start | bytes 393224 | tf_op jit(solution)/shard_map/ppermute | solution.py:239
  26.3 0.4 collective-permute-start.20
  26.6 1.3 %collective-permute-start.19 = (f32[128,256]{1,0:T(8,128)S(1)}, f32[128,256]{1,0:T(8,128)S(1)}, u32[]{:S(2)}, u32[]{:S(2)}) collective-permute-start(f32[128,256]{1,0:T(8,128)S(1)} %add_add_fusion.2), channel_id=1, source_target_pairs={{0,1},{1,2},{2,3},{3,0},{4,5},{5,6},{6,7},{7,4},{8,9},{9,10},{10,1... | collective-permute-start | bytes 393224 | tf_op jit(solution)/shard_map/ppermute | solution.py:239
  28.0 3.0 %collective-permute-done.21 = f32[128,256]{1,0:T(8,128)S(1)} collective-permute-done((f32[128,256]{1,0:T(8,128)S(1)}, f32[128,256]{1,0:T(8,128)S(1)}, u32[]{:S(2)}, u32[]{:S(2)}) %collective-permute-start.21) | collective-permute-done | bytes 131104 | tf_op jit(solution)/shard_map/ppermute | solution.py:239
  30.9 3.0 %collective-permute-done.20 = f32[128,256]{1,0:T(8,128)S(1)} collective-permute-done((f32[128,256]{1,0:T(8,128)S(1)}, f32[128,256]{1,0:T(8,128)S(1)}, u32[]{:S(2)}, u32[]{:S(2)}) %collective-permute-start.20) | collective-permute-done | bytes 131104 | tf_op jit(solution)/shard_map/ppermute | solution.py:239
  33.9 1.0 collective-permute-done.19
  35.0 0.8 pad_maximum_fusion
  35.8 0.0 all-gather.3.cloned.1.call-update
  35.8 1.3 %collective-permute-start.10 = (f32[3,128,128]{2,1,0:T(8,128)S(1)}, f32[3,128,128]{2,1,0:T(8,128)S(1)}, u32[]{:S(2)}, u32[]{:S(2)}) collective-permute-start(f32[3,128,128]{2,1,0:T(8,128)S(1)} %add_add_fusion), channel_id=1, source_target_pairs={{0,4},{1,5},{8,12},{9,13},{16,20},{17,21},{24,28},{25,29},{32,36},... | collective-permute-start | bytes 589832 | tf_op jit(solution)/shard_map/ppermute | solution.py:239
  37.1 16.8 %collective-permute-done.10 = f32[3,128,128]{2,1,0:T(8,128)S(1)} collective-permute-done((f32[3,128,128]{2,1,0:T(8,128)S(1)}, f32[3,128,128]{2,1,0:T(8,128)S(1)}, u32[]{:S(2)}, u32[]{:S(2)}) %collective-permute-start.10) | collective-permute-done | bytes 196640 | tf_op jit(solution)/shard_map/ppermute | solution.py:239
  54.0 2.3 %collective-permute-start.13 = (f32[3,128,128]{2,1,0:T(8,128)S(1)}, f32[3,128,128]{2,1,0:T(8,128)S(1)}, u32[]{:S(2)}, u32[]{:S(2)}) collective-permute-start(f32[3,128,128]{2,1,0:T(8,128)S(1)} %add.56), channel_id=1, source_target_pairs={{0,1},{1,2},{4,5},{5,6},{8,9},{9,10},{12,13},{13,14},{16,17},{17,1... | collective-permute-start | bytes 589832 | tf_op jit(solution)/shard_map/ppermute | solution.py:239
  56.2 1.3 %collective-permute-start.12 = (f32[3,128,128]{2,1,0:T(8,128)S(1)}, f32[3,128,128]{2,1,0:T(8,128)S(1)}, u32[]{:S(2)}, u32[]{:S(2)}) collective-permute-start(f32[3,128,128]{2,1,0:T(8,128)S(1)} %add.56), channel_id=1, source_target_pairs={{0,2},{1,3},{4,6},{5,7},{8,10},{9,11},{12,14},{13,15},{16,18},{17,... | collective-permute-start | bytes 589832 | tf_op jit(solution)/shard_map/ppermute | solution.py:239
  57.6 1.9 %collective-permute-start.11 = (f32[3,128,128]{2,1,0:T(8,128)S(1)}, f32[3,128,128]{2,1,0:T(8,128)S(1)}, u32[]{:S(2)}, u32[]{:S(2)}) collective-permute-start(f32[3,128,128]{2,1,0:T(8,128)S(1)} %add.56), channel_id=1, source_target_pairs={{0,3},{1,0},{4,7},{5,4},{8,11},{9,8},{12,15},{13,12},{16,19},{17,1... | collective-permute-start | bytes 589832 | tf_op jit(solution)/shard_map/ppermute | solution.py:239
  59.5 0.0 collective-permute-done.13
  59.5 2.0 %collective-permute-done.12 = f32[3,128,128]{2,1,0:T(8,128)S(1)} collective-permute-done((f32[3,128,128]{2,1,0:T(8,128)S(1)}, f32[3,128,128]{2,1,0:T(8,128)S(1)}, u32[]{:S(2)}, u32[]{:S(2)}) %collective-permute-start.12) | collective-permute-done | bytes 196640 | tf_op jit(solution)/shard_map/ppermute | solution.py:239
  61.5 3.6 %collective-permute-done.11 = f32[3,128,128]{2,1,0:T(8,128)S(1)} collective-permute-done((f32[3,128,128]{2,1,0:T(8,128)S(1)}, f32[3,128,128]{2,1,0:T(8,128)S(1)}, u32[]{:S(2)}, u32[]{:S(2)}) %collective-permute-start.11) | collective-permute-done | bytes 196640 | tf_op jit(solution)/shard_map/ppermute | solution.py:239
  65.2 0.1 collective-permute-start.14
  65.3 1.7 %collective-permute-done.14 = f32[2,3,128,128]{3,2,1,0:T(8,128)S(1)} collective-permute-done((f32[2,3,128,128]{3,2,1,0:T(8,128)S(1)}, f32[2,3,128,128]{3,2,1,0:T(8,128)S(1)}, u32[]{:S(2)}, u32[]{:S(2)}) %collective-permute-start.14) | collective-permute-done | bytes 393248 | tf_op jit(solution)/shard_map/ppermute | solution.py:239
  67.0 0.1 broadcast_select_fusion
  67.1 0.0 copy-start
  67.1 0.7 collective-permute-start.17
  67.8 1.3 %collective-permute-start.16 = (f32[2,256,256]{2,1,0:T(8,128)S(1)}, f32[2,256,256]{2,1,0:T(8,128)S(1)}, u32[]{:S(2)}, u32[]{:S(2)}) collective-permute-start(f32[2,256,256]{2,1,0:T(8,128)S(1)} %bitcast.43), channel_id=1, source_target_pairs={{0,128},{1,129},{2,130},{3,131},{4,132},{5,133},{6,134},{7,135},{8... | collective-permute-start | bytes 1572872 | tf_op jit(solution)/shard_map/ppermute | solution.py:239
  69.1 0.9 collective-permute-start.15
  70.0 20.5 %factor_pivots.1 = (f32[256,256]{1,0:T(8,128)S(1)}, f32[256,256]{1,0:T(8,128)S(1)}, f32[256,256]{1,0:T(8,128)S(1)}) custom-call(f32[2,3,128,128]{3,2,1,0:T(8,128)S(1)} %get-tuple-element.28.even, f32[2,3,128,128]{3,2,1,0:T(8,128)S(1)} %get-tuple-element.29.odd), custom_call_target="tpu_custom_call" | custom-call | flops 24999999488 | bytes 1048576 | tf_op jit(solution)/shard_map/factor_pivots/pallas_call | solution.py:119
  90.5 0.0 collective-permute-done.17
  90.5 4.6 %collective-permute-done.16 = f32[2,256,256]{2,1,0:T(8,128)S(1)} collective-permute-done((f32[2,256,256]{2,1,0:T(8,128)S(1)}, f32[2,256,256]{2,1,0:T(8,128)S(1)}, u32[]{:S(2)}, u32[]{:S(2)}) %collective-permute-start.16) | collective-permute-done | bytes 524320 | tf_op jit(solution)/shard_map/ppermute | solution.py:239
  95.1 0.0 collective-permute-done.15
  95.1 0.1 select_select_fusion.y0
  95.2 0.1 collective-permute-start.18
  95.3 0.1 pad_add_fusion.ids
  95.4 1.8 %collective-permute-done.18.y1 = f32[2,256,256]{2,1,0:T(8,128)S(1)} collective-permute-done((f32[2,256,256]{2,1,0:T(8,128)S(1)}, f32[2,256,256]{2,1,0:T(8,128)S(1)}, u32[]{:S(2)}, u32[]{:S(2)}) %collective-permute-start.18) | collective-permute-done | bytes 524320 | tf_op jit(solution)/shard_map/ppermute | solution.py:239
  97.2 0.0 copy-done
  97.2 2.7 %solve_columns.1 = (bf16[2,256,256]{2,1,0:T(8,128)(2,1)S(1)}, bf16[2,256,256]{2,1,0:T(8,128)(2,1)S(1)}, bf16[2,256,256]{2,1,0:T(8,128)(2,1)S(1)}, bf16[2,2,512,256]{3,2,1,0:T(8,128)(2,1)S(1)}) custom-call(s32[4]{0:T(128)S(1)} %pad_add_fusion.ids, s32[64,64]{1,0:T(8,128)S(1)} %copy-done, f32[2,256,256]{2,1,0:T(8,128)S(1)} %select_select_fusion.y0, ...), custom_call_target="tpu_custom_call" | custom-call | flops 3000000000 | bytes 4194304 | tf_op jit(solution)/shard_map/solve_columns/pallas_call | solution.py:150
  99.9 0.0 all-gather.3.cloned.1.call-done
  99.9 13.2 %update.1 = f32[2,4,1024,128]{3,2,1,0:T(8,128)} custom-call(s32[4]{0:T(128)S(1)} %pad_add_fusion.ids, s32[64,64]{1,0:T(8,128)S(1)} %copy-done, f32[2,4,1024,128]{3,2,1,0:T(8,128)} %bitcast.51, f32[8,4,128,256]{3,2,1,0:T(8,128)} %bitcast.52, bf16[2,256,256]{2,1,0:T(8,128)(2,1)S(1)} %get-tuple-element.43.back0, ...), custom_call_target="tpu_custom_call" | custom-call | flops 12000000000 | bytes 14680064 | tf_op jit(solution)/shard_map/update/pallas_call | solution.py:213
  (10 shorter events, 0.3 us)
Async XLA Ops:
  6.5 93.4 %all-gather.3.cloned.1.call-start = ((), (), s32[]{:S(2)}) async-start(), calls=%async_computation | async-start | bytes 4718592 | tf_op jit(solution)/shard_map/all_gather | solution.py:276
  8.1 4.0 %collective-permute-start.5 = (f32[3,128,128]{2,1,0:T(8,128)S(1)}, f32[3,128,128]{2,1,0:T(8,128)S(1)}, u32[]{:S(2)}, u32[]{:S(2)}) collective-permute-start(f32[3,128,128]{2,1,0:T(8,128)S(1)} %pad_maximum_fusion.2), channel_id=1, source_target_pairs={{0,192},{1,193},{32,224},{33,225}} | collective-permute-start | bytes 589832 | tf_op jit(solution)/shard_map/ppermute | solution.py:239
  8.7 4.0 %collective-permute-start.4 = (f32[3,128,128]{2,1,0:T(8,128)S(1)}, f32[3,128,128]{2,1,0:T(8,128)S(1)}, u32[]{:S(2)}, u32[]{:S(2)}) collective-permute-start(f32[3,128,128]{2,1,0:T(8,128)S(1)} %pad_maximum_fusion.2), channel_id=1, source_target_pairs={{0,64},{1,65},{32,96},{33,97}} | collective-permute-start | bytes 589832 | tf_op jit(solution)/shard_map/ppermute | solution.py:239
  9.4 4.6 %collective-permute-start.6 = (f32[3,128,128]{2,1,0:T(8,128)S(1)}, f32[3,128,128]{2,1,0:T(8,128)S(1)}, u32[]{:S(2)}, u32[]{:S(2)}) collective-permute-start(f32[3,128,128]{2,1,0:T(8,128)S(1)} %pad_maximum_fusion.2), channel_id=1, source_target_pairs={{0,128},{1,129},{32,160},{33,161}} | collective-permute-start | bytes 589832 | tf_op jit(solution)/shard_map/ppermute | solution.py:239
  10.6 4.1 %collective-permute-start.1 = (f32[128,256]{1,0:T(8,128)S(1)}, f32[128,256]{1,0:T(8,128)S(1)}, u32[]{:S(2)}, u32[]{:S(2)}) collective-permute-start(f32[128,256]{1,0:T(8,128)S(1)} %get-tuple-element.51), channel_id=1, source_target_pairs={{0,1},{1,33},{2,65},{3,97},{4,129},{5,161},{6,193},{7,225},{8,9},{... | collective-permute-start | bytes 393224 | tf_op jit(solution)/shard_map/ppermute | solution.py:264
  11.3 4.2 %collective-permute-start.3 = (f32[128,256]{1,0:T(8,128)S(1)}, f32[128,256]{1,0:T(8,128)S(1)}, u32[]{:S(2)}, u32[]{:S(2)}) collective-permute-start(f32[128,256]{1,0:T(8,128)S(1)} %get-tuple-element.52), channel_id=1, source_target_pairs={{0,3},{1,35},{2,67},{3,99},{4,131},{5,163},{6,195},{7,227},{8,11},... | collective-permute-start | bytes 393224 | tf_op jit(solution)/shard_map/ppermute | solution.py:264
  12.1 4.1 %collective-permute-start.2 = (f32[128,256]{1,0:T(8,128)S(1)}, f32[128,256]{1,0:T(8,128)S(1)}, u32[]{:S(2)}, u32[]{:S(2)}) collective-permute-start(f32[128,256]{1,0:T(8,128)S(1)} %get-tuple-element.53), channel_id=1, source_target_pairs={{0,2},{1,34},{2,66},{3,98},{4,130},{5,162},{6,194},{7,226},{8,10},... | collective-permute-start | bytes 393224 | tf_op jit(solution)/shard_map/ppermute | solution.py:264
  12.7 12.1 %collective-permute-start = (f32[128,256]{1,0:T(8,128)S(1)}, f32[128,256]{1,0:T(8,128)S(1)}, u32[]{:S(2)}, u32[]{:S(2)}) collective-permute-start(f32[128,256]{1,0:T(8,128)S(1)} %get-tuple-element.54), channel_id=1, source_target_pairs={{0,0},{1,32},{2,64},{3,96},{4,128},{5,160},{6,192},{7,224},{8,8},{... | collective-permute-start | bytes 393224 | tf_op jit(solution)/shard_map/ppermute | solution.py:264
  14.1 10.8 %collective-permute-start.9 = (f32[3,128,128]{2,1,0:T(8,128)S(1)}, f32[3,128,128]{2,1,0:T(8,128)S(1)}, u32[]{:S(2)}, u32[]{:S(2)}) collective-permute-start(f32[3,128,128]{2,1,0:T(8,128)S(1)} %add_add_fusion.1), channel_id=1, source_target_pairs={{0,16},{1,17},{32,48},{33,49},{64,80},{65,81},{96,112},{97,113},{1... | collective-permute-start | bytes 589832 | tf_op jit(solution)/shard_map/ppermute | solution.py:239
  14.8 10.1 %collective-permute-start.8 = (f32[3,128,128]{2,1,0:T(8,128)S(1)}, f32[3,128,128]{2,1,0:T(8,128)S(1)}, u32[]{:S(2)}, u32[]{:S(2)}) collective-permute-start(f32[3,128,128]{2,1,0:T(8,128)S(1)} %add_add_fusion.1), channel_id=1, source_target_pairs={{0,24},{1,25},{32,56},{33,57},{64,88},{65,89},{96,120},{97,121},{1... | collective-permute-start | bytes 589832 | tf_op jit(solution)/shard_map/ppermute | solution.py:239
  15.5 9.4 %collective-permute-start.7 = (f32[3,128,128]{2,1,0:T(8,128)S(1)}, f32[3,128,128]{2,1,0:T(8,128)S(1)}, u32[]{:S(2)}, u32[]{:S(2)}) collective-permute-start(f32[3,128,128]{2,1,0:T(8,128)S(1)} %add_add_fusion.1), channel_id=1, source_target_pairs={{0,8},{1,9},{32,40},{33,41},{64,72},{65,73},{96,104},{97,105},{128... | collective-permute-start | bytes 589832 | tf_op jit(solution)/shard_map/ppermute | solution.py:239
  25.0 5.9 %collective-permute-start.21 = (f32[128,256]{1,0:T(8,128)S(1)}, f32[128,256]{1,0:T(8,128)S(1)}, u32[]{:S(2)}, u32[]{:S(2)}) collective-permute-start(f32[128,256]{1,0:T(8,128)S(1)} %add_add_fusion.2), channel_id=1, source_target_pairs={{0,3},{1,0},{2,1},{3,2},{4,7},{5,4},{6,5},{7,6},{8,11},{9,8},{10,9... | collective-permute-start | bytes 393224 | tf_op jit(solution)/shard_map/ppermute | solution.py:239
  26.3 7.7 %collective-permute-start.20 = (f32[128,256]{1,0:T(8,128)S(1)}, f32[128,256]{1,0:T(8,128)S(1)}, u32[]{:S(2)}, u32[]{:S(2)}) collective-permute-start(f32[128,256]{1,0:T(8,128)S(1)} %add_add_fusion.2), channel_id=1, source_target_pairs={{0,2},{1,3},{2,0},{3,1},{4,6},{5,7},{6,4},{7,5},{8,10},{9,11},{10,... | collective-permute-start | bytes 393224 | tf_op jit(solution)/shard_map/ppermute | solution.py:239
  26.6 8.3 %collective-permute-start.19 = (f32[128,256]{1,0:T(8,128)S(1)}, f32[128,256]{1,0:T(8,128)S(1)}, u32[]{:S(2)}, u32[]{:S(2)}) collective-permute-start(f32[128,256]{1,0:T(8,128)S(1)} %add_add_fusion.2), channel_id=1, source_target_pairs={{0,1},{1,2},{2,3},{3,0},{4,5},{5,6},{6,7},{7,4},{8,9},{9,10},{10,1... | collective-permute-start | bytes 393224 | tf_op jit(solution)/shard_map/ppermute | solution.py:239
  35.8 18.1 %collective-permute-start.10 = (f32[3,128,128]{2,1,0:T(8,128)S(1)}, f32[3,128,128]{2,1,0:T(8,128)S(1)}, u32[]{:S(2)}, u32[]{:S(2)}) collective-permute-start(f32[3,128,128]{2,1,0:T(8,128)S(1)} %add_add_fusion), channel_id=1, source_target_pairs={{0,4},{1,5},{8,12},{9,13},{16,20},{17,21},{24,28},{25,29},{32,36},... | collective-permute-start | bytes 589832 | tf_op jit(solution)/shard_map/ppermute | solution.py:239
  54.0 5.6 %collective-permute-start.13 = (f32[3,128,128]{2,1,0:T(8,128)S(1)}, f32[3,128,128]{2,1,0:T(8,128)S(1)}, u32[]{:S(2)}, u32[]{:S(2)}) collective-permute-start(f32[3,128,128]{2,1,0:T(8,128)S(1)} %add.56), channel_id=1, source_target_pairs={{0,1},{1,2},{4,5},{5,6},{8,9},{9,10},{12,13},{13,14},{16,17},{17,1... | collective-permute-start | bytes 589832 | tf_op jit(solution)/shard_map/ppermute | solution.py:239
  56.2 5.3 %collective-permute-start.12 = (f32[3,128,128]{2,1,0:T(8,128)S(1)}, f32[3,128,128]{2,1,0:T(8,128)S(1)}, u32[]{:S(2)}, u32[]{:S(2)}) collective-permute-start(f32[3,128,128]{2,1,0:T(8,128)S(1)} %add.56), channel_id=1, source_target_pairs={{0,2},{1,3},{4,6},{5,7},{8,10},{9,11},{12,14},{13,15},{16,18},{17,... | collective-permute-start | bytes 589832 | tf_op jit(solution)/shard_map/ppermute | solution.py:239
  57.6 7.6 %collective-permute-start.11 = (f32[3,128,128]{2,1,0:T(8,128)S(1)}, f32[3,128,128]{2,1,0:T(8,128)S(1)}, u32[]{:S(2)}, u32[]{:S(2)}) collective-permute-start(f32[3,128,128]{2,1,0:T(8,128)S(1)} %add.56), channel_id=1, source_target_pairs={{0,3},{1,0},{4,7},{5,4},{8,11},{9,8},{12,15},{13,12},{16,19},{17,1... | collective-permute-start | bytes 589832 | tf_op jit(solution)/shard_map/ppermute | solution.py:239
  65.2 1.8 %collective-permute-start.14 = (f32[2,3,128,128]{3,2,1,0:T(8,128)S(1)}, f32[2,3,128,128]{3,2,1,0:T(8,128)S(1)}, u32[]{:S(2)}, u32[]{:S(2)}) collective-permute-start(f32[2,3,128,128]{3,2,1,0:T(8,128)S(1)} %pad_maximum_fusion.1), channel_id=1, source_target_pairs={{0,32},{1,33},{2,34},{3,35},{4,36},{5,37},{6,38},{7,39},{8,40},{9,... | collective-permute-start | bytes 1179656 | tf_op jit(solution)/shard_map/ppermute | solution.py:239
  67.1 30.1 %copy-start = (s32[64,64]{1,0:T(8,128)S(1)}, s32[64,64]{1,0:T(8,128)}, u32[]{:S(2)}) copy-start(s32[64,64]{1,0:T(8,128)} %pattern.3) | copy-start | bytes 49156
  67.1 23.4 %collective-permute-start.17 = (f32[2,256,256]{2,1,0:T(8,128)S(1)}, f32[2,256,256]{2,1,0:T(8,128)S(1)}, u32[]{:S(2)}, u32[]{:S(2)}) collective-permute-start(f32[2,256,256]{2,1,0:T(8,128)S(1)} %bitcast.42), channel_id=1, source_target_pairs={{0,64},{1,65},{2,66},{3,67},{4,68},{5,69},{6,70},{7,71},{8,72},{9,... | collective-permute-start | bytes 1572872 | tf_op jit(solution)/shard_map/ppermute | solution.py:239
  67.8 27.3 %collective-permute-start.16 = (f32[2,256,256]{2,1,0:T(8,128)S(1)}, f32[2,256,256]{2,1,0:T(8,128)S(1)}, u32[]{:S(2)}, u32[]{:S(2)}) collective-permute-start(f32[2,256,256]{2,1,0:T(8,128)S(1)} %bitcast.43), channel_id=1, source_target_pairs={{0,128},{1,129},{2,130},{3,131},{4,132},{5,133},{6,134},{7,135},{8... | collective-permute-start | bytes 1572872 | tf_op jit(solution)/shard_map/ppermute | solution.py:239
  69.1 26.0 %collective-permute-start.15 = (f32[2,256,256]{2,1,0:T(8,128)S(1)}, f32[2,256,256]{2,1,0:T(8,128)S(1)}, u32[]{:S(2)}, u32[]{:S(2)}) collective-permute-start(f32[2,256,256]{2,1,0:T(8,128)S(1)} %bitcast.44), channel_id=1, source_target_pairs={{0,192},{1,193},{2,194},{3,195},{4,196},{5,197},{6,198},{7,199},{8... | collective-permute-start | bytes 1572872 | tf_op jit(solution)/shard_map/ppermute | solution.py:239
  95.2 2.0 %collective-permute-start.18 = (f32[2,256,256]{2,1,0:T(8,128)S(1)}, f32[2,256,256]{2,1,0:T(8,128)S(1)}, u32[]{:S(2)}, u32[]{:S(2)}) collective-permute-start(f32[2,256,256]{2,1,0:T(8,128)S(1)} %select_select_fusion.y0), channel_id=1, source_target_pairs={{0,32},{1,33},{2,34},{3,35},{4,36},{5,37},{6,38},{7,39},{8,40},{9,... | collective-permute-start | bytes 1572872 | tf_op jit(solution)/shard_map/ppermute | solution.py:239
Sparse Core Ops, SparseCore 0:
  36.0 63.5 all-gather.2

commit v8 on v7

--- a/solution.py
+++ b/solution.py
@@ -257,7 +257,7 @@
 
     corner = head[0]
     own = jnp.stack([corner[:HALF, :HALF], corner[:HALF, HALF:], corner[HALF:, HALF:]])
-    along = [shifted(own, x=k, where=lambda a, b, c, d: a == 0 and c == 0 and d < 2) for k in (1, 3, 2)]
+    along = [shifted(own, x=k, where=lambda a, b, c, d: a == 0 and c == 0 and d < 2) for k in (1, 2, 3)]
     parts = []
     for m in range(4):
         pairs = [(32 * c + s, (s % 8) * 32 + 8 * (s // 8) + 4 * c + m) for c in range(2) for s in range(32)]
@@ -269,12 +269,13 @@
     mine, pivot = tie(mine, pivot)
 
     pivot = pivot + shifted(pivot, z=1, where=lambda a, b, c, d: c % 2 == 0 and d < 2)
-    turns = [shifted(mine, y=k) for k in (1, 2, 3)]
-    g = jnp.stack([mine] + turns)
+    turns = {k: shifted(mine, y=k) for k in (1, 3, 2)}
+    g = jnp.stack([mine] + [turns[k] for k in (1, 2, 3)])
 
     groups = [[NY * b + a for b in range(NZ)] for a in range(NY)]
     g = lax.all_gather(g, "col", axis=0, axis_index_groups=groups)
-    got = [pivot] + [shifted(pivot, y=k, where=lambda a, b, c, d: d < 2) for k in (1, 2, 3)]
+    turns = {k: shifted(pivot, y=k, where=lambda a, b, c, d: d < 2) for k in (1, 3, 2)}
+    got = [pivot] + [turns[k] for k in (1, 2, 3)]
     both = jnp.stack([pick(y, got), pick((y + 3) % 4, got)])
     swapped = shifted(both, core=1)
     even = jnp.where(core == 0, both, swapped)

time: 122 us -> 122 us (level)
  the two profiles are of different devices: /device:TPU:36 before, /device:TPU:21 now
where the time goes in v8:
time: 122 us; the launch traced here: 121 us
  waiting for transfers between devices  37.5 us (31%)
  Pallas kernels  35.8 us (29%)
  starting transfers between devices  30.5 us (25%)
  between operations  13.8 us (11%)
  local copies, waits for them, and re-layouts  2.01 us (2%)
  other arithmetic  1.36 us (1%)
    ppermute x18, starting transfers between devices, shifted(): return lax.ppermute(value, AXES, pairs)  27.2 us
    ppermute x18, waiting for transfers between devices, shifted(): return lax.ppermute(value, AXES, pairs)  25.7 us
    pallas_call x1, Pallas kernels, factor_pivots(): pl.pallas_call(pivots_kernel, out_shape=(shape, shape, shape), in_specs=[...  20.5 us
    pallas_call x1, Pallas kernels, update(): pl.pallas_call(update_kernel, out_shape=jax.ShapeDtypeStruct(local.shape,...  12.7 us
    ppermute x4, waiting for transfers between devices, per_device(): parts.append(lax.ppermute(quarters[m], AXES, pairs))  7.17 us
    all_gather x1, waiting for transfers between devices, per_device(): g = lax.all_gather(g, 'col', axis=0, axis_index_groups=groups)  4.6 us
    ppermute x4, starting transfers between devices, per_device(): parts.append(lax.ppermute(quarters[m], AXES, pairs))  3.3 us
    pallas_call x1, Pallas kernels, solve_columns(): pl.pallas_call(columns_kernel, out_shape=(parts, parts, parts, jax.ShapeD...  2.66 us
  transfers between devices with their start and end apart: 23, of which 9 were waited for; matrix products, arithmetic and copies ran while one was open for 1% of the time, Pallas kernels for 19%

profile of v8, /device:TPU:21, one launch (start us, length us, event | category | flops | bytes accessed | tf_op | source)
XLA Modules:
  0.0 121.0 jit_solution(5731383486685370202)
XLA Ops:
  6.5 0.0 all-gather.3.cloned.1.call-start
  6.5 1.4 %slice.27 = f32[1,1,256,2,1,256]{5,4,3,2,1,0:T(1,128)S(1)} slice(f32[8,1,256,2,1,256]{5,4,3,2,1,0:T(1,128)} %param.2), slice={[0:1], [0:1], [0:256], [0:2], [0:1], [0:256]} | slice | bytes 1048576 | tf_op jit(solution)/shard_map/slice | solution.py:255
  8.1 0.7 collective-permute-start.5
  8.7 0.7 collective-permute-start.4
  9.4 0.7 collective-permute-start.6
  10.1 0.5 copy.12
  10.6 0.7 collective-permute-start.1
  11.3 0.7 collective-permute-start.3
  12.0 0.0 collective-permute-done.5
  12.1 1.3 %collective-permute-start.2 = (f32[128,256]{1,0:T(8,128)S(1)}, f32[128,256]{1,0:T(8,128)S(1)}, u32[]{:S(2)}, u32[]{:S(2)}) collective-permute-start(f32[128,256]{1,0:T(8,128)S(1)} %get-tuple-element.53), channel_id=1, source_target_pairs={{0,2},{1,34},{2,66},{3,98},{4,130},{5,162},{6,194},{7,226},{8,10},... | collective-permute-start | bytes 393224 | tf_op jit(solution)/shard_map/ppermute | solution.py:264
  13.4 0.0 collective-permute-done.4
  13.4 0.7 collective-permute-start
  14.0 0.0 collective-permute-done.6
  14.1 0.7 collective-permute-start.9
  14.8 0.0 collective-permute-done.1
  14.8 0.7 collective-permute-start.8
  15.5 0.0 collective-permute-done.3
  15.5 0.7 collective-permute-start.7
  16.2 7.2 %collective-permute-done.2 = f32[128,256]{1,0:T(8,128)S(1)} collective-permute-done((f32[128,256]{1,0:T(8,128)S(1)}, f32[128,256]{1,0:T(8,128)S(1)}, u32[]{:S(2)}, u32[]{:S(2)}) %collective-permute-start.2) | collective-permute-done | bytes 131104 | tf_op jit(solution)/shard_map/ppermute | solution.py:264
  23.3 0.0 collective-permute-done
  23.4 0.0 collective-permute-done.9
  23.4 0.0 collective-permute-done.8
  23.4 0.0 collective-permute-done.7
  23.4 0.1 add_add_fusion
  23.5 8.6 %collective-permute-start.21 = (f32[128,256]{1,0:T(8,128)S(1)}, f32[128,256]{1,0:T(8,128)S(1)}, u32[]{:S(2)}, u32[]{:S(2)}) collective-permute-start(f32[128,256]{1,0:T(8,128)S(1)} %add_add_fusion.2), channel_id=1, source_target_pairs={{0,3},{1,0},{2,1},{3,2},{4,7},{5,4},{6,5},{7,6},{8,11},{9,8},{10,9... | collective-permute-start | bytes 393224 | tf_op jit(solution)/shard_map/ppermute | solution.py:239
  32.0 0.0 collective-permute-start.20
  32.0 1.9 %collective-permute-start.19 = (f32[128,256]{1,0:T(8,128)S(1)}, f32[128,256]{1,0:T(8,128)S(1)}, u32[]{:S(2)}, u32[]{:S(2)}) collective-permute-start(f32[128,256]{1,0:T(8,128)S(1)} %add_add_fusion.2), channel_id=1, source_target_pairs={{0,1},{1,2},{2,3},{3,0},{4,5},{5,6},{6,7},{7,4},{8,9},{9,10},{10,1... | collective-permute-start | bytes 393224 | tf_op jit(solution)/shard_map/ppermute | solution.py:239
  33.9 0.1 collective-permute-done.21
  34.0 3.4 %collective-permute-done.20 = f32[128,256]{1,0:T(8,128)S(1)} collective-permute-done((f32[128,256]{1,0:T(8,128)S(1)}, f32[128,256]{1,0:T(8,128)S(1)}, u32[]{:S(2)}, u32[]{:S(2)}) %collective-permute-start.20) | collective-permute-done | bytes 131104 | tf_op jit(solution)/shard_map/ppermute | solution.py:239
  37.4 0.0 collective-permute-done.19
  37.4 0.8 pad_maximum_fusion
  38.2 0.0 all-gather.3.cloned.1.call-update
  38.2 0.7 collective-permute-start.10
  38.9 0.0 collective-permute-done.10
  38.9 1.3 %collective-permute-start.13 = (f32[3,128,128]{2,1,0:T(8,128)S(1)}, f32[3,128,128]{2,1,0:T(8,128)S(1)}, u32[]{:S(2)}, u32[]{:S(2)}) collective-permute-start(f32[3,128,128]{2,1,0:T(8,128)S(1)} %add.56), channel_id=1, source_target_pairs={{0,1},{1,2},{4,5},{5,6},{8,9},{9,10},{12,13},{13,14},{16,17},{17,1... | collective-permute-start | bytes 589832 | tf_op jit(solution)/shard_map/ppermute | solution.py:239
  40.2 1.3 %collective-permute-start.12 = (f32[3,128,128]{2,1,0:T(8,128)S(1)}, f32[3,128,128]{2,1,0:T(8,128)S(1)}, u32[]{:S(2)}, u32[]{:S(2)}) collective-permute-start(f32[3,128,128]{2,1,0:T(8,128)S(1)} %add.56), channel_id=1, source_target_pairs={{0,2},{1,3},{4,6},{5,7},{8,10},{9,11},{12,14},{13,15},{16,18},{17,... | collective-permute-start | bytes 589832 | tf_op jit(solution)/shard_map/ppermute | solution.py:239
  41.5 0.7 collective-permute-start.11
  42.2 6.8 %collective-permute-done.13 = f32[3,128,128]{2,1,0:T(8,128)S(1)} collective-permute-done((f32[3,128,128]{2,1,0:T(8,128)S(1)}, f32[3,128,128]{2,1,0:T(8,128)S(1)}, u32[]{:S(2)}, u32[]{:S(2)}) %collective-permute-start.13) | collective-permute-done | bytes 196640 | tf_op jit(solution)/shard_map/ppermute | solution.py:239
  49.1 3.7 %collective-permute-done.12 = f32[3,128,128]{2,1,0:T(8,128)S(1)} collective-permute-done((f32[3,128,128]{2,1,0:T(8,128)S(1)}, f32[3,128,128]{2,1,0:T(8,128)S(1)}, u32[]{:S(2)}, u32[]{:S(2)}) %collective-permute-start.12) | collective-permute-done | bytes 196640 | tf_op jit(solution)/shard_map/ppermute | solution.py:239
  52.8 0.0 collective-permute-done.11
  52.9 5.0 %collective-permute-start.14 = (f32[2,3,128,128]{3,2,1,0:T(8,128)S(1)}, f32[2,3,128,128]{3,2,1,0:T(8,128)S(1)}, u32[]{:S(2)}, u32[]{:S(2)}) collective-permute-start(f32[2,3,128,128]{3,2,1,0:T(8,128)S(1)} %pad_maximum_fusion.1), channel_id=1, source_target_pairs={{0,32},{1,33},{2,34},{3,35},{4,36},{5,37},{6,38},{7,39},{8,40},{9,... | collective-permute-start | bytes 1179656 | tf_op jit(solution)/shard_map/ppermute | solution.py:239
  57.9 1.3 %collective-permute-done.14 = f32[2,3,128,128]{3,2,1,0:T(8,128)S(1)} collective-permute-done((f32[2,3,128,128]{3,2,1,0:T(8,128)S(1)}, f32[2,3,128,128]{3,2,1,0:T(8,128)S(1)}, u32[]{:S(2)}, u32[]{:S(2)}) %collective-permute-start.14) | collective-permute-done | bytes 393248 | tf_op jit(solution)/shard_map/ppermute | solution.py:239
  59.2 0.1 broadcast_select_fusion
  59.3 0.0 copy-start
  59.3 0.7 collective-permute-start.17
  60.0 1.3 %collective-permute-start.16 = (f32[2,256,256]{2,1,0:T(8,128)S(1)}, f32[2,256,256]{2,1,0:T(8,128)S(1)}, u32[]{:S(2)}, u32[]{:S(2)}) collective-permute-start(f32[2,256,256]{2,1,0:T(8,128)S(1)} %bitcast.43), channel_id=1, source_target_pairs={{0,128},{1,129},{2,130},{3,131},{4,132},{5,133},{6,134},{7,135},{8... | collective-permute-start | bytes 1572872 | tf_op jit(solution)/shard_map/ppermute | solution.py:239
  61.3 0.9 collective-permute-start.15
  62.2 20.5 %factor_pivots.1 = (f32[256,256]{1,0:T(8,128)S(1)}, f32[256,256]{1,0:T(8,128)S(1)}, f32[256,256]{1,0:T(8,128)S(1)}) custom-call(f32[2,3,128,128]{3,2,1,0:T(8,128)S(1)} %get-tuple-element.28.even, f32[2,3,128,128]{3,2,1,0:T(8,128)S(1)} %get-tuple-element.29.odd), custom_call_target="tpu_custom_call" | custom-call | flops 24999999488 | bytes 1048576 | tf_op jit(solution)/shard_map/factor_pivots/pallas_call | solution.py:119
  82.7 0.0 collective-permute-done.17
  82.8 8.9 %collective-permute-done.16 = f32[2,256,256]{2,1,0:T(8,128)S(1)} collective-permute-done((f32[2,256,256]{2,1,0:T(8,128)S(1)}, f32[2,256,256]{2,1,0:T(8,128)S(1)}, u32[]{:S(2)}, u32[]{:S(2)}) %collective-permute-start.16) | collective-permute-done | bytes 524320 | tf_op jit(solution)/shard_map/ppermute | solution.py:239
  91.7 0.0 collective-permute-done.15
  91.7 0.1 select_select_fusion.y0
  91.8 0.9 collective-permute-start.18
  92.7 0.1 pad_add_fusion.ids
  92.8 1.5 %collective-permute-done.18.y1 = f32[2,256,256]{2,1,0:T(8,128)S(1)} collective-permute-done((f32[2,256,256]{2,1,0:T(8,128)S(1)}, f32[2,256,256]{2,1,0:T(8,128)S(1)}, u32[]{:S(2)}, u32[]{:S(2)}) %collective-permute-start.18) | collective-permute-done | bytes 524320 | tf_op jit(solution)/shard_map/ppermute | solution.py:239
  94.2 0.0 copy-done
  94.2 2.7 %solve_columns.1 = (bf16[2,256,256]{2,1,0:T(8,128)(2,1)S(1)}, bf16[2,256,256]{2,1,0:T(8,128)(2,1)S(1)}, bf16[2,256,256]{2,1,0:T(8,128)(2,1)S(1)}, bf16[2,2,512,256]{3,2,1,0:T(8,128)(2,1)S(1)}) custom-call(s32[4]{0:T(128)S(1)} %pad_add_fusion.ids, s32[64,64]{1,0:T(8,128)S(1)} %copy-done, f32[2,256,256]{2,1,0:T(8,128)S(1)} %select_select_fusion.y0, ...), custom_call_target="tpu_custom_call" | custom-call | flops 3000000000 | bytes 4194304 | tf_op jit(solution)/shard_map/solve_columns/pallas_call | solution.py:150
  96.9 4.6 %all-gather.3.cloned.1.call-done = f32[32,128,256]{2,1,0:T(8,128)} async-done(((f32[4,128,256]{2,1,0:T(8,128)}), f32[32,128,256]{2,1,0:T(8,128)}) %all-gather.3.cloned.1.call-update) | async-done | bytes 4194320 | tf_op jit(solution)/shard_map/all_gather | solution.py:276
  101.5 12.7 %update.1 = f32[2,4,1024,128]{3,2,1,0:T(8,128)} custom-call(s32[4]{0:T(128)S(1)} %pad_add_fusion.ids, s32[64,64]{1,0:T(8,128)S(1)} %copy-done, f32[2,4,1024,128]{3,2,1,0:T(8,128)} %bitcast.51, f32[8,4,128,256]{3,2,1,0:T(8,128)} %bitcast.52, bf16[2,256,256]{2,1,0:T(8,128)(2,1)S(1)} %get-tuple-element.43.back0, ...), custom_call_target="tpu_custom_call" | custom-call | flops 12000000000 | bytes 14680064 | tf_op jit(solution)/shard_map/update/pallas_call | solution.py:213
  (10 shorter events, 0.3 us)
Async XLA Ops:
  6.5 95.0 %all-gather.3.cloned.1.call-start = ((), (), s32[]{:S(2)}) async-start(), calls=%async_computation | async-start | bytes 4718592 | tf_op jit(solution)/shard_map/all_gather | solution.py:276
  8.1 4.0 %collective-permute-start.5 = (f32[3,128,128]{2,1,0:T(8,128)S(1)}, f32[3,128,128]{2,1,0:T(8,128)S(1)}, u32[]{:S(2)}, u32[]{:S(2)}) collective-permute-start(f32[3,128,128]{2,1,0:T(8,128)S(1)} %pad_maximum_fusion.2), channel_id=1, source_target_pairs={{0,128},{1,129},{32,160},{33,161}} | collective-permute-start | bytes 589832 | tf_op jit(solution)/shard_map/ppermute | solution.py:239
  8.7 4.6 %collective-permute-start.4 = (f32[3,128,128]{2,1,0:T(8,128)S(1)}, f32[3,128,128]{2,1,0:T(8,128)S(1)}, u32[]{:S(2)}, u32[]{:S(2)}) collective-permute-start(f32[3,128,128]{2,1,0:T(8,128)S(1)} %pad_maximum_fusion.2), channel_id=1, source_target_pairs={{0,64},{1,65},{32,96},{33,97}} | collective-permute-start | bytes 589832 | tf_op jit(solution)/shard_map/ppermute | solution.py:239
  9.4 4.6 %collective-permute-start.6 = (f32[3,128,128]{2,1,0:T(8,128)S(1)}, f32[3,128,128]{2,1,0:T(8,128)S(1)}, u32[]{:S(2)}, u32[]{:S(2)}) collective-permute-start(f32[3,128,128]{2,1,0:T(8,128)S(1)} %pad_maximum_fusion.2), channel_id=1, source_target_pairs={{0,192},{1,193},{32,224},{33,225}} | collective-permute-start | bytes 589832 | tf_op jit(solution)/shard_map/ppermute | solution.py:239
  10.6 4.1 %collective-permute-start.1 = (f32[128,256]{1,0:T(8,128)S(1)}, f32[128,256]{1,0:T(8,128)S(1)}, u32[]{:S(2)}, u32[]{:S(2)}) collective-permute-start(f32[128,256]{1,0:T(8,128)S(1)} %get-tuple-element.51), channel_id=1, source_target_pairs={{0,1},{1,33},{2,65},{3,97},{4,129},{5,161},{6,193},{7,225},{8,9},{... | collective-permute-start | bytes 393224 | tf_op jit(solution)/shard_map/ppermute | solution.py:264
  11.3 4.2 %collective-permute-start.3 = (f32[128,256]{1,0:T(8,128)S(1)}, f32[128,256]{1,0:T(8,128)S(1)}, u32[]{:S(2)}, u32[]{:S(2)}) collective-permute-start(f32[128,256]{1,0:T(8,128)S(1)} %get-tuple-element.52), channel_id=1, source_target_pairs={{0,3},{1,35},{2,67},{3,99},{4,131},{5,163},{6,195},{7,227},{8,11},... | collective-permute-start | bytes 393224 | tf_op jit(solution)/shard_map/ppermute | solution.py:264
  12.1 11.3 %collective-permute-start.2 = (f32[128,256]{1,0:T(8,128)S(1)}, f32[128,256]{1,0:T(8,128)S(1)}, u32[]{:S(2)}, u32[]{:S(2)}) collective-permute-start(f32[128,256]{1,0:T(8,128)S(1)} %get-tuple-element.53), channel_id=1, source_target_pairs={{0,2},{1,34},{2,66},{3,98},{4,130},{5,162},{6,194},{7,226},{8,10},... | collective-permute-start | bytes 393224 | tf_op jit(solution)/shard_map/ppermute | solution.py:264
  13.4 10.0 %collective-permute-start = (f32[128,256]{1,0:T(8,128)S(1)}, f32[128,256]{1,0:T(8,128)S(1)}, u32[]{:S(2)}, u32[]{:S(2)}) collective-permute-start(f32[128,256]{1,0:T(8,128)S(1)} %get-tuple-element.54), channel_id=1, source_target_pairs={{0,0},{1,32},{2,64},{3,96},{4,128},{5,160},{6,192},{7,224},{8,8},{... | collective-permute-start | bytes 393224 | tf_op jit(solution)/shard_map/ppermute | solution.py:264
  14.1 9.3 %collective-permute-start.9 = (f32[3,128,128]{2,1,0:T(8,128)S(1)}, f32[3,128,128]{2,1,0:T(8,128)S(1)}, u32[]{:S(2)}, u32[]{:S(2)}) collective-permute-start(f32[3,128,128]{2,1,0:T(8,128)S(1)} %add_add_fusion.1), channel_id=1, source_target_pairs={{0,16},{1,17},{32,48},{33,49},{64,80},{65,81},{96,112},{97,113},{1... | collective-permute-start | bytes 589832 | tf_op jit(solution)/shard_map/ppermute | solution.py:239
  14.8 8.6 %collective-permute-start.8 = (f32[3,128,128]{2,1,0:T(8,128)S(1)}, f32[3,128,128]{2,1,0:T(8,128)S(1)}, u32[]{:S(2)}, u32[]{:S(2)}) collective-permute-start(f32[3,128,128]{2,1,0:T(8,128)S(1)} %add_add_fusion.1), channel_id=1, source_target_pairs={{0,24},{1,25},{32,56},{33,57},{64,88},{65,89},{96,120},{97,121},{1... | collective-permute-start | bytes 589832 | tf_op jit(solution)/shard_map/ppermute | solution.py:239
  15.5 7.9 %collective-permute-start.7 = (f32[3,128,128]{2,1,0:T(8,128)S(1)}, f32[3,128,128]{2,1,0:T(8,128)S(1)}, u32[]{:S(2)}, u32[]{:S(2)}) collective-permute-start(f32[3,128,128]{2,1,0:T(8,128)S(1)} %add_add_fusion.1), channel_id=1, source_target_pairs={{0,8},{1,9},{32,40},{33,41},{64,72},{65,73},{96,104},{97,105},{128... | collective-permute-start | bytes 589832 | tf_op jit(solution)/shard_map/ppermute | solution.py:239
  23.5 10.5 %collective-permute-start.21 = (f32[128,256]{1,0:T(8,128)S(1)}, f32[128,256]{1,0:T(8,128)S(1)}, u32[]{:S(2)}, u32[]{:S(2)}) collective-permute-start(f32[128,256]{1,0:T(8,128)S(1)} %add_add_fusion.2), channel_id=1, source_target_pairs={{0,3},{1,0},{2,1},{3,2},{4,7},{5,4},{6,5},{7,6},{8,11},{9,8},{10,9... | collective-permute-start | bytes 393224 | tf_op jit(solution)/shard_map/ppermute | solution.py:239
  32.0 5.3 %collective-permute-start.20 = (f32[128,256]{1,0:T(8,128)S(1)}, f32[128,256]{1,0:T(8,128)S(1)}, u32[]{:S(2)}, u32[]{:S(2)}) collective-permute-start(f32[128,256]{1,0:T(8,128)S(1)} %add_add_fusion.2), channel_id=1, source_target_pairs={{0,2},{1,3},{2,0},{3,1},{4,6},{5,7},{6,4},{7,5},{8,10},{9,11},{10,... | collective-permute-start | bytes 393224 | tf_op jit(solution)/shard_map/ppermute | solution.py:239
  32.0 5.3 %collective-permute-start.19 = (f32[128,256]{1,0:T(8,128)S(1)}, f32[128,256]{1,0:T(8,128)S(1)}, u32[]{:S(2)}, u32[]{:S(2)}) collective-permute-start(f32[128,256]{1,0:T(8,128)S(1)} %add_add_fusion.2), channel_id=1, source_target_pairs={{0,1},{1,2},{2,3},{3,0},{4,5},{5,6},{6,7},{7,4},{8,9},{9,10},{10,1... | collective-permute-start | bytes 393224 | tf_op jit(solution)/shard_map/ppermute | solution.py:239
  38.2 0.7 collective-permute-start.10
  38.9 10.1 %collective-permute-start.13 = (f32[3,128,128]{2,1,0:T(8,128)S(1)}, f32[3,128,128]{2,1,0:T(8,128)S(1)}, u32[]{:S(2)}, u32[]{:S(2)}) collective-permute-start(f32[3,128,128]{2,1,0:T(8,128)S(1)} %add.56), channel_id=1, source_target_pairs={{0,1},{1,2},{4,5},{5,6},{8,9},{9,10},{12,13},{13,14},{16,17},{17,1... | collective-permute-start | bytes 589832 | tf_op jit(solution)/shard_map/ppermute | solution.py:239
  40.2 12.5 %collective-permute-start.12 = (f32[3,128,128]{2,1,0:T(8,128)S(1)}, f32[3,128,128]{2,1,0:T(8,128)S(1)}, u32[]{:S(2)}, u32[]{:S(2)}) collective-permute-start(f32[3,128,128]{2,1,0:T(8,128)S(1)} %add.56), channel_id=1, source_target_pairs={{0,2},{1,3},{4,6},{5,7},{8,10},{9,11},{12,14},{13,15},{16,18},{17,... | collective-permute-start | bytes 589832 | tf_op jit(solution)/shard_map/ppermute | solution.py:239
  41.5 11.2 %collective-permute-start.11 = (f32[3,128,128]{2,1,0:T(8,128)S(1)}, f32[3,128,128]{2,1,0:T(8,128)S(1)}, u32[]{:S(2)}, u32[]{:S(2)}) collective-permute-start(f32[3,128,128]{2,1,0:T(8,128)S(1)} %add.56), channel_id=1, source_target_pairs={{0,3},{1,0},{4,7},{5,4},{8,11},{9,8},{12,15},{13,12},{16,19},{17,1... | collective-permute-start | bytes 589832 | tf_op jit(solution)/shard_map/ppermute | solution.py:239
  52.9 6.4 %collective-permute-start.14 = (f32[2,3,128,128]{3,2,1,0:T(8,128)S(1)}, f32[2,3,128,128]{3,2,1,0:T(8,128)S(1)}, u32[]{:S(2)}, u32[]{:S(2)}) collective-permute-start(f32[2,3,128,128]{3,2,1,0:T(8,128)S(1)} %pad_maximum_fusion.1), channel_id=1, source_target_pairs={{0,32},{1,33},{2,34},{3,35},{4,36},{5,37},{6,38},{7,39},{8,40},{9,... | collective-permute-start | bytes 1179656 | tf_op jit(solution)/shard_map/ppermute | solution.py:239
  59.3 34.9 %copy-start = (s32[64,64]{1,0:T(8,128)S(1)}, s32[64,64]{1,0:T(8,128)}, u32[]{:S(2)}) copy-start(s32[64,64]{1,0:T(8,128)} %pattern.3) | copy-start | bytes 49156
  59.3 23.4 %collective-permute-start.17 = (f32[2,256,256]{2,1,0:T(8,128)S(1)}, f32[2,256,256]{2,1,0:T(8,128)S(1)}, u32[]{:S(2)}, u32[]{:S(2)}) collective-permute-start(f32[2,256,256]{2,1,0:T(8,128)S(1)} %bitcast.42), channel_id=1, source_target_pairs={{0,64},{1,65},{2,66},{3,67},{4,68},{5,69},{6,70},{7,71},{8,72},{9,... | collective-permute-start | bytes 1572872 | tf_op jit(solution)/shard_map/ppermute | solution.py:239
  60.0 31.7 %collective-permute-start.16 = (f32[2,256,256]{2,1,0:T(8,128)S(1)}, f32[2,256,256]{2,1,0:T(8,128)S(1)}, u32[]{:S(2)}, u32[]{:S(2)}) collective-permute-start(f32[2,256,256]{2,1,0:T(8,128)S(1)} %bitcast.43), channel_id=1, source_target_pairs={{0,128},{1,129},{2,130},{3,131},{4,132},{5,133},{6,134},{7,135},{8... | collective-permute-start | bytes 1572872 | tf_op jit(solution)/shard_map/ppermute | solution.py:239
  61.3 30.4 %collective-permute-start.15 = (f32[2,256,256]{2,1,0:T(8,128)S(1)}, f32[2,256,256]{2,1,0:T(8,128)S(1)}, u32[]{:S(2)}, u32[]{:S(2)}) collective-permute-start(f32[2,256,256]{2,1,0:T(8,128)S(1)} %bitcast.44), channel_id=1, source_target_pairs={{0,192},{1,193},{2,194},{3,195},{4,196},{5,197},{6,198},{7,199},{8... | collective-permute-start | bytes 1572872 | tf_op jit(solution)/shard_map/ppermute | solution.py:239
  91.8 2.4 %collective-permute-start.18 = (f32[2,256,256]{2,1,0:T(8,128)S(1)}, f32[2,256,256]{2,1,0:T(8,128)S(1)}, u32[]{:S(2)}, u32[]{:S(2)}) collective-permute-start(f32[2,256,256]{2,1,0:T(8,128)S(1)} %select_select_fusion.y0), channel_id=1, source_target_pairs={{0,32},{1,33},{2,34},{3,35},{4,36},{5,37},{6,38},{7,39},{8,40},{9,... | collective-permute-start | bytes 1572872 | tf_op jit(solution)/shard_map/ppermute | solution.py:239
Sparse Core Ops, SparseCore 0:
  38.3 63.1 all-gather.2
